TPU v7x, 256 devices: a whole 4x4x8 slice. The times are simulated.
256 devices in a mesh: dp: 16 (over z, y_hi), shard: 16 (over y_lo, x, core).
Axes of the slice: x: 4, y: 4 (y_hi: 2, y_lo: 2; y = y_hi * 2 + y_lo), z: 8, core: 2. Of those that a mesh axis runs over, the one named last changes fastest.
Arguments:
- hid_teacher: bfloat16 [8192, 2048], P(('dp', 'shard')), may hold values from -40 to 40
- hid_student: bfloat16 [8192, 2048], P(('dp', 'shard')), may hold values from -40 to 40
- proj_teacher: bfloat16 [2048, 384], P('shard'), may hold values from -0.176776695 to 0.176776695
- proj_student: bfloat16 [2048, 384], P('shard'), may hold values from -0.125 to 0.125
- proto_teacher: bfloat16 [384, 65536], P(None, 'shard'), may hold values from -0.61237244 to 0.61237244
- proto_student: bfloat16 [384, 65536], P(None, 'shard'), may hold values from -0.61237244 to 0.61237244
Outputs:
- loss: float32 [], replicated
- grad_proj: float32 [2048, 384], P('shard')
- grad_proto: float32 [384, 65536], P('dp', 'shard')
All inputs are finite; a program needn't handle non-finite values.
Results may differ from a plain program's by a relative error of at most 0.003.
The roundings to bfloat16 on the way count: a program that leaves them out, or rounds other values in their place, can miss the bound.
Values may be sent and summed in bfloat16 or wider, within the bound.
No kernel may reach another device: no remote copies, remote signals or barrier semaphores. Data moves between devices by JAX's collectives and lax.ppermute only.
A program may use at most 128 MiB of HBM per device.

v0:
```python
import jax
import jax.numpy as jnp
from jax import lax
from jax.sharding import PartitionSpec as P

ITERS = 3
GRAD_SCALE = 256


TAU_T = 0.04
TAU_S = 0.1
EPS = 1e-06
ROW_DIMS = (((0,), (0,)), ((), ()))
COL_DIMS = (((1,), (1,)), ((), ()))


def unit_rows(proj_out):
    norm = jnp.sqrt(jnp.sum(proj_out * proj_out, axis=1, keepdims=True) + EPS)
    return (proj_out / norm, norm)


def unit_columns(weight):
    wide = weight.astype(jnp.float32)
    norm = jnp.sqrt(jnp.sum(wide * wide, axis=0) + EPS)
    return ((wide / norm).astype(jnp.bfloat16), norm)


def column_step(row_scale, teacher_exp):
    mass = lax.psum(jnp.sum(row_scale[:, None] * teacher_exp, axis=0), "dp")
    return 1.0 / mass


def row_step(weighted):
    return 1.0 / lax.psum(jnp.sum(weighted, axis=1), "shard")


def norm_backward(dzhat, unit_s, norm_s):
    inner = jnp.sum(unit_s * dzhat, axis=1, keepdims=True)
    return ((dzhat - unit_s * inner) / norm_s).astype(jnp.bfloat16)


def local(hid_teacher, hid_student, proj_teacher, proj_student, proto_teacher, proto_student):
    v_t, _ = unit_columns(proto_teacher)
    v_s, col_norm = unit_columns(proto_student)
    y_t = jnp.dot(
        hid_teacher,
        lax.all_gather(proj_teacher, "shard", axis=0, tiled=True),
        preferred_element_type=jnp.float32,
    )
    y_s = jnp.dot(
        hid_student,
        lax.all_gather(proj_student, "shard", axis=0, tiled=True),
        preferred_element_type=jnp.float32,
    )
    unit_t = unit_rows(y_t)[0]
    unit_s, norm_s = unit_rows(y_s)
    z_t, z_s = (
        lax.all_gather(unit_t.astype(jnp.bfloat16), "shard", axis=0, tiled=True),
        lax.all_gather(unit_s.astype(jnp.bfloat16), "shard", axis=0, tiled=True),
    )
    teacher_exp = jnp.exp(jnp.dot(z_t, v_t, preferred_element_type=jnp.float32) / TAU_T)
    scores = jnp.dot(z_s, v_s, preferred_element_type=jnp.float32)
    student_exp = jnp.exp(scores / TAU_S)
    row_scale = jnp.ones((teacher_exp.shape[0],), jnp.float32)
    col_scale = column_step(row_scale, teacher_exp)
    for step in range(ITERS - 1):
        row_scale = row_step(teacher_exp * col_scale[None, :])
        col_scale = column_step(row_scale, teacher_exp)
    weighted = teacher_exp * col_scale[None, :]
    row_scale = row_step(weighted)
    target = weighted * row_scale[:, None]
    expsum, cross = lax.psum(
        (jnp.sum(student_exp, axis=1), jnp.sum(target * scores, axis=1)), "shard"
    )
    prob = student_exp / expsum[:, None]
    row_count = z_s.shape[0] * lax.axis_size("dp")
    loss = lax.psum(jnp.sum(jnp.log(expsum) - cross / TAU_S), "dp") / row_count
    grad_logits = (GRAD_SCALE / TAU_S * (prob - target)).astype(jnp.bfloat16)
    block = grad_logits
    dzhat = lax.psum_scatter(
        lax.dot_general(block, v_s, COL_DIMS, preferred_element_type=jnp.float32),
        "shard",
        scatter_dimension=0,
        tiled=True,
    )
    dy = norm_backward(dzhat, unit_s, norm_s)
    block = hid_student
    proj_term = lax.psum_scatter(
        lax.dot_general(block, dy, ROW_DIMS, preferred_element_type=jnp.float32),
        "shard",
        scatter_dimension=0,
        tiled=True,
    )
    grad_proj = lax.psum(proj_term, "dp")
    own_rows = v_s.shape[0] // lax.axis_size("dp")
    block = z_s
    dproto = lax.psum_scatter(
        lax.dot_general(block, grad_logits, ROW_DIMS, preferred_element_type=jnp.float32),
        "dp",
        scatter_dimension=0,
        tiled=True,
    )
    v_own = lax.dynamic_slice_in_dim(v_s, lax.axis_index("dp") * own_rows, own_rows, 0).astype(
        jnp.float32
    )
    dots = lax.psum(jnp.sum(v_own * dproto, axis=0), "dp")
    grad_proto = (dproto - v_own * dots[None, :]) / col_norm[None, :]
    return (loss, grad_proj, grad_proto)


def solution(mesh):
    placed = (
        P(("dp", "shard"), None),
        P(("dp", "shard"), None),
        P("shard", None),
        P("shard", None),
        P(None, "shard"),
        P(None, "shard"),
    )
    return jax.shard_map(
        local,
        mesh=mesh,
        in_specs=placed,
        out_specs=(P(), P("shard", None), P("dp", "shard")),
        check_vma=False,
    )
```

profile of v0, /device:TPU:2, one launch (start us, length us, event | category | flops | bytes accessed | tf_op | source)
XLA Modules:
  0.0 1064.2 jit_solution(2246345299456497674)
XLA Ops:
  8.7 2.7 fusion.3
  11.5 2.6 fusion.1
  15.0 33.2 %all-gather.5.cloned.1.call-done = bf16[2048,384]{1,0:T(8,128)(2,1)} async-done(((bf16[128,384]{1,0:T(8,128)(2,1)}), bf16[2048,384]{1,0:T(8,128)(2,1)}) %all-gather.5.cloned.1.call-update) | async-done | bytes 1572880 | tf_op jit(solution)/shard_map/all_gather | solution.py:47
  48.2 1.9 multiply_reduce_fusion.7
  50.1 18.2 %all_gather.15 = bf16[512,384]{1,0:T(8,128)(2,1)S(1)} all-gather(bf16[32,384]{1,0:T(8,128)(2,1)S(1)} %divide_convert_fusion.1), channel_id=1, replica_groups=mesh['dp'=16,'shard'=16] {'shard'}, dimensions={0}, use_global_device_ids=true | all-gather | bytes 417792 | tf_op jit(solution)/shard_map/all_gather | solution.py:58
  68.3 7.6 fusion.13
  75.9 77.3 %psum.78 = f32[4096]{0:T(1024)S(1)} all-reduce(f32[4096]{0:T(1024)S(1)} %get-tuple-element.16), channel_id=1, replica_groups=mesh['dp'=16,'shard'=16] {'dp'}, use_global_device_ids=true, to_apply=%region_7.0 | all-reduce | flops 4096 | bytes 32768 | tf_op jit(solution)/shard_map/psum | solution.py:29
  153.1 4.1 multiply_reduce_fusion.4
  157.2 24.5 %psum.79 = f32[512]{0:T(512)S(1)} all-reduce(f32[512]{0:T(512)S(1)} %multiply_reduce_fusion.4), channel_id=1, replica_groups=mesh['dp'=16,'shard'=16] {'shard'}, use_global_device_ids=true, to_apply=%region_9.0 | all-reduce | flops 512 | bytes 4096 | tf_op jit(solution)/shard_map/psum | solution.py:34
  181.7 4.6 multiply_reduce_fusion.3
  186.3 71.9 %psum.80 = f32[4096]{0:T(1024)S(1)} all-reduce(f32[4096]{0:T(1024)S(1)} %multiply_reduce_fusion.3), channel_id=1, replica_groups=mesh['dp'=16,'shard'=16] {'dp'}, use_global_device_ids=true, to_apply=%region_11.0 | all-reduce | flops 4096 | bytes 32768 | tf_op jit(solution)/shard_map/psum | solution.py:29
  258.2 4.1 multiply_reduce_fusion.2
  262.2 27.1 %psum.81 = f32[512]{0:T(512)S(1)} all-reduce(f32[512]{0:T(512)S(1)} %multiply_reduce_fusion.2), channel_id=1, replica_groups=mesh['dp'=16,'shard'=16] {'shard'}, use_global_device_ids=true, to_apply=%region_13.0 | all-reduce | flops 512 | bytes 4096 | tf_op jit(solution)/shard_map/psum | solution.py:34
  289.4 4.6 multiply_reduce_fusion.1
  293.9 73.1 %psum.82 = f32[4096]{0:T(1024)S(1)} all-reduce(f32[4096]{0:T(1024)S(1)} %multiply_reduce_fusion.1), channel_id=1, replica_groups=mesh['dp'=16,'shard'=16] {'dp'}, use_global_device_ids=true, to_apply=%region_15.0 | all-reduce | flops 4096 | bytes 32768 | tf_op jit(solution)/shard_map/psum | solution.py:29
  367.1 4.0 multiply_reduce_fusion.5
  371.1 27.1 %psum.83 = f32[512]{0:T(512)S(1)} all-reduce(f32[512]{0:T(512)S(1)} %multiply_reduce_fusion.5), channel_id=1, replica_groups=mesh['dp'=16,'shard'=16] {'shard'}, use_global_device_ids=true, to_apply=%region_17.0 | all-reduce | flops 512 | bytes 4096 | tf_op jit(solution)/shard_map/psum | solution.py:34
  398.2 1.9 multiply_reduce_fusion.8
  400.2 21.5 %all_gather.13 = bf16[512,384]{1,0:T(8,128)(2,1)S(1)} all-gather(bf16[32,384]{1,0:T(8,128)(2,1)S(1)} %fusion.12), channel_id=1, replica_groups=mesh['dp'=16,'shard'=16] {'shard'}, dimensions={0}, use_global_device_ids=true | all-gather | bytes 417792 | tf_op jit(solution)/shard_map/all_gather | solution.py:59
  421.7 8.0 fusion
  429.7 24.7 %all-reduce = (f32[512]{0:T(512)S(1)}, f32[512]{0:T(512)S(1)}) all-reduce(f32[512]{0:T(512)S(1)} %get-tuple-element.7, f32[512]{0:T(512)S(1)} %get-tuple-element.6), channel_id=1, replica_groups=mesh['dp'=16,'shard'=16] {'shard'}, use_global_device_ids=true, to_apply=%region_19.0 | all-reduce | flops 1024 | bytes 8192 | tf_op jit(solution)/shard_map/psum | solution.py:72
  454.4 7.2 multiply_convert_fusion
  461.7 2.0 copy-done.1
  463.7 3.3 fusion.14
  467.0 57.2 %reduce-scatter.4.cloned.1.call-done = f32[32,384]{1,0:T(8,128)} async-done(((f32[512,384]{1,0:T(8,128)}), f32[32,384]{1,0:T(8,128)}) %reduce-scatter.4.cloned.1.call-update) | async-done | bytes 49168 | tf_op jit(solution)/shard_map/reduce_scatter | solution.py:80
  525.3 3.2 convolution_bitcast_fusion
  528.6 6.8 fusion.15
  535.4 59.2 %reduce-scatter.6.cloned.1.call-done = f32[128,384]{0,1:T(8,128)} async-done(((f32[2048,384]{0,1:T(8,128)}), f32[128,384]{0,1:T(8,128)}) %reduce-scatter.6.cloned.1.call-update) | async-done | bytes 196624 | tf_op jit(solution)/shard_map/reduce_scatter | solution.py:88
  595.3 226.7 %reduce-scatter.8.cloned.1.call-done = f32[24,4096]{1,0:T(8,128)} async-done(((f32[384,4096]{1,0:T(8,128)}), f32[24,4096]{1,0:T(8,128)}) %reduce-scatter.8.cloned.1.call-update) | async-done | bytes 393232 | tf_op jit(solution)/shard_map/reduce_scatter | solution.py:97
  823.1 156.6 %all-reduce.4.cloned.1.call-done = f32[128,384]{0,1:T(8,128)} async-done(((f32[128,384]{0,1:T(8,128)}), f32[128,384]{0,1:T(8,128)}) %all-reduce.4.cloned.1.call-update) | async-done | bytes 196624 | tf_op jit(solution)/shard_map/psum | solution.py:94
  981.4 72.4 %all-reduce.1 = (f32[]{:T(128)}, f32[4096]{0:T(1024)S(1)}) all-reduce(f32[]{:T(128)} %subtract_reduce_fusion, f32[4096]{0:T(1024)S(1)} %fusion.7), channel_id=1, replica_groups=mesh['dp'=16,'shard'=16] {'dp'}, use_global_device_ids=true, to_apply=%region_21.0 | all-reduce | flops 4097 | bytes 32776 | tf_op jit(solution)/shard_map/psum | solution.py:77
  1054.4 1.8 fusion.9
  (39 shorter events, 7.2 us)
Async XLA Ops:
  7.2 391.1 %copy-start = (bf16[32,2048]{1,0:T(8,128)(2,1)S(1)}, bf16[32,2048]{1,0:T(8,128)(2,1)}, u32[]{:S(2)}) copy-start(bf16[32,2048]{1,0:T(8,128)(2,1)} %param.7) | copy-start | bytes 393220
  7.2 41.0 %all-gather.5.cloned.1.call-start = ((), (), s32[]{:S(2)}) async-start(), calls=%async_computation.4 | async-start | bytes 1671168 | tf_op jit(solution)/shard_map/all_gather | solution.py:47
  7.9 390.3 %all-gather.3.cloned.1.call-start = ((), (), s32[]{:S(2)}) async-start(), calls=%async_computation.3 | async-start | bytes 1671168 | tf_op jit(solution)/shard_map/all_gather | solution.py:52
  8.7 39.5 %copy-start.4 = (bf16[32,2048]{1,0:T(8,128)(2,1)S(1)}, bf16[32,2048]{1,0:T(8,128)(2,1)}, u32[]{:S(2)}) copy-start(bf16[32,2048]{1,0:T(8,128)(2,1)} %param.6) | copy-start | bytes 393220
  8.7 515.6 %reduce-scatter.4.cloned.1.call-start = ((), (), s32[]{:S(2)}) async-start(), calls=%async_computation.5 | async-start | bytes 835584 | tf_op jit(solution)/shard_map/reduce_scatter | solution.py:80
  8.7 5.3 copy-start.2
  421.7 8.0 copy-start.3
  461.7 2.0 copy-start.1
  467.0 127.6 %reduce-scatter.6.cloned.1.call-start = ((), (), s32[]{:S(2)}) async-start(), calls=%async_computation.6 | async-start | bytes 3342336 | tf_op jit(solution)/shard_map/reduce_scatter | solution.py:88
  528.5 293.5 %reduce-scatter.8.cloned.1.call-start = ((), (), s32[]{:S(2)}) async-start(), calls=%async_computation.8 | async-start | bytes 6684672 | tf_op jit(solution)/shard_map/reduce_scatter | solution.py:97
  535.4 444.3 %all-reduce.4.cloned.1.call-start = ((), (), s32[]{:S(2)}) async-start(), calls=%async_computation.7 | async-start | bytes 393216 | tf_op jit(solution)/shard_map/psum | solution.py:94
Sparse Core Ops, SparseCore 0:
  9.9 38.2 all-gather.4
  50.0 35.7 all-gather.2
  467.1 57.1 reduce-scatter.3
  528.6 65.9 reduce-scatter.5
  599.2 222.7 reduce-scatter.7
  824.5 155.1 all-reduce.3
where the time goes:
time: 1070 us; the launch traced here: 1060 us
  waiting for transfers between devices  534 us (50%)
  blocking collectives  438 us (41%)
  other arithmetic  39.4 us (4%)
  matrix products  32.5 us (3%)
  between operations  16 us (1%)
    reduce_scatter x1, waiting for transfers between devices, local(): lax.psum_scatter(lax.dot_general(block, grad_logits, ROW_DIMS, preferred_...  227 us
    psum x3, blocking collectives, column_step(): mass = lax.psum(jnp.sum(row_scale[:, None] * teacher_exp, axis=0), 'dp')  222 us
    psum x1, waiting for transfers between devices, local(): grad_proj = lax.psum(proj_term, 'dp')  157 us
    psum x3, blocking collectives, row_step(): return 1.0 / lax.psum(jnp.sum(weighted, axis=1), 'shard')  78.8 us
    psum x1, blocking collectives, local(): loss = lax.psum(jnp.sum(jnp.log(expsum) - cross / TAU_S), 'dp') / row_count  72.4 us
    reduce_scatter x1, waiting for transfers between devices, local(): lax.psum_scatter(lax.dot_general(block, dy, ROW_DIMS, preferred_element_t...  59.2 us
    reduce_scatter x1, waiting for transfers between devices, local(): lax.psum_scatter(lax.dot_general(block, v_s, COL_DIMS, preferred_element_...  57.2 us
    all_gather x1, waiting for transfers between devices, local(): lax.all_gather(proj_teacher, 'shard', axis=0, tiled=True)  33.2 us
  transfers between devices with their start and end apart: 6, of which 5 were waited for; matrix products, arithmetic and copies ran while one was open for 4% of the time, Pallas kernels for 0%

commit v1 on v0

v1 whole, which is shorter than its diff:
```python
import jax
import jax.numpy as jnp
from jax import lax
from jax.sharding import Mesh, PartitionSpec as P

ITERS = 3
GRAD_SCALE = 256
TAU_T = 0.04
TAU_S = 0.1
EPS = 1e-06
LANES = 128
ROW_DIMS = (((0,), (0,)), ((), ()))
COL_DIMS = (((1,), (1,)), ((), ()))

DP = ("z", "yh")
SHARD = ("yl", "x", "c")
PLANE = ("yh", "yl", "x", "c")


def unit_rows(proj_out):
    norm = jnp.sqrt(jnp.sum(proj_out * proj_out, axis=1, keepdims=True) + EPS)
    return (proj_out / norm, norm)


def unit_columns(weight):
    wide = weight.astype(jnp.float32)
    norm = jnp.sqrt(jnp.sum(wide * wide, axis=0) + EPS)
    return ((wide / norm).astype(jnp.bfloat16), norm)


def spread(block, axes):
    count = lax.axis_size(axes)
    return lax.all_to_all(
        jnp.broadcast_to(block[None], (count,) + block.shape), axes, 0, 0, tiled=True
    )


def total(vector, axes):
    return jnp.sum(spread(vector.reshape(-1, LANES), axes), axis=0).reshape(vector.shape)


def scatter_sum(parts, axes):
    count = lax.axis_size(axes)
    own = parts.shape[0] // count
    blocks = parts.reshape((count, own) + parts.shape[1:])
    return jnp.sum(lax.all_to_all(blocks, axes, 0, 0, tiled=True), axis=0)


def norm_backward(dzhat, unit_s, norm_s):
    inner = jnp.sum(unit_s * dzhat, axis=1, keepdims=True)
    return ((dzhat - unit_s * inner) / norm_s).astype(jnp.bfloat16)


def local(hid_teacher, hid_student, proj_teacher, proj_student, proto_teacher, proto_student):
    rows, bot = hid_teacher.shape[0], proj_teacher.shape[1]
    half = proto_teacher.shape[1] // lax.axis_size("yh")
    side = lax.axis_index("yh")
    first = side * half
    v_t, _ = unit_columns(lax.dynamic_slice_in_dim(proto_teacher, first, half, 1))
    v_s, col_norm = unit_columns(lax.dynamic_slice_in_dim(proto_student, first, half, 1))

    y_t = jnp.dot(
        hid_teacher,
        lax.all_gather(proj_teacher, SHARD, axis=0, tiled=True),
        preferred_element_type=jnp.float32,
    )
    y_s = jnp.dot(
        hid_student,
        lax.all_gather(proj_student, SHARD, axis=0, tiled=True),
        preferred_element_type=jnp.float32,
    )
    unit_s, norm_s = unit_rows(y_s)
    z_t = spread(unit_rows(y_t)[0].astype(jnp.bfloat16), PLANE).reshape(-1, bot)
    wide_s = lax.all_gather(y_s, PLANE, axis=0, tiled=True)
    z_s = unit_rows(wide_s)[0].astype(jnp.bfloat16)
    hid_group = lax.all_gather(hid_student, SHARD, axis=0, tiled=True)

    teacher_exp = jnp.exp(jnp.dot(z_t, v_t, preferred_element_type=jnp.float32) / TAU_T)
    row_scale = jnp.ones((teacher_exp.shape[0],), jnp.float32)
    col_scale = 1.0 / total(jnp.sum(row_scale[:, None] * teacher_exp, axis=0), "z")
    for step in range(ITERS - 1):
        row_scale = 1.0 / total(jnp.sum(teacher_exp * col_scale[None, :], axis=1), PLANE)
        col_scale = 1.0 / total(jnp.sum(row_scale[:, None] * teacher_exp, axis=0), "z")
    scores = jnp.dot(z_s, v_s, preferred_element_type=jnp.float32)
    student_exp = jnp.exp(scores / TAU_S)
    weighted = teacher_exp * col_scale[None, :]
    sums = total(
        jnp.stack(
            [
                jnp.sum(weighted, axis=1),
                jnp.sum(student_exp, axis=1),
                jnp.sum(weighted * scores, axis=1),
            ]
        ),
        PLANE,
    )
    row_scale, expsum, cross = 1.0 / sums[0], sums[1], sums[2]
    row_scale, expsum, cross = lax.optimization_barrier((row_scale, expsum, cross))
    row_loss = jnp.sum(jnp.log(expsum) - row_scale * cross / TAU_S)
    target = weighted * row_scale[:, None]
    prob = student_exp / expsum[:, None]
    grad_logits = (GRAD_SCALE / TAU_S * (prob - target)).astype(jnp.bfloat16)

    dproto = lax.psum_scatter(
        lax.dot_general(z_s, grad_logits, ROW_DIMS, preferred_element_type=jnp.float32),
        "z",
        scatter_dimension=0,
        tiled=True,
    )
    dzhat = scatter_sum(
        lax.dot_general(grad_logits, v_s, COL_DIMS, preferred_element_type=jnp.float32), PLANE
    )
    dy = norm_backward(dzhat, unit_s, norm_s)
    dy_group = spread(dy, SHARD).reshape(-1, bot)
    depth = proj_student.shape[0]
    hid_block = lax.dynamic_slice_in_dim(
        hid_group, lax.axis_index(SHARD) * depth, depth, 1
    )
    proj_term = lax.dot_general(hid_block, dy_group, ROW_DIMS, preferred_element_type=jnp.float32)
    proj_part = scatter_sum(proj_term, DP)

    own = dproto.shape[0]
    v_own = lax.dynamic_slice_in_dim(v_s, lax.axis_index("z") * own, own, 0).astype(jnp.float32)
    dots = jnp.sum(v_own * dproto, axis=0)
    flat = jnp.concatenate(
        [proj_part.reshape(-1, LANES), dots.reshape(-1, LANES), jnp.full((8, LANES), row_loss)]
    )
    parts = spread(flat, DP)
    cut = proj_part.size // LANES
    grad_proj = parts[:, :cut].reshape(-1, bot)
    sides = parts[:, cut:].reshape(lax.axis_size("z"), lax.axis_size("yh"), -1)
    sums = jnp.sum(lax.dynamic_index_in_dim(sides, side, 1, keepdims=False), axis=0)
    dots = sums[:half]
    row_count = hid_teacher.shape[0] * lax.axis_size(DP + SHARD)
    loss = sums[half] / row_count
    grad = (dproto - v_own * dots[None, :]) / col_norm[None, :]
    grad = grad.reshape(lax.axis_size("yh"), -1, half)
    grad = lax.all_to_all(grad, "yh", 0, 0, tiled=True)
    grad_proto = jnp.concatenate([grad[0], grad[1]], axis=1)
    return (loss, grad_proj, grad_proto)


def solution(mesh):
    fine = Mesh(mesh.devices.reshape(8, 2, 2, 4, 2), DP + SHARD)
    everything = DP + SHARD
    placed = (
        P(everything, None),
        P(everything, None),
        P(SHARD, None),
        P(SHARD, None),
        P(None, SHARD),
        P(None, SHARD),
    )
    return jax.shard_map(
        local,
        mesh=fine,
        in_specs=placed,
        out_specs=(P(), P(SHARD, None), P(DP, SHARD)),
        check_vma=False,
    )
```

time: 1070 us -> 345 us (0.32)
  blocking collectives: 438 us -> 39.8 us
  waiting for transfers between devices: 534 us -> 173 us
  starting transfers between devices: 0.24 us -> 39.8 us
    psum x8 -> x0, blocking collectives: 398 us -> none  [the longest x3 222 us: column_step(): mass = lax.psum(jnp.sum(row_scale[:, None] * teacher_exp, axis=0), 'dp')]
    reduce_scatter x3 -> x1, waiting for transfers between devices: 343 us -> 0.02 us  [local(): lax.psum_scatter(lax.dot_general(z_s, grad_logits, ROW_DIMS, preferred_el...]
    psum x1 -> x0, waiting for transfers between devices: 157 us -> none  [local(): grad_proj = lax.psum(proj_term, 'dp')]
    all_to_all x0 -> x9, waiting for transfers between devices: none -> 96.1 us  [the longest x6 56 us: spread(): lax.all_to_all(jnp.broadcast_to(block[None], (count,) + block.shape), axe...]
    all_gather x2 -> x4, waiting for transfers between devices: 33.2 us -> 75.3 us  [the longest x1 39.5 us: local(): lax.all_gather(proj_teacher, SHARD, axis=0, tiled=True)]
    all_to_all x0 -> x3, blocking collectives: none -> 39.8 us  [spread(): lax.all_to_all(jnp.broadcast_to(block[None], (count,) + block.shape), axe...]
    all_gather x2 -> x0, blocking collectives: 39.7 us -> none  [the longest x1 21.5 us: local(): lax.all_gather(unit_s.astype(jnp.bfloat16), 'shard', axis=0, tiled=True)]
    all_to_all x0 -> x9, starting transfers between devices: none -> 39.5 us  [the longest x6 27.3 us: spread(): lax.all_to_all(jnp.broadcast_to(block[None], (count,) + block.shape), axe...]
  transfers between devices with their start and end apart: 6 -> 14, of which waited for: 5 -> 11; matrix products, arithmetic and copies ran while one was open for 4% -> 19% of each run, Pallas kernels for 0% -> 0%
where the time goes in v1:
time: 345 us; the launch traced here: 344 us
  waiting for transfers between devices  173 us (50%)
  starting transfers between devices  39.8 us (12%)
  blocking collectives  39.8 us (12%)
  matrix products  32.3 us (9%)
  other arithmetic  31.8 us (9%)
  between operations  16 us (5%)
  local copies, waits for them, and re-layouts  11 us (3%)
    all_to_all x6, waiting for transfers between devices, spread(): lax.all_to_all(jnp.broadcast_to(block[None], (count,) + block.shape), axe...  56 us
    all_to_all x3, blocking collectives, spread(): lax.all_to_all(jnp.broadcast_to(block[None], (count,) + block.shape), axe...  39.8 us
    all_gather x1, waiting for transfers between devices, local(): lax.all_gather(proj_teacher, SHARD, axis=0, tiled=True)  39.5 us
    all_gather x1, waiting for transfers between devices, local(): lax.all_gather(proj_student, SHARD, axis=0, tiled=True)  35.8 us
    all_to_all x2, waiting for transfers between devices, scatter_sum(): return jnp.sum(lax.all_to_all(blocks, axes, 0, 0, tiled=True), axis=0)  34.5 us
    all_to_all x6, starting transfers between devices, spread(): lax.all_to_all(jnp.broadcast_to(block[None], (count,) + block.shape), axe...  27.3 us
    dot_general x1, matrix products, local(): scores = jnp.dot(z_s, v_s, preferred_element_type=jnp.float32)  10.8 us
    all_to_all x2, starting transfers between devices, scatter_sum(): return jnp.sum(lax.all_to_all(blocks, axes, 0, 0, tiled=True), axis=0)  8.73 us
  transfers between devices with their start and end apart: 14, of which 11 were waited for; matrix products, arithmetic and copies ran while one was open for 19% of the time, Pallas kernels for 0%

profile of v1, /device:TPU:2, one launch (start us, length us, event | category | flops | bytes accessed | tf_op | source)
XLA Modules:
  0.0 343.9 jit_solution(12179641737740825705)
XLA Ops:
  8.7 39.5 %all-gather.11.cloned.1.call-done = bf16[2048,384]{1,0:T(8,128)(2,1)} async-done(((bf16[128,384]{1,0:T(8,128)(2,1)}), bf16[2048,384]{1,0:T(8,128)(2,1)}) %all-gather.11.cloned.1.call-update) | async-done | bytes 1572880 | tf_op jit(solution)/shard_map/all_gather | solution.py:64
  50.1 35.8 %all-gather.7.cloned.1.call-done = bf16[2048,384]{1,0:T(8,128)(2,1)} async-done(((bf16[128,384]{1,0:T(8,128)(2,1)}), bf16[2048,384]{1,0:T(8,128)(2,1)}) %all-gather.7.cloned.1.call-update) | async-done | bytes 1572880 | tf_op jit(solution)/shard_map/all_gather | solution.py:69
  89.5 6.6 %all-to-all-start = ((bf16[32,32,384]{2,1,0:T(8,128)(2,1)}), bf16[32,32,384]{2,1,0:T(8,128)(2,1)}, u32[]{:S(2)}, u32[]{:S(2)}) async-start(bf16[32,32,384]{2,1,0:T(8,128)(2,1)} %broadcast_in_dim.32), calls=%async_computation | async-start | bytes 1572864 | tf_op jit(solution)/shard_map/all_to_all | solution.py:33
  96.5 13.3 %all-to-all-done = bf16[32,32,384]{2,1,0:T(8,128)(2,1)} async-done(((bf16[32,32,384]{2,1,0:T(8,128)(2,1)}), bf16[32,32,384]{2,1,0:T(8,128)(2,1)}, u32[]{:S(2)}, u32[]{:S(2)}) %all-to-all-start) | async-done | bytes 786464 | tf_op jit(solution)/shard_map/all_to_all | solution.py:33
  109.7 6.7 %fusion.18 = (f32[2048]{0:T(1024)S(1)}, f32[1024,2048]{1,0:T(8,128)}) fusion(bf16[1024,384]{1,0:T(8,128)(2,1)} %bitcast.2, f32[2048]{0:T(1024)S(1)} %add_sqrt_fusion, bf16[384,4096]{1,0:T(8,128)(2,1)S(1)} %copy-done.7, s32[]{:T(128)S(6)} %select_n.15), kind=kOutput, calls=%fused_computation.61 | convolution fusion | flops 1617164288 | bytes 10764292 | tf_op jit(solution)/shard_map/dot_general | solution.py:78
  116.4 15.2 %all_to_all.60 = f32[8,16,128]{2,1,0:T(8,128)S(1)} all-to-all(f32[8,16,128]{2,1,0:T(8,128)S(1)} %broadcast_in_dim.34), channel_id=1, replica_groups=mesh['z'=8,'yh'=2,'yl'=2,'x'=4,'c'=2] {'z'}, dimensions={0} | all-to-all | bytes 131072 | tf_op jit(solution)/shard_map/all_to_all | solution.py:33
  131.6 4.2 %multiply_reduce_fusion.4 = f32[1024]{0:T(1024)S(1)} fusion(f32[1024,2048]{1,0:T(8,128)} %get-tuple-element.22, f32[2048]{0:T(1024)S(1)} %divide_bitcast_fusion.2), kind=kLoop, calls=%fused_computation.5 | loop fusion | flops 4193280 | bytes 8400896 | tf_op jit(solution)/shard_map/reduce_sum | solution.py:82
  135.8 11.0 %all_to_all.61 = f32[32,8,128]{2,1,0:T(8,128)S(1)} all-to-all(f32[32,8,128]{2,1,0:T(8,128)S(1)} %broadcast_in_dim.36), channel_id=1, replica_groups=mesh['z'=8,'yh'=2,'yl'=2,'x'=4,'c'=2] {'yh','yl','x','c'}, dimensions={0} | all-to-all | bytes 262144 | tf_op jit(solution)/shard_map/all_to_all | solution.py:33
  146.8 4.2 %multiply_reduce_fusion.3 = f32[2048]{0:T(1024)S(1)} fusion(f32[1024,2048]{1,0:T(8,128)} %get-tuple-element.22, f32[1024]{0:T(1024)S(1)} %divide_bitcast_fusion.4), kind=kLoop, calls=%fused_computation.4 | loop fusion | flops 4192256 | bytes 8400896 | tf_op jit(solution)/shard_map/reduce_sum | solution.py:83
  151.6 3.4 all-to-all-start.3
  155.9 7.4 %all-to-all-done.3 = f32[8,16,128]{2,1,0:T(8,128)S(1)} async-done(((f32[8,16,128]{2,1,0:T(8,128)}), f32[8,16,128]{2,1,0:T(8,128)S(1)}, u32[]{:S(2)}, u32[]{:S(2)}) %all-to-all-start.3) | async-done | bytes 65568 | tf_op jit(solution)/shard_map/all_to_all | solution.py:33
  163.3 4.0 %multiply_reduce_fusion.2 = f32[1024]{0:T(1024)S(1)} fusion(f32[1024,2048]{1,0:T(8,128)} %get-tuple-element.22, f32[2048]{0:T(1024)S(1)} %divide_bitcast_fusion.1), kind=kLoop, calls=%fused_computation.3 | loop fusion | flops 4193280 | bytes 8400896 | tf_op jit(solution)/shard_map/reduce_sum | solution.py:82
  168.0 4.9 %all-to-all-start.4 = ((f32[32,8,128]{2,1,0:T(8,128)}), f32[32,8,128]{2,1,0:T(8,128)S(1)}, u32[]{:S(2)}, u32[]{:S(2)}) async-start(f32[32,8,128]{2,1,0:T(8,128)} %broadcast_in_dim.40), calls=%async_computation.4 | async-start | bytes 262144 | tf_op jit(solution)/shard_map/all_to_all | solution.py:33
  172.9 7.5 %all-to-all-done.4 = f32[32,8,128]{2,1,0:T(8,128)S(1)} async-done(((f32[32,8,128]{2,1,0:T(8,128)}), f32[32,8,128]{2,1,0:T(8,128)S(1)}, u32[]{:S(2)}, u32[]{:S(2)}) %all-to-all-start.4) | async-done | bytes 131104 | tf_op jit(solution)/shard_map/all_to_all | solution.py:33
  180.5 4.1 %multiply_reduce_fusion.1 = f32[2048]{0:T(1024)S(1)} fusion(f32[1024,2048]{1,0:T(8,128)} %get-tuple-element.22, f32[1024]{0:T(1024)S(1)} %divide_bitcast_fusion.3), kind=kLoop, calls=%fused_computation.2 | loop fusion | flops 4192256 | bytes 8400896 | tf_op jit(solution)/shard_map/reduce_sum | solution.py:83
  185.3 3.4 all-to-all-start.5
  190.5 6.5 %all-to-all-done.5 = f32[8,16,128]{2,1,0:T(8,128)S(1)} async-done(((f32[8,16,128]{2,1,0:T(8,128)}), f32[8,16,128]{2,1,0:T(8,128)S(1)}, u32[]{:S(2)}, u32[]{:S(2)}) %all-to-all-start.5) | async-done | bytes 65568 | tf_op jit(solution)/shard_map/all_to_all | solution.py:33
  198.7 10.8 %multiply_reduce_fusion.5 = (f32[1024]{0:T(1024)S(1)}, f32[1024]{0:T(1024)S(1)}, f32[1024]{0:T(1024)S(1)}, f32[1024,2048]{1,0:T(8,128)}) fusion(f32[1024,2048]{1,0:T(8,128)} %get-tuple-element.22, f32[2048]{0:T(1024)S(1)} %divide_bitcast_fusion, bf16[384,2048]{1,0:T(8,128)(2,1)} %fusion.2, f32[1024,384]{1,0:T(8,128)} %all-gather.9.cloned.1.call-done, ...), kind=kOutput, calls=%fused_computation.9 | convolution fusion | flops 1623979008 | bytes 19947520 | tf_op jit(solution)/shard_map/dot_general | solution.py:84
  209.6 13.6 %all_to_all.62 = f32[32,24,128]{2,1,0:T(8,128)S(1)} all-to-all(f32[32,24,128]{2,1,0:T(8,128)S(1)} %broadcast_in_dim.44), channel_id=1, replica_groups=mesh['z'=8,'yh'=2,'yl'=2,'x'=4,'c'=2] {'yh','yl','x','c'}, dimensions={0} | all-to-all | bytes 786432 | tf_op jit(solution)/shard_map/all_to_all | solution.py:33
  223.3 7.3 %multiply_convert_fusion = bf16[1024,2048]{1,0:T(8,128)(2,1)S(1)} fusion(f32[1024,2048]{1,0:T(8,128)} %get-tuple-element.23, f32[1024,2048]{1,0:T(8,128)} %get-tuple-element.22, f32[1024]{0:T(1024)S(1)} %get-tuple-element.7, f32[1024]{0:T(1024)S(1)} %get-tuple-element.6, f32[2048]{0:T(1024)S(1)} %divide_bitcast_fusion), kind=kLoop, calls=%fused_computation | loop fusion | flops 14680064 | bytes 20987904 | tf_op jit(solution)/shard_map/convert_element_type | solution.py:102
  232.5 3.6 %fusion.15 = f32[384,2048]{1,0:T(8,128)} fusion(bf16[1024,2048]{1,0:T(8,128)(2,1)S(1)} %multiply_convert_fusion, f32[1024,384]{1,0:T(8,128)S(1)} %copy-done.4, f32[1024]{0:T(1024)S(1)} %add_sqrt_fusion.2), kind=kOutput, calls=%fused_computation.58 | convolution fusion | flops 1611399168 | bytes 8916992 | tf_op jit(solution)/shard_map/dot_general | solution.py:105
  237.5 5.8 %fusion.19 = f32[1024,384]{1,0:T(8,128)} fusion(bf16[1024,2048]{1,0:T(8,128)(2,1)} %copy-done.1, bf16[384,2048]{1,0:T(8,128)(2,1)S(1)} %copy-done.3), kind=kOutput, calls=%fused_computation.62 | convolution fusion | flops 1610612736 | bytes 7340032 | tf_op jit(solution)/shard_map/dot_general | solution.py:111
  243.3 5.2 %all-to-all-start.7 = ((f32[32,32,384]{2,1,0:T(8,128)}), f32[32,32,384]{2,1,0:T(8,128)S(1)}, u32[]{:S(2)}, u32[]{:S(2)}) async-start(f32[32,32,384]{2,1,0:T(8,128)} %bitcast.51), calls=%async_computation.7 | async-start | bytes 3145728 | tf_op jit(solution)/shard_map/all_to_all | solution.py:46
  248.5 22.1 %all-to-all-done.7 = f32[32,32,384]{2,1,0:T(8,128)S(1)} async-done(((f32[32,32,384]{2,1,0:T(8,128)}), f32[32,32,384]{2,1,0:T(8,128)S(1)}, u32[]{:S(2)}, u32[]{:S(2)}) %all-to-all-start.7) | async-done | bytes 1572896 | tf_op jit(solution)/shard_map/all_to_all | solution.py:46
  271.9 5.5 %all-to-all-start.8 = ((bf16[16,32,384]{2,1,0:T(8,128)(2,1)}), bf16[16,32,384]{2,1,0:T(8,128)(2,1)S(1)}, u32[]{:S(2)}, u32[]{:S(2)}) async-start(bf16[16,32,384]{2,1,0:T(8,128)(2,1)} %broadcast_in_dim.45), calls=%async_computation.8 | async-start | bytes 786432 | tf_op jit(solution)/shard_map/all_to_all | solution.py:33
  278.4 5.4 %all-to-all-done.8 = bf16[16,32,384]{2,1,0:T(8,128)(2,1)S(1)} async-done(((bf16[16,32,384]{2,1,0:T(8,128)(2,1)}), bf16[16,32,384]{2,1,0:T(8,128)(2,1)S(1)}, u32[]{:S(2)}, u32[]{:S(2)}) %all-to-all-start.8) | async-done | bytes 393248 | tf_op jit(solution)/shard_map/all_to_all | solution.py:33
  284.7 3.5 %all-to-all-start.9 = ((f32[16,8,384]{2,1,0:T(8,128)}), f32[16,8,384]{2,1,0:T(8,128)S(1)}, u32[]{:S(2)}, u32[]{:S(2)}) async-start(f32[16,8,384]{2,1,0:T(8,128)} %fusion.11), calls=%async_computation.9 | async-start | bytes 393216 | tf_op jit(solution)/shard_map/all_to_all | solution.py:46
  289.6 12.4 %all-to-all-done.9 = f32[16,8,384]{2,1,0:T(8,128)S(1)} async-done(((f32[16,8,384]{2,1,0:T(8,128)}), f32[16,8,384]{2,1,0:T(8,128)S(1)}, u32[]{:S(2)}, u32[]{:S(2)}) %all-to-all-start.9) | async-done | bytes 196640 | tf_op jit(solution)/shard_map/all_to_all | solution.py:46
  304.0 3.6 %all-to-all-start.10 = ((f32[16,48,128]{2,1,0:T(8,128)}), f32[16,48,128]{2,1,0:T(8,128)S(1)}, u32[]{:S(2)}, u32[]{:S(2)}) async-start(f32[16,48,128]{2,1,0:T(8,128)} %broadcast_in_dim.93), calls=%async_computation.11 | async-start | bytes 786432 | tf_op jit(solution)/shard_map/all_to_all | solution.py:33
  307.6 15.9 %all-to-all-done.10 = f32[16,48,128]{2,1,0:T(8,128)S(1)} async-done(((f32[16,48,128]{2,1,0:T(8,128)}), f32[16,48,128]{2,1,0:T(8,128)S(1)}, u32[]{:S(2)}, u32[]{:S(2)}) %all-to-all-start.10) | async-done | bytes 393248 | tf_op jit(solution)/shard_map/all_to_all | solution.py:33
  324.6 3.5 %all-to-all-start.11 = ((f32[2,24,2048]{2,1,0:T(8,128)}), f32[2,24,2048]{2,1,0:T(8,128)S(1)}, u32[]{:S(2)}, u32[]{:S(2)}) async-start(f32[2,24,2048]{2,1,0:T(8,128)} %bitcast.24), calls=%async_computation.12 | async-start | bytes 786432 | tf_op jit(solution)/shard_map/all_to_all | solution.py:138
  330.0 5.5 %all-to-all-done.11 = f32[2,24,2048]{2,1,0:T(8,128)S(1)} async-done(((f32[2,24,2048]{2,1,0:T(8,128)}), f32[2,24,2048]{2,1,0:T(8,128)S(1)}, u32[]{:S(2)}, u32[]{:S(2)}) %all-to-all-start.11) | async-done | bytes 393248 | tf_op jit(solution)/shard_map/all_to_all | solution.py:138
  (86 shorter events, 26.8 us)
Async XLA Ops:
  7.2 41.0 %copy-start = (bf16[32,2048]{1,0:T(8,128)(2,1)S(1)}, bf16[32,2048]{1,0:T(8,128)(2,1)}, u32[]{:S(2)}) copy-start(bf16[32,2048]{1,0:T(8,128)(2,1)} %param.6) | copy-start | bytes 393220
  7.2 88.9 %copy-start.7 = (bf16[384,4096]{1,0:T(8,128)(2,1)S(1)}, bf16[384,4096]{1,0:T(8,128)(2,1)}, u32[]{:S(2)}) copy-start(bf16[384,4096]{1,0:T(8,128)(2,1)} %param.10) | copy-start | bytes 9437188
  7.2 41.0 %all-gather.11.cloned.1.call-start = ((), (), s32[]{:S(2)}) async-start(), calls=%async_computation.16 | async-start | bytes 1671168 | tf_op jit(solution)/shard_map/all_gather | solution.py:64
  7.9 77.9 %all-gather.7.cloned.1.call-start = ((), (), s32[]{:S(2)}) async-start(), calls=%async_computation.14 | async-start | bytes 1671168 | tf_op jit(solution)/shard_map/all_gather | solution.py:69
  8.7 188.4 %all-gather.9.cloned.1.call-start = ((), (), s32[]{:S(2)}) async-start(), calls=%async_computation.15 | async-start | bytes 1622016 | tf_op jit(solution)/shard_map/all_gather | solution.py:74
  89.5 20.2 %all-to-all-start = ((bf16[32,32,384]{2,1,0:T(8,128)(2,1)}), bf16[32,32,384]{2,1,0:T(8,128)(2,1)}, u32[]{:S(2)}, u32[]{:S(2)}) async-start(bf16[32,32,384]{2,1,0:T(8,128)(2,1)} %broadcast_in_dim.32), calls=%async_computation | async-start | bytes 1572864 | tf_op jit(solution)/shard_map/all_to_all | solution.py:33
  146.8 8.7 %copy-start.2 = (bf16[384,4096]{1,0:T(8,128)(2,1)S(1)}, bf16[384,4096]{1,0:T(8,128)(2,1)}, u32[]{:S(2)}) copy-start(bf16[384,4096]{1,0:T(8,128)(2,1)} %param.11) | copy-start | bytes 9437188
  151.6 11.7 %all-to-all-start.3 = ((f32[8,16,128]{2,1,0:T(8,128)}), f32[8,16,128]{2,1,0:T(8,128)S(1)}, u32[]{:S(2)}, u32[]{:S(2)}) async-start(f32[8,16,128]{2,1,0:T(8,128)} %broadcast_in_dim.38), calls=%async_computation.3 | async-start | bytes 131072 | tf_op jit(solution)/shard_map/all_to_all | solution.py:33
  155.0 122.3 %all-gather.5.cloned.1.call-start = ((), (), s32[]{:S(2)}) async-start(), calls=%async_computation.13 | async-start | bytes 2228224 | tf_op jit(solution)/shard_map/all_gather | solution.py:76
  168.0 12.5 %all-to-all-start.4 = ((f32[32,8,128]{2,1,0:T(8,128)}), f32[32,8,128]{2,1,0:T(8,128)S(1)}, u32[]{:S(2)}, u32[]{:S(2)}) async-start(f32[32,8,128]{2,1,0:T(8,128)} %broadcast_in_dim.40), calls=%async_computation.4 | async-start | bytes 262144 | tf_op jit(solution)/shard_map/all_to_all | solution.py:33
  185.3 11.7 %all-to-all-start.5 = ((f32[8,16,128]{2,1,0:T(8,128)}), f32[8,16,128]{2,1,0:T(8,128)S(1)}, u32[]{:S(2)}, u32[]{:S(2)}) async-start(f32[8,16,128]{2,1,0:T(8,128)} %broadcast_in_dim.42), calls=%async_computation.5 | async-start | bytes 131072 | tf_op jit(solution)/shard_map/all_to_all | solution.py:33
  188.6 113.4 %reduce-scatter.2.cloned.1.call-start = ((), (), s32[]{:S(2)}) async-start(), calls=%async_computation.17 | async-start | bytes 3538944 | tf_op jit(solution)/shard_map/reduce_scatter | solution.py:104
  223.3 9.2 %copy-start.4 = (f32[1024,384]{1,0:T(8,128)S(1)}, f32[1024,384]{1,0:T(8,128)}, u32[]{:S(2)}) copy-start(f32[1024,384]{1,0:T(8,128)} %all-gather.9.cloned.1.call-done) | copy-start | bytes 4718596
  230.6 1.9 copy-start.1
  236.1 1.4 copy-start.3
  243.3 27.5 %copy-start.6 = (f32[32,384]{1,0:T(8,128)S(1)}, f32[32,384]{1,0:T(8,128)}, u32[]{:S(2)}) copy-start(f32[32,384]{1,0:T(8,128)} %get-tuple-element.25) | copy-start | bytes 147460
  243.3 27.4 %all-to-all-start.7 = ((f32[32,32,384]{2,1,0:T(8,128)}), f32[32,32,384]{2,1,0:T(8,128)S(1)}, u32[]{:S(2)}, u32[]{:S(2)}) async-start(f32[32,32,384]{2,1,0:T(8,128)} %bitcast.51), calls=%async_computation.7 | async-start | bytes 3145728 | tf_op jit(solution)/shard_map/all_to_all | solution.py:46
  271.9 12.0 %all-to-all-start.8 = ((bf16[16,32,384]{2,1,0:T(8,128)(2,1)}), bf16[16,32,384]{2,1,0:T(8,128)(2,1)S(1)}, u32[]{:S(2)}, u32[]{:S(2)}) async-start(bf16[16,32,384]{2,1,0:T(8,128)(2,1)} %broadcast_in_dim.45), calls=%async_computation.8 | async-start | bytes 786432 | tf_op jit(solution)/shard_map/all_to_all | solution.py:33
  284.7 17.3 %all-to-all-start.9 = ((f32[16,8,384]{2,1,0:T(8,128)}), f32[16,8,384]{2,1,0:T(8,128)S(1)}, u32[]{:S(2)}, u32[]{:S(2)}) async-start(f32[16,8,384]{2,1,0:T(8,128)} %fusion.11), calls=%async_computation.9 | async-start | bytes 393216 | tf_op jit(solution)/shard_map/all_to_all | solution.py:46
  302.1 21.7 %copy-start.5 = (f32[48,2048]{1,0:T(8,128)S(1)}, f32[48,2048]{1,0:T(8,128)}, u32[]{:S(2)}) copy-start(f32[48,2048]{1,0:T(8,128)} %reduce-scatter.2.cloned.1.call-done) | copy-start | bytes 1179652
  304.0 19.5 %all-to-all-start.10 = ((f32[16,48,128]{2,1,0:T(8,128)}), f32[16,48,128]{2,1,0:T(8,128)S(1)}, u32[]{:S(2)}, u32[]{:S(2)}) async-start(f32[16,48,128]{2,1,0:T(8,128)} %broadcast_in_dim.93), calls=%async_computation.11 | async-start | bytes 786432 | tf_op jit(solution)/shard_map/all_to_all | solution.py:33
  324.6 10.8 %all-to-all-start.11 = ((f32[2,24,2048]{2,1,0:T(8,128)}), f32[2,24,2048]{2,1,0:T(8,128)S(1)}, u32[]{:S(2)}, u32[]{:S(2)}) async-start(f32[2,24,2048]{2,1,0:T(8,128)} %bitcast.24), calls=%async_computation.12 | async-start | bytes 786432 | tf_op jit(solution)/shard_map/all_to_all | solution.py:138
Sparse Core Ops, SparseCore 0:
  9.9 38.2 all-gather.10
  50.0 35.7 all-gather.6
  89.0 49.9 all-gather.8
  157.4 35.3 all-gather.4
  236.3 40.3 reduce-scatter.1

commit v2 on v1

--- a/solution.py
+++ b/solution.py
@@ -46,6 +46,23 @@
     return jnp.sum(lax.all_to_all(blocks, axes, 0, 0, tiled=True), axis=0)
 
 
+def project_split(hidden, weight):
+    rows, depth = hidden.shape[0], weight.shape[0]
+    yl, x, c = (lax.axis_size(axis) for axis in SHARD)
+    share = spread(weight, ("yl", "c")).reshape(yl * c * depth, -1)
+    pieces = hidden.reshape(rows, yl, x, c, depth).transpose(2, 0, 1, 3, 4)
+    pieces = lax.all_to_all(pieces.reshape(x, rows, -1), "x", 0, 0, tiled=True)
+    part = jnp.dot(pieces.reshape(x * rows, -1), share, preferred_element_type=jnp.float32)
+    return scatter_sum(part, "x")
+
+
+def swap(block):
+    count = lax.axis_size("yh")
+    parts = block.reshape((count, -1, block.shape[1]))
+    parts = lax.all_to_all(parts, "yh", 0, 0, tiled=True)
+    return jnp.concatenate([parts[i] for i in range(count)], axis=1)
+
+
 def norm_backward(dzhat, unit_s, norm_s):
     inner = jnp.sum(unit_s * dzhat, axis=1, keepdims=True)
     return ((dzhat - unit_s * inner) / norm_s).astype(jnp.bfloat16)
@@ -57,20 +74,16 @@
     side = lax.axis_index("yh")
     first = side * half
     v_t, _ = unit_columns(lax.dynamic_slice_in_dim(proto_teacher, first, half, 1))
-    v_s, col_norm = unit_columns(lax.dynamic_slice_in_dim(proto_student, first, half, 1))
+    v_all, norm_all = unit_columns(proto_student)
+    v_s = lax.dynamic_slice_in_dim(v_all, first, half, 1)
+    v_t, v_s = lax.optimization_barrier((v_t, v_s))
 
-    y_t = jnp.dot(
-        hid_teacher,
-        lax.all_gather(proj_teacher, SHARD, axis=0, tiled=True),
-        preferred_element_type=jnp.float32,
-    )
-    y_s = jnp.dot(
-        hid_student,
-        lax.all_gather(proj_student, SHARD, axis=0, tiled=True),
-        preferred_element_type=jnp.float32,
-    )
+    y_t = project_split(hid_teacher, proj_teacher)
+    z_t = spread(unit_rows(y_t)[0].astype(jnp.bfloat16), PLANE).reshape(-1, bot)
+    gathered = lax.all_gather(proj_student, SHARD, axis=0, tiled=True)
+    gathered, z_t = lax.optimization_barrier((gathered, z_t))
+    y_s = jnp.dot(hid_student, gathered, preferred_element_type=jnp.float32)
     unit_s, norm_s = unit_rows(y_s)
-    z_t = spread(unit_rows(y_t)[0].astype(jnp.bfloat16), PLANE).reshape(-1, bot)
     wide_s = lax.all_gather(y_s, PLANE, axis=0, tiled=True)
     z_s = unit_rows(wide_s)[0].astype(jnp.bfloat16)
     hid_group = lax.all_gather(hid_student, SHARD, axis=0, tiled=True)
@@ -101,15 +114,17 @@
     prob = student_exp / expsum[:, None]
     grad_logits = (GRAD_SCALE / TAU_S * (prob - target)).astype(jnp.bfloat16)
 
+    dzhat_part = lax.dot_general(
+        grad_logits, v_s, COL_DIMS, preferred_element_type=jnp.float32
+    )
+    grad_logits, dzhat_part = lax.optimization_barrier((grad_logits, dzhat_part))
     dproto = lax.psum_scatter(
         lax.dot_general(z_s, grad_logits, ROW_DIMS, preferred_element_type=jnp.float32),
         "z",
         scatter_dimension=0,
         tiled=True,
     )
-    dzhat = scatter_sum(
-        lax.dot_general(grad_logits, v_s, COL_DIMS, preferred_element_type=jnp.float32), PLANE
-    )
+    dzhat = scatter_sum(dzhat_part, PLANE)
     dy = norm_backward(dzhat, unit_s, norm_s)
     dy_group = spread(dy, SHARD).reshape(-1, bot)
     depth = proj_student.shape[0]
@@ -122,21 +137,24 @@
     own = dproto.shape[0]
     v_own = lax.dynamic_slice_in_dim(v_s, lax.axis_index("z") * own, own, 0).astype(jnp.float32)
     dots = jnp.sum(v_own * dproto, axis=0)
+    swapped = swap(dproto)
+    last = own // lax.axis_size("yh")
+    v_swapped = lax.dynamic_slice_in_dim(v_all, lax.axis_index(DP) * last, last, 0).astype(
+        jnp.float32
+    )
     flat = jnp.concatenate(
         [proj_part.reshape(-1, LANES), dots.reshape(-1, LANES), jnp.full((8, LANES), row_loss)]
     )
     parts = spread(flat, DP)
     cut = proj_part.size // LANES
     grad_proj = parts[:, :cut].reshape(-1, bot)
-    sides = parts[:, cut:].reshape(lax.axis_size("z"), lax.axis_size("yh"), -1)
-    sums = jnp.sum(lax.dynamic_index_in_dim(sides, side, 1, keepdims=False), axis=0)
-    dots = sums[:half]
+    sides = jnp.sum(
+        parts[:, cut:].reshape(lax.axis_size("z"), lax.axis_size("yh"), -1), axis=0
+    )
+    dots = sides[:, :half].reshape(-1)
     row_count = hid_teacher.shape[0] * lax.axis_size(DP + SHARD)
-    loss = sums[half] / row_count
-    grad = (dproto - v_own * dots[None, :]) / col_norm[None, :]
-    grad = grad.reshape(lax.axis_size("yh"), -1, half)
-    grad = lax.all_to_all(grad, "yh", 0, 0, tiled=True)
-    grad_proto = jnp.concatenate([grad[0], grad[1]], axis=1)
+    loss = sides[0, half] / row_count
+    grad_proto = (swapped - v_swapped * dots[None, :]) / norm_all[None, :]
     return (loss, grad_proj, grad_proto)
 
 

time: 345 us -> 308 us (0.89)
  waiting for transfers between devices: 173 us -> 87.5 us
  starting transfers between devices: 39.8 us -> 54.5 us
  other arithmetic: 31.8 us -> 45.3 us
  local copies, waits for them, and re-layouts: 11 us -> 21.1 us
  blocking collectives: 39.8 us -> 49.5 us
    all_gather x2 -> x1, waiting for transfers between devices: 75.3 us -> 0.01 us  [local(): gathered = lax.all_gather(proj_student, SHARD, axis=0, tiled=True)]
    all_to_all x6, waiting for transfers between devices: 56 us -> 41.6 us  [spread(): lax.all_to_all(jnp.broadcast_to(block[None], (count,) + block.shape), axe...]
    all_to_all x3 -> x4, blocking collectives: 39.8 us -> 49.5 us  [spread(): lax.all_to_all(jnp.broadcast_to(block[None], (count,) + block.shape), axe...]
    all_to_all x1 -> x2, starting transfers between devices: 3.47 us -> 9.03 us  [the longest x1 5.56 us: project_split(): pieces = lax.all_to_all(pieces.reshape(x, rows, -1), 'x', 0, 0, tiled=True)]
    all_to_all x2 -> x3, starting transfers between devices: 8.73 us -> 14.3 us  [scatter_sum(): return jnp.sum(lax.all_to_all(blocks, axes, 0, 0, tiled=True), axis=0)]
    reduce_sum x2, other arithmetic: 0.69 us -> 5.06 us  [unit_columns(): norm = jnp.sqrt(jnp.sum(wide * wide, axis=0) + EPS)]
    all_to_all x2 -> x3, waiting for transfers between devices: 34.5 us -> 38.3 us  [scatter_sum(): return jnp.sum(lax.all_to_all(blocks, axes, 0, 0, tiled=True), axis=0)]
    all_to_all x6, starting transfers between devices: 27.3 us -> 30.9 us  [spread(): lax.all_to_all(jnp.broadcast_to(block[None], (count,) + block.shape), axe...]
  transfers between devices with their start and end apart: 14 -> 15, of which waited for: 11 -> 11; matrix products, arithmetic and copies ran while one was open for 19% -> 25% of each run, Pallas kernels for 0% -> 0%
where the time goes in v2:
time: 308 us; the launch traced here: 306 us
  waiting for transfers between devices  87.5 us (28%)
  starting transfers between devices  54.5 us (18%)
  blocking collectives  49.5 us (16%)
  other arithmetic  45.3 us (15%)
  matrix products  31.9 us (10%)
  local copies, waits for them, and re-layouts  21.1 us (7%)
  between operations  16 us (5%)
    all_to_all x4, blocking collectives, spread(): lax.all_to_all(jnp.broadcast_to(block[None], (count,) + block.shape), axe...  49.5 us
    all_to_all x6, waiting for transfers between devices, spread(): lax.all_to_all(jnp.broadcast_to(block[None], (count,) + block.shape), axe...  41.6 us
    all_to_all x3, waiting for transfers between devices, scatter_sum(): return jnp.sum(lax.all_to_all(blocks, axes, 0, 0, tiled=True), axis=0)  38.3 us
    all_to_all x6, starting transfers between devices, spread(): lax.all_to_all(jnp.broadcast_to(block[None], (count,) + block.shape), axe...  30.9 us
    all_to_all x3, starting transfers between devices, scatter_sum(): return jnp.sum(lax.all_to_all(blocks, axes, 0, 0, tiled=True), axis=0)  14.3 us
    dot_general x1, matrix products, local(): scores = jnp.dot(z_s, v_s, preferred_element_type=jnp.float32)  10.9 us
    reduce_sum x2, other arithmetic, local(): jnp.sum(teacher_exp * col_scale[None, :], axis=1)  8.05 us
    reduce_sum x2, other arithmetic, local(): jnp.sum(row_scale[:, None] * teacher_exp, axis=0)  8.01 us
  transfers between devices with their start and end apart: 15, of which 11 were waited for; matrix products, arithmetic and copies ran while one was open for 25% of the time, Pallas kernels for 0%

profile of v2, /device:TPU:2, one launch (start us, length us, event | category | flops | bytes accessed | tf_op | source)
XLA Modules:
  0.0 305.6 jit_solution(12082158681994660959)
XLA Ops:
  9.1 5.6 %all-to-all-start = ((bf16[4,32,512]{2,1,0:T(8,128)(2,1)}), bf16[4,32,512]{2,1,0:T(8,128)(2,1)S(1)}, u32[]{:S(2)}, u32[]{:S(2)}) async-start(bf16[4,32,512]{2,1,0:T(8,128)(2,1)} %reshape.152), calls=%async_computation | async-start | bytes 262144 | tf_op jit(solution)/shard_map/all_to_all | solution.py:54
  20.0 3.5 %all-to-all-start.1 = ((bf16[4,128,384]{2,1,0:T(8,128)(2,1)}), bf16[4,128,384]{2,1,0:T(8,128)(2,1)S(1)}, u32[]{:S(2)}, u32[]{:S(2)}) async-start(bf16[4,128,384]{2,1,0:T(8,128)(2,1)} %broadcast_in_dim.34), calls=%async_computation.1 | async-start | bytes 786432 | tf_op jit(solution)/shard_map/all_to_all | solution.py:33
  32.7 4.8 %all-to-all-start.2 = ((f32[4,32,384]{2,1,0:T(8,128)}), f32[4,32,384]{2,1,0:T(8,128)S(1)}, u32[]{:S(2)}, u32[]{:S(2)}) async-start(f32[4,32,384]{2,1,0:T(8,128)} %fusion.13), calls=%async_computation.2 | async-start | bytes 393216 | tf_op jit(solution)/shard_map/all_to_all | solution.py:46
  38.2 4.9 %all-to-all-done.2 = f32[4,32,384]{2,1,0:T(8,128)S(1)} async-done(((f32[4,32,384]{2,1,0:T(8,128)}), f32[4,32,384]{2,1,0:T(8,128)S(1)}, u32[]{:S(2)}, u32[]{:S(2)}) %all-to-all-start.2) | async-done | bytes 196640 | tf_op jit(solution)/shard_map/all_to_all | solution.py:46
  44.3 6.3 %all-to-all-start.3 = ((bf16[32,32,384]{2,1,0:T(8,128)(2,1)}), bf16[32,32,384]{2,1,0:T(8,128)(2,1)}, u32[]{:S(2)}, u32[]{:S(2)}) async-start(bf16[32,32,384]{2,1,0:T(8,128)(2,1)} %broadcast_in_dim.35), calls=%async_computation.3 | async-start | bytes 1572864 | tf_op jit(solution)/shard_map/all_to_all | solution.py:33
  54.7 9.6 %all-to-all-done.3 = bf16[32,32,384]{2,1,0:T(8,128)(2,1)} async-done(((bf16[32,32,384]{2,1,0:T(8,128)(2,1)}), bf16[32,32,384]{2,1,0:T(8,128)(2,1)}, u32[]{:S(2)}, u32[]{:S(2)}) %all-to-all-start.3) | async-done | bytes 786464 | tf_op jit(solution)/shard_map/all_to_all | solution.py:33
  64.3 7.3 %fusion.12 = (f32[2048]{0:T(1024)S(1)}, f32[1024,2048]{1,0:T(8,128)}) fusion(bf16[1024,384]{1,0:T(8,128)(2,1)} %bitcast.5, bf16[384,2048]{1,0:T(8,128)(2,1)} %fusion.4), kind=kOutput, calls=%fused_computation.58 | convolution fusion | flops 1614804992 | bytes 10756096 | tf_op jit(solution)/shard_map/dot_general | solution.py:91
  72.2 8.0 %all-to-all-start.4 = ((f32[8,16,128]{2,1,0:T(8,128)}), f32[8,16,128]{2,1,0:T(8,128)S(1)}, u32[]{:S(2)}, u32[]{:S(2)}) async-start(f32[8,16,128]{2,1,0:T(8,128)} %broadcast_in_dim.37), calls=%async_computation.4 | async-start | bytes 131072 | tf_op jit(solution)/shard_map/all_to_all | solution.py:33
  83.3 5.3 %all-to-all-done.4 = f32[8,16,128]{2,1,0:T(8,128)S(1)} async-done(((f32[8,16,128]{2,1,0:T(8,128)}), f32[8,16,128]{2,1,0:T(8,128)S(1)}, u32[]{:S(2)}, u32[]{:S(2)}) %all-to-all-start.4) | async-done | bytes 65568 | tf_op jit(solution)/shard_map/all_to_all | solution.py:33
  88.6 4.0 %multiply_reduce_fusion.4 = f32[1024]{0:T(1024)S(1)} fusion(f32[1024,2048]{1,0:T(8,128)} %get-tuple-element.32, f32[2048]{0:T(1024)S(1)} %divide_bitcast_fusion.2), kind=kLoop, calls=%fused_computation.5 | loop fusion | flops 4193280 | bytes 8400896 | tf_op jit(solution)/shard_map/reduce_sum | solution.py:95
  92.7 11.2 %all_to_all.75 = f32[32,8,128]{2,1,0:T(8,128)S(1)} all-to-all(f32[32,8,128]{2,1,0:T(8,128)S(1)} %broadcast_in_dim.39), channel_id=1, replica_groups=mesh['z'=8,'yh'=2,'yl'=2,'x'=4,'c'=2] {'yh','yl','x','c'}, dimensions={0} | all-to-all | bytes 262144 | tf_op jit(solution)/shard_map/all_to_all | solution.py:33
  103.9 4.0 %multiply_reduce_fusion.3 = f32[2048]{0:T(1024)S(1)} fusion(f32[1024,2048]{1,0:T(8,128)} %get-tuple-element.32, f32[1024]{0:T(1024)S(1)} %divide_bitcast_fusion.4), kind=kLoop, calls=%fused_computation.4 | loop fusion | flops 4192256 | bytes 8400896 | tf_op jit(solution)/shard_map/reduce_sum | solution.py:96
  107.9 10.8 %all_to_all.76 = f32[8,16,128]{2,1,0:T(8,128)S(1)} all-to-all(f32[8,16,128]{2,1,0:T(8,128)S(1)} %broadcast_in_dim.41), channel_id=1, replica_groups=mesh['z'=8,'yh'=2,'yl'=2,'x'=4,'c'=2] {'z'}, dimensions={0} | all-to-all | bytes 131072 | tf_op jit(solution)/shard_map/all_to_all | solution.py:33
  118.7 4.0 %multiply_reduce_fusion.2 = f32[1024]{0:T(1024)S(1)} fusion(f32[1024,2048]{1,0:T(8,128)} %get-tuple-element.32, f32[2048]{0:T(1024)S(1)} %divide_bitcast_fusion.1), kind=kLoop, calls=%fused_computation.3 | loop fusion | flops 4193280 | bytes 8400896 | tf_op jit(solution)/shard_map/reduce_sum | solution.py:95
  122.8 11.4 %all_to_all.77 = f32[32,8,128]{2,1,0:T(8,128)S(1)} all-to-all(f32[32,8,128]{2,1,0:T(8,128)S(1)} %broadcast_in_dim.43), channel_id=1, replica_groups=mesh['z'=8,'yh'=2,'yl'=2,'x'=4,'c'=2] {'yh','yl','x','c'}, dimensions={0} | all-to-all | bytes 262144 | tf_op jit(solution)/shard_map/all_to_all | solution.py:33
  134.2 4.0 %multiply_reduce_fusion.1 = f32[2048]{0:T(1024)S(1)} fusion(f32[1024,2048]{1,0:T(8,128)} %get-tuple-element.32, f32[1024]{0:T(1024)S(1)} %divide_bitcast_fusion.3), kind=kLoop, calls=%fused_computation.2 | loop fusion | flops 4192256 | bytes 8400896 | tf_op jit(solution)/shard_map/reduce_sum | solution.py:96
  138.9 3.4 %all-to-all-start.8 = ((f32[8,16,128]{2,1,0:T(8,128)}), f32[8,16,128]{2,1,0:T(8,128)S(1)}, u32[]{:S(2)}, u32[]{:S(2)}) async-start(f32[8,16,128]{2,1,0:T(8,128)} %broadcast_in_dim.45), calls=%async_computation.8 | async-start | bytes 131072 | tf_op jit(solution)/shard_map/all_to_all | solution.py:33
  143.2 7.3 %all-to-all-done.8 = f32[8,16,128]{2,1,0:T(8,128)S(1)} async-done(((f32[8,16,128]{2,1,0:T(8,128)}), f32[8,16,128]{2,1,0:T(8,128)S(1)}, u32[]{:S(2)}, u32[]{:S(2)}) %all-to-all-start.8) | async-done | bytes 65568 | tf_op jit(solution)/shard_map/all_to_all | solution.py:33
  152.2 10.9 %multiply_reduce_fusion.5 = (f32[1024]{0:T(1024)S(1)}, f32[1024]{0:T(1024)S(1)}, f32[1024]{0:T(1024)S(1)}, f32[1024,2048]{1,0:T(8,128)}) fusion(f32[1024,2048]{1,0:T(8,128)} %get-tuple-element.32, f32[2048]{0:T(1024)S(1)} %divide_bitcast_fusion, bf16[384,2048]{1,0:T(8,128)(2,1)} %constant_dynamic-slice_fusion, ...), kind=kOutput, calls=%fused_computation.11 | convolution fusion | flops 1623979008 | bytes 19947520 | tf_op jit(solution)/shard_map/dot_general | solution.py:97
  163.2 16.1 %all_to_all.78 = f32[32,24,128]{2,1,0:T(8,128)S(1)} all-to-all(f32[32,24,128]{2,1,0:T(8,128)S(1)} %broadcast_in_dim.47), channel_id=1, replica_groups=mesh['z'=8,'yh'=2,'yl'=2,'x'=4,'c'=2] {'yh','yl','x','c'}, dimensions={0} | all-to-all | bytes 786432 | tf_op jit(solution)/shard_map/all_to_all | solution.py:33
  181.3 7.2 %multiply_convert_fusion = bf16[1024,2048]{1,0:T(8,128)(2,1)S(1)} fusion(f32[1024,2048]{1,0:T(8,128)} %get-tuple-element.33, f32[1024,2048]{1,0:T(8,128)} %get-tuple-element.32, f32[1024]{0:T(1024)S(1)} %get-tuple-element.17, f32[1024]{0:T(1024)S(1)} %get-tuple-element.16, f32[2048]{0:T(1024)} %copy-done.11), kind=kLoop, calls=%fused_computation | loop fusion | flops 14680064 | bytes 20987904 | tf_op jit(solution)/shard_map/convert_element_type | solution.py:115
  188.6 3.5 %fusion.14 = f32[1024,384]{1,0:T(8,128)} fusion(bf16[1024,2048]{1,0:T(8,128)(2,1)S(1)} %multiply_convert_fusion, bf16[384,2048]{1,0:T(8,128)(2,1)S(1)} %copy-done.3), kind=kOutput, calls=%fused_computation.60 | convolution fusion | flops 1610612736 | bytes 7340032 | tf_op jit(solution)/shard_map/dot_general | solution.py:117
  192.1 3.6 %fusion.9 = f32[384,2048]{1,0:T(8,128)} fusion(bf16[1024,2048]{1,0:T(8,128)(2,1)S(1)} %multiply_convert_fusion, f32[1024,384]{1,0:T(8,128)S(1)} %copy-done.4, f32[1024]{0:T(1024)S(1)} %copy-done.13), kind=kOutput, calls=%fused_computation.55 | convolution fusion | flops 1611399168 | bytes 8916992 | tf_op jit(solution)/shard_map/dot_general | solution.py:122
  195.8 6.0 %all-to-all-start.10 = ((f32[32,32,384]{2,1,0:T(8,128)}), f32[32,32,384]{2,1,0:T(8,128)}, u32[]{:S(2)}, u32[]{:S(2)}) async-start(f32[32,32,384]{2,1,0:T(8,128)} %bitcast.63), calls=%async_computation.10 | async-start | bytes 3145728 | tf_op jit(solution)/shard_map/all_to_all | solution.py:46
  201.8 22.2 %all-to-all-done.10 = f32[32,32,384]{2,1,0:T(8,128)} async-done(((f32[32,32,384]{2,1,0:T(8,128)}), f32[32,32,384]{2,1,0:T(8,128)}, u32[]{:S(2)}, u32[]{:S(2)}) %all-to-all-start.10) | async-done | bytes 1572896 | tf_op jit(solution)/shard_map/all_to_all | solution.py:46
  226.5 5.5 %all-to-all-start.11 = ((bf16[16,32,384]{2,1,0:T(8,128)(2,1)}), bf16[16,32,384]{2,1,0:T(8,128)(2,1)S(1)}, u32[]{:S(2)}, u32[]{:S(2)}) async-start(bf16[16,32,384]{2,1,0:T(8,128)(2,1)} %broadcast_in_dim.48), calls=%async_computation.11 | async-start | bytes 786432 | tf_op jit(solution)/shard_map/all_to_all | solution.py:33
  240.3 3.5 %all-to-all-start.12 = ((f32[16,8,384]{2,1,0:T(8,128)}), f32[16,8,384]{2,1,0:T(8,128)S(1)}, u32[]{:S(2)}, u32[]{:S(2)}) async-start(f32[16,8,384]{2,1,0:T(8,128)} %fusion.6), calls=%async_computation.12 | async-start | bytes 393216 | tf_op jit(solution)/shard_map/all_to_all | solution.py:46
  246.4 11.2 %all-to-all-done.12 = f32[16,8,384]{2,1,0:T(8,128)S(1)} async-done(((f32[16,8,384]{2,1,0:T(8,128)}), f32[16,8,384]{2,1,0:T(8,128)S(1)}, u32[]{:S(2)}, u32[]{:S(2)}) %all-to-all-start.12) | async-done | bytes 196640 | tf_op jit(solution)/shard_map/all_to_all | solution.py:46
  258.2 3.5 %all-to-all-start.14 = ((f32[2,24,2048]{2,1,0:T(8,128)}), f32[2,24,2048]{2,1,0:T(8,128)S(1)}, u32[]{:S(2)}, u32[]{:S(2)}) async-start(f32[2,24,2048]{2,1,0:T(8,128)} %bitcast.64), calls=%async_computation.15 | async-start | bytes 786432 | tf_op jit(solution)/shard_map/all_to_all | solution.py:62
  264.2 4.9 %all-to-all-done.14 = f32[2,24,2048]{2,1,0:T(8,128)S(1)} async-done(((f32[2,24,2048]{2,1,0:T(8,128)}), f32[2,24,2048]{2,1,0:T(8,128)S(1)}, u32[]{:S(2)}, u32[]{:S(2)}) %all-to-all-start.14) | async-done | bytes 393248 | tf_op jit(solution)/shard_map/all_to_all | solution.py:62
  270.6 4.2 %all-to-all-start.13 = ((f32[16,48,128]{2,1,0:T(8,128)}), f32[16,48,128]{2,1,0:T(8,128)}, u32[]{:S(2)}, u32[]{:S(2)}) async-start(f32[16,48,128]{2,1,0:T(8,128)} %broadcast_in_dim.99), calls=%async_computation.14 | async-start | bytes 786432 | tf_op jit(solution)/shard_map/all_to_all | solution.py:33
  275.6 13.8 %all-to-all-done.13 = f32[16,48,128]{2,1,0:T(8,128)} async-done(((f32[16,48,128]{2,1,0:T(8,128)}), f32[16,48,128]{2,1,0:T(8,128)}, u32[]{:S(2)}, u32[]{:S(2)}) %all-to-all-start.13) | async-done | bytes 393248 | tf_op jit(solution)/shard_map/all_to_all | solution.py:33
  (110 shorter events, 58.2 us)
Async XLA Ops:
  7.2 16.3 %copy-start = (bf16[384,4096]{1,0:T(8,128)(2,1)S(1)}, bf16[384,4096]{1,0:T(8,128)(2,1)}, u32[]{:S(2)}) copy-start(bf16[384,4096]{1,0:T(8,128)(2,1)} %param.11) | copy-start | bytes 9437188
  7.2 12.1 %copy-start.8 = (bf16[128,384]{1,0:T(8,128)(2,1)S(1)}, bf16[128,384]{1,0:T(8,128)(2,1)}, u32[]{:S(2)}) copy-start(bf16[128,384]{1,0:T(8,128)(2,1)} %param.8) | copy-start | bytes 294916
  9.1 10.1 %all-to-all-start = ((bf16[4,32,512]{2,1,0:T(8,128)(2,1)}), bf16[4,32,512]{2,1,0:T(8,128)(2,1)S(1)}, u32[]{:S(2)}, u32[]{:S(2)}) async-start(bf16[4,32,512]{2,1,0:T(8,128)(2,1)} %reshape.152), calls=%async_computation | async-start | bytes 262144 | tf_op jit(solution)/shard_map/all_to_all | solution.py:54
  14.7 49.6 %all-gather.6.cloned.1.call-start = ((), (), s32[]{:S(2)}) async-start(), calls=%async_computation.17 | async-start | bytes 1671168 | tf_op jit(solution)/shard_map/all_gather | solution.py:83
  19.2 0.8 copy-start.7
  20.0 10.9 %all-to-all-start.1 = ((bf16[4,128,384]{2,1,0:T(8,128)(2,1)}), bf16[4,128,384]{2,1,0:T(8,128)(2,1)S(1)}, u32[]{:S(2)}, u32[]{:S(2)}) async-start(bf16[4,128,384]{2,1,0:T(8,128)(2,1)} %broadcast_in_dim.34), calls=%async_computation.1 | async-start | bytes 786432 | tf_op jit(solution)/shard_map/all_to_all | solution.py:33
  26.0 24.6 %copy-start.1 = (bf16[384,4096]{1,0:T(8,128)(2,1)S(1)}, bf16[384,4096]{1,0:T(8,128)(2,1)}, u32[]{:S(2)}) copy-start(bf16[384,4096]{1,0:T(8,128)(2,1)} %fusion.2) | copy-start | bytes 9437188
  32.7 10.4 %all-to-all-start.2 = ((f32[4,32,384]{2,1,0:T(8,128)}), f32[4,32,384]{2,1,0:T(8,128)S(1)}, u32[]{:S(2)}, u32[]{:S(2)}) async-start(f32[4,32,384]{2,1,0:T(8,128)} %fusion.13), calls=%async_computation.2 | async-start | bytes 393216 | tf_op jit(solution)/shard_map/all_to_all | solution.py:46
  44.3 20.0 %all-to-all-start.3 = ((bf16[32,32,384]{2,1,0:T(8,128)(2,1)}), bf16[32,32,384]{2,1,0:T(8,128)(2,1)}, u32[]{:S(2)}, u32[]{:S(2)}) async-start(bf16[32,32,384]{2,1,0:T(8,128)(2,1)} %broadcast_in_dim.35), calls=%async_computation.3 | async-start | bytes 1572864 | tf_op jit(solution)/shard_map/all_to_all | solution.py:33
  50.7 2.5 copy-start.2
  64.3 16.0 %copy-start.6 = (bf16[32,2048]{1,0:T(8,128)(2,1)S(1)}, bf16[32,2048]{1,0:T(8,128)(2,1)}, u32[]{:S(2)}) copy-start(bf16[32,2048]{1,0:T(8,128)(2,1)} %param.7) | copy-start | bytes 393220
  72.2 16.4 %all-to-all-start.4 = ((f32[8,16,128]{2,1,0:T(8,128)}), f32[8,16,128]{2,1,0:T(8,128)S(1)}, u32[]{:S(2)}, u32[]{:S(2)}) async-start(f32[8,16,128]{2,1,0:T(8,128)} %broadcast_in_dim.37), calls=%async_computation.4 | async-start | bytes 131072 | tf_op jit(solution)/shard_map/all_to_all | solution.py:33
  80.2 70.3 %all-gather.8.cloned.1.call-start = ((), (), s32[]{:S(2)}) async-start(), calls=%async_computation.18 | async-start | bytes 1622016 | tf_op jit(solution)/shard_map/all_gather | solution.py:87
  138.9 11.7 %all-to-all-start.8 = ((f32[8,16,128]{2,1,0:T(8,128)}), f32[8,16,128]{2,1,0:T(8,128)S(1)}, u32[]{:S(2)}, u32[]{:S(2)}) async-start(f32[8,16,128]{2,1,0:T(8,128)} %broadcast_in_dim.45), calls=%async_computation.8 | async-start | bytes 131072 | tf_op jit(solution)/shard_map/all_to_all | solution.py:33
  142.2 89.8 %all-gather.4.cloned.1.call-start = ((), (), s32[]{:S(2)}) async-start(), calls=%async_computation.16 | async-start | bytes 2228224 | tf_op jit(solution)/shard_map/all_gather | solution.py:89
  143.0 115.3 %reduce-scatter.2.cloned.1.call-start = ((), (), s32[]{:S(2)}) async-start(), calls=%async_computation.19 | async-start | bytes 3538944 | tf_op jit(solution)/shard_map/reduce_scatter | solution.py:121
  150.5 12.6 %copy-start.11 = (f32[2048]{0:T(1024)}, f32[2048]{0:T(1024)S(1)}, u32[]{:S(2)}) copy-start(f32[2048]{0:T(1024)S(1)} %divide_bitcast_fusion) | copy-start | bytes 24580
  152.2 10.9 %copy-start.12 = (f32[1024]{0:T(1024)}, f32[1024]{0:T(1024)S(1)}, u32[]{:S(2)}) copy-start(f32[1024]{0:T(1024)S(1)} %add_sqrt_fusion.2) | copy-start | bytes 12292
  181.3 7.3 %copy-start.9 = (f32[1024]{0:T(1024)}, f32[1024]{0:T(1024)S(1)}, u32[]{:S(2)}) copy-start(f32[1024]{0:T(1024)S(1)} %get-tuple-element.16) | copy-start | bytes 12292
  181.3 7.3 %copy-start.10 = (f32[1024]{0:T(1024)}, f32[1024]{0:T(1024)S(1)}, u32[]{:S(2)}) copy-start(f32[1024]{0:T(1024)S(1)} %get-tuple-element.17) | copy-start | bytes 12292
  181.3 7.3 %copy-start.3 = (bf16[384,2048]{1,0:T(8,128)(2,1)S(1)}, bf16[384,2048]{1,0:T(8,128)(2,1)}, u32[]{:S(2)}) copy-start(bf16[384,2048]{1,0:T(8,128)(2,1)} %constant_dynamic-slice_fusion) | copy-start | bytes 4718596
  188.6 3.5 %copy-start.4 = (f32[1024,384]{1,0:T(8,128)S(1)}, f32[1024,384]{1,0:T(8,128)}, u32[]{:S(2)}) copy-start(f32[1024,384]{1,0:T(8,128)} %all-gather.8.cloned.1.call-done) | copy-start | bytes 4718596
  188.6 3.5 %copy-start.13 = (f32[1024]{0:T(1024)S(1)}, f32[1024]{0:T(1024)}, u32[]{:S(2)}) copy-start(f32[1024]{0:T(1024)} %copy-done.12) | copy-start | bytes 12292
  195.7 6.0 %copy-start.14 = (f32[32]{0:T(128)S(1)}, f32[32]{0:T(128)}, u32[]{:S(2)}) copy-start(f32[32]{0:T(128)} %get-tuple-element.34) | copy-start | bytes 388
  195.7 29.7 %copy-start.5 = (f32[32,384]{1,0:T(8,128)S(1)}, f32[32,384]{1,0:T(8,128)}, u32[]{:S(2)}) copy-start(f32[32,384]{1,0:T(8,128)} %get-tuple-element.35) | copy-start | bytes 147460
  195.8 28.2 %all-to-all-start.10 = ((f32[32,32,384]{2,1,0:T(8,128)}), f32[32,32,384]{2,1,0:T(8,128)}, u32[]{:S(2)}, u32[]{:S(2)}) async-start(f32[32,32,384]{2,1,0:T(8,128)} %bitcast.63), calls=%async_computation.10 | async-start | bytes 3145728 | tf_op jit(solution)/shard_map/all_to_all | solution.py:46
  226.5 12.0 %all-to-all-start.11 = ((bf16[16,32,384]{2,1,0:T(8,128)(2,1)}), bf16[16,32,384]{2,1,0:T(8,128)(2,1)S(1)}, u32[]{:S(2)}, u32[]{:S(2)}) async-start(bf16[16,32,384]{2,1,0:T(8,128)(2,1)} %broadcast_in_dim.48), calls=%async_computation.11 | async-start | bytes 786432 | tf_op jit(solution)/shard_map/all_to_all | solution.py:33
  240.3 17.3 %all-to-all-start.12 = ((f32[16,8,384]{2,1,0:T(8,128)}), f32[16,8,384]{2,1,0:T(8,128)S(1)}, u32[]{:S(2)}, u32[]{:S(2)}) async-start(f32[16,8,384]{2,1,0:T(8,128)} %fusion.6), calls=%async_computation.12 | async-start | bytes 393216 | tf_op jit(solution)/shard_map/all_to_all | solution.py:46
  258.2 10.9 %all-to-all-start.14 = ((f32[2,24,2048]{2,1,0:T(8,128)}), f32[2,24,2048]{2,1,0:T(8,128)S(1)}, u32[]{:S(2)}, u32[]{:S(2)}) async-start(f32[2,24,2048]{2,1,0:T(8,128)} %bitcast.64), calls=%async_computation.15 | async-start | bytes 786432 | tf_op jit(solution)/shard_map/all_to_all | solution.py:62
  270.6 18.8 %all-to-all-start.13 = ((f32[16,48,128]{2,1,0:T(8,128)}), f32[16,48,128]{2,1,0:T(8,128)}, u32[]{:S(2)}, u32[]{:S(2)}) async-start(f32[16,48,128]{2,1,0:T(8,128)} %broadcast_in_dim.99), calls=%async_computation.14 | async-start | bytes 786432 | tf_op jit(solution)/shard_map/all_to_all | solution.py:33
Sparse Core Ops, SparseCore 0:
  17.4 39.1 all-gather.5
  84.2 47.0 all-gather.7
  144.9 37.9 all-gather.3
  195.9 40.8 reduce-scatter.1

commit v3 on v2

--- a/solution.py
+++ b/solution.py
@@ -1,6 +1,10 @@
+import functools
+
 import jax
 import jax.numpy as jnp
 from jax import lax
+from jax.experimental import pallas as pl
+from jax.experimental.pallas import tpu as pltpu
 from jax.sharding import Mesh, PartitionSpec as P
 
 ITERS = 3
@@ -9,6 +13,9 @@
 TAU_S = 0.1
 EPS = 1e-06
 LANES = 128
+ROWS_BLOCK = 256
+CHUNK = 512
+VMEM_LIMIT = 32 * 1024 * 1024
 ROW_DIMS = (((0,), (0,)), ((), ()))
 COL_DIMS = (((1,), (1,)), ((), ()))
 
@@ -28,15 +35,15 @@
     return ((wide / norm).astype(jnp.bfloat16), norm)
 
 
+def exchange(blocks, axes):
+    return lax.all_to_all(blocks, axes, 0, 0, tiled=True)
+
+
 def spread(block, axes):
     count = lax.axis_size(axes)
     return lax.all_to_all(
         jnp.broadcast_to(block[None], (count,) + block.shape), axes, 0, 0, tiled=True
     )
-
-
-def total(vector, axes):
-    return jnp.sum(spread(vector.reshape(-1, LANES), axes), axis=0).reshape(vector.shape)
 
 
 def scatter_sum(parts, axes):
@@ -57,10 +64,290 @@
 
 
 def swap(block):
-    count = lax.axis_size("yh")
-    parts = block.reshape((count, -1, block.shape[1]))
-    parts = lax.all_to_all(parts, "yh", 0, 0, tiled=True)
-    return jnp.concatenate([parts[i] for i in range(count)], axis=1)
+    side, count = lax.axis_index("yh"), lax.axis_size("yh")
+    rows = block.shape[0] // count
+    kept = lax.dynamic_slice_in_dim(block, side * rows, rows, 0)
+    sent = lax.dynamic_slice_in_dim(block, (1 - side) * rows, rows, 0)
+    got = lax.ppermute(sent, "yh", [(0, 1), (1, 0)])
+    return jnp.where(
+        side == 0,
+        jnp.concatenate([kept, got], axis=1),
+        jnp.concatenate([got, kept], axis=1),
+    )
+
+
+def lane_rows(row):
+    return jnp.concatenate(
+        [row[:, i * LANES : (i + 1) * LANES] for i in range(row.shape[1] // LANES)], axis=0
+    )
+
+
+def one_row(block):
+    return jnp.concatenate([block[i : i + 1] for i in range(block.shape[0])], axis=1)
+
+
+def down(block):
+    return jnp.concatenate(
+        [
+            jnp.broadcast_to(block[i : i + 1], (LANES, LANES)).T
+            for i in range(block.shape[0])
+        ],
+        axis=0,
+    )
+
+
+def lane_sums(wide):
+    ones = jnp.ones((8, LANES), jnp.float32)
+    row = lax.dot_general(
+        ones, wide, COL_DIMS, precision=lax.Precision.HIGHEST, preferred_element_type=jnp.float32
+    )
+    return lane_rows(row[0:1])
+
+
+def fold_lanes(wide):
+    pieces = [wide[:, i * LANES : (i + 1) * LANES] for i in range(wide.shape[1] // LANES)]
+    return functools.reduce(lambda a, b: a + b, pieces)
+
+
+def fold_rows(tall):
+    return jnp.sum(tall.reshape(-1, 8, tall.shape[1]), axis=0)
+
+
+def repeat_out(out_ref, block):
+    out_ref[...] = jnp.broadcast_to(block[None], out_ref.shape)
+
+
+def first_kernel(z_ref, v_ref, exp_ref, out_ref, acc):
+    step = pl.program_id(0)
+
+    @pl.when(step == 0)
+    def _():
+        acc[...] = jnp.zeros_like(acc)
+
+    width = v_ref.shape[1]
+    for start in range(0, width, CHUNK):
+        cols = slice(start, start + CHUNK)
+        product = jnp.dot(z_ref[...], v_ref[:, cols], preferred_element_type=jnp.float32)
+        block = jnp.exp(product * (1.0 / TAU_T))
+        exp_ref[:, cols] = block
+        acc[:, cols] += fold_rows(block)
+
+    @pl.when(step == pl.num_programs(0) - 1)
+    def _():
+        repeat_out(out_ref, lane_rows(jnp.sum(acc[...], axis=0, keepdims=True)))
+
+
+def row_kernel(parts_ref, exp_ref, out_ref, scale, acc):
+    step = pl.program_id(0)
+
+    @pl.when(step == 0)
+    def _():
+        scale[...] = one_row(1.0 / jnp.sum(parts_ref[...], axis=0))
+
+    rows, width = exp_ref.shape
+    block = exp_ref[:, 0:LANES] * scale[:, 0:LANES]
+    for start in range(LANES, width, LANES):
+        cols = slice(start, start + LANES)
+        block += exp_ref[:, cols] * scale[:, cols]
+    acc[pl.ds(pl.multiple_of(step * rows, rows), rows), :] = block
+
+    @pl.when(step == pl.num_programs(0) - 1)
+    def _():
+        repeat_out(out_ref, lane_sums(acc[...]))
+
+
+def column_kernel(parts_ref, exp_ref, out_ref, scale, acc):
+    step = pl.program_id(0)
+
+    @pl.when(step == 0)
+    def _():
+        scale[...] = down(1.0 / jnp.sum(parts_ref[...], axis=0))
+        acc[...] = jnp.zeros_like(acc)
+
+    rows, width = exp_ref.shape
+    factor = scale[pl.ds(pl.multiple_of(step * rows, rows), rows), :]
+    for start in range(0, width, LANES):
+        cols = slice(start, start + LANES)
+        acc[:, cols] += fold_rows(exp_ref[:, cols] * factor)
+
+    @pl.when(step == pl.num_programs(0) - 1)
+    def _():
+        repeat_out(out_ref, lane_rows(jnp.sum(acc[...], axis=0, keepdims=True)))
+
+
+def student_kernel(parts_ref, exp_ref, z_ref, v_ref, out_ref, scale, acc):
+    step = pl.program_id(0)
+
+    @pl.when(step == 0)
+    def _():
+        scale[...] = one_row(1.0 / jnp.sum(parts_ref[...], axis=0))
+
+    rows, width = exp_ref.shape
+    here = pl.ds(pl.multiple_of(step * rows, rows), rows)
+    mass = jnp.zeros((rows, LANES), jnp.float32)
+    exps = jnp.zeros((rows, LANES), jnp.float32)
+    cross = jnp.zeros((rows, LANES), jnp.float32)
+    for start in range(0, width, CHUNK):
+        cols = slice(start, start + CHUNK)
+        scores = jnp.dot(z_ref[...], v_ref[:, cols], preferred_element_type=jnp.float32)
+        weighted = exp_ref[:, cols] * scale[:, cols]
+        mass += fold_lanes(weighted)
+        exps += fold_lanes(jnp.exp(scores * (1.0 / TAU_S)))
+        cross += fold_lanes(weighted * scores)
+    acc[0, here, :] = mass
+    acc[1, here, :] = exps
+    acc[2, here, :] = cross
+
+    @pl.when(step == pl.num_programs(0) - 1)
+    def _():
+        sums = [lane_sums(acc[i]) for i in range(3)]
+        repeat_out(out_ref, jnp.concatenate(sums, axis=0))
+
+
+def gradient_kernel(
+    row_parts_ref, col_parts_ref, exp_ref, z_ref, zt_ref, v_ref, dz_ref, dp_ref,
+    scale, teacher, student, grad,
+):
+    step = pl.program_id(0)
+    rows, width = exp_ref.shape
+    tall = rows // LANES
+
+    @pl.when(step == 0)
+    def _():
+        sums = jnp.sum(row_parts_ref[...], axis=0)
+        factor = GRAD_SCALE / TAU_S
+        teacher[...] = down(factor / sums[0:tall])
+        student[...] = down(factor / sums[tall : 2 * tall])
+        scale[...] = 1.0 / jnp.sum(col_parts_ref[...], axis=0)
+        dz_ref[...] = jnp.zeros_like(dz_ref)
+
+    groups = width // LANES
+    col = one_row(scale[pl.ds(pl.multiple_of(step * groups, groups), groups), :])
+    for start in range(0, rows, ROWS_BLOCK):
+        here = slice(start, start + ROWS_BLOCK)
+        scores = jnp.dot(z_ref[here, :], v_ref[...], preferred_element_type=jnp.float32)
+        prob = jnp.exp(scores * (1.0 / TAU_S))
+        for piece in range(0, width, LANES):
+            cols = slice(piece, piece + LANES)
+            target = exp_ref[here, cols] * col[:, cols] * teacher[here, :]
+            grad[here, cols] = (prob[:, cols] * student[here, :] - target).astype(jnp.bfloat16)
+        dz_ref[here, :] += lax.dot_general(
+            grad[here, :], v_ref[...], COL_DIMS, preferred_element_type=jnp.float32
+        )
+    dp_ref[...] = jnp.dot(zt_ref[...], grad[...], preferred_element_type=jnp.float32)
+
+
+def params():
+    return pltpu.CompilerParams(
+        dimension_semantics=("arbitrary",), vmem_limit_bytes=VMEM_LIMIT
+    )
+
+
+def cost(flops, size, exps=0):
+    return pl.CostEstimate(flops=flops, bytes_accessed=size, transcendentals=exps)
+
+
+def whole(shape):
+    return pl.BlockSpec(shape, lambda i: (0,) * len(shape))
+
+
+def f32(*shape):
+    return jax.ShapeDtypeStruct(shape, jnp.float32)
+
+
+def first_pass(z, v, copies):
+    rows, width = z.shape[0], v.shape[1]
+    spread_shape = (copies, width // LANES, LANES)
+    return pl.pallas_call(
+        first_kernel,
+        grid=(rows // ROWS_BLOCK,),
+        in_specs=[pl.BlockSpec((ROWS_BLOCK, z.shape[1]), lambda i: (i, 0)), whole(v.shape)],
+        out_specs=[pl.BlockSpec((ROWS_BLOCK, width), lambda i: (i, 0)), whole(spread_shape)],
+        out_shape=[f32(rows, width), f32(*spread_shape)],
+        scratch_shapes=[pltpu.VMEM((8, width), jnp.float32)],
+        compiler_params=params(),
+        cost_estimate=cost(2 * z.size * width, rows * width * 4, rows * width),
+    )(z, v)
+
+
+def row_pass(parts, exp, copies):
+    rows, width = exp.shape
+    out = (copies, rows // LANES, LANES)
+    return pl.pallas_call(
+        row_kernel,
+        grid=(rows // ROWS_BLOCK,),
+        in_specs=[whole(parts.shape), pl.BlockSpec((ROWS_BLOCK, width), lambda i: (i, 0))],
+        out_specs=whole(out),
+        out_shape=f32(*out),
+        scratch_shapes=[pltpu.VMEM((1, width), jnp.float32), pltpu.VMEM((rows, LANES), jnp.float32)],
+        compiler_params=params(),
+        cost_estimate=cost(2 * exp.size, exp.size * 4),
+    )(parts, exp)
+
+
+def column_pass(parts, exp, copies):
+    rows, width = exp.shape
+    out = (copies, width // LANES, LANES)
+    return pl.pallas_call(
+        column_kernel,
+        grid=(rows // ROWS_BLOCK,),
+        in_specs=[whole(parts.shape), pl.BlockSpec((ROWS_BLOCK, width), lambda i: (i, 0))],
+        out_specs=whole(out),
+        out_shape=f32(*out),
+        scratch_shapes=[pltpu.VMEM((rows, LANES), jnp.float32), pltpu.VMEM((8, width), jnp.float32)],
+        compiler_params=params(),
+        cost_estimate=cost(2 * exp.size, exp.size * 4),
+    )(parts, exp)
+
+
+def student_pass(parts, exp, z, v, copies):
+    rows, width = exp.shape
+    out = (copies, 3 * rows // LANES, LANES)
+    return pl.pallas_call(
+        student_kernel,
+        grid=(rows // ROWS_BLOCK,),
+        in_specs=[
+            whole(parts.shape),
+            pl.BlockSpec((ROWS_BLOCK, width), lambda i: (i, 0)),
+            pl.BlockSpec((ROWS_BLOCK, z.shape[1]), lambda i: (i, 0)),
+            whole(v.shape),
+        ],
+        out_specs=whole(out),
+        out_shape=f32(*out),
+        scratch_shapes=[
+            pltpu.VMEM((1, width), jnp.float32),
+            pltpu.VMEM((3, rows, LANES), jnp.float32),
+        ],
+        compiler_params=params(),
+        cost_estimate=cost(2 * z.size * width, exp.size * 4, exp.size),
+    )(parts, exp, z, v)
+
+
+def gradient_pass(row_parts, col_parts, exp, z, zt, v):
+    rows, width = exp.shape
+    bot = z.shape[1]
+    return pl.pallas_call(
+        gradient_kernel,
+        grid=(width // CHUNK,),
+        in_specs=[
+            whole(row_parts.shape),
+            whole(col_parts.shape),
+            pl.BlockSpec((rows, CHUNK), lambda i: (0, i)),
+            whole(z.shape),
+            whole(zt.shape),
+            pl.BlockSpec((bot, CHUNK), lambda i: (0, i)),
+        ],
+        out_specs=[whole((rows, bot)), pl.BlockSpec((bot, CHUNK), lambda i: (0, i))],
+        out_shape=[f32(rows, bot), f32(bot, width)],
+        scratch_shapes=[
+            pltpu.VMEM((width // LANES, LANES), jnp.float32),
+            pltpu.VMEM((rows, LANES), jnp.float32),
+            pltpu.VMEM((rows, LANES), jnp.float32),
+            pltpu.VMEM((rows, CHUNK), jnp.bfloat16),
+        ],
+        compiler_params=params(),
+        cost_estimate=cost(6 * z.size * width, exp.size * 4, exp.size),
+    )(row_parts, col_parts, exp, z, zt, v)
 
 
 def norm_backward(dzhat, unit_s, norm_s):
@@ -88,42 +375,17 @@
     z_s = unit_rows(wide_s)[0].astype(jnp.bfloat16)
     hid_group = lax.all_gather(hid_student, SHARD, axis=0, tiled=True)
 
-    teacher_exp = jnp.exp(jnp.dot(z_t, v_t, preferred_element_type=jnp.float32) / TAU_T)
-    row_scale = jnp.ones((teacher_exp.shape[0],), jnp.float32)
-    col_scale = 1.0 / total(jnp.sum(row_scale[:, None] * teacher_exp, axis=0), "z")
+    columns, planes = lax.axis_size("z"), lax.axis_size(PLANE)
+    teacher_exp, mass = first_pass(z_t, v_t, columns)
+    col_parts = exchange(mass, "z")
     for step in range(ITERS - 1):
-        row_scale = 1.0 / total(jnp.sum(teacher_exp * col_scale[None, :], axis=1), PLANE)
-        col_scale = 1.0 / total(jnp.sum(row_scale[:, None] * teacher_exp, axis=0), "z")
-    scores = jnp.dot(z_s, v_s, preferred_element_type=jnp.float32)
-    student_exp = jnp.exp(scores / TAU_S)
-    weighted = teacher_exp * col_scale[None, :]
-    sums = total(
-        jnp.stack(
-            [
-                jnp.sum(weighted, axis=1),
-                jnp.sum(student_exp, axis=1),
-                jnp.sum(weighted * scores, axis=1),
-            ]
-        ),
-        PLANE,
-    )
-    row_scale, expsum, cross = 1.0 / sums[0], sums[1], sums[2]
-    row_scale, expsum, cross = lax.optimization_barrier((row_scale, expsum, cross))
-    row_loss = jnp.sum(jnp.log(expsum) - row_scale * cross / TAU_S)
-    target = weighted * row_scale[:, None]
-    prob = student_exp / expsum[:, None]
-    grad_logits = (GRAD_SCALE / TAU_S * (prob - target)).astype(jnp.bfloat16)
-
-    dzhat_part = lax.dot_general(
-        grad_logits, v_s, COL_DIMS, preferred_element_type=jnp.float32
-    )
-    grad_logits, dzhat_part = lax.optimization_barrier((grad_logits, dzhat_part))
-    dproto = lax.psum_scatter(
-        lax.dot_general(z_s, grad_logits, ROW_DIMS, preferred_element_type=jnp.float32),
-        "z",
-        scatter_dimension=0,
-        tiled=True,
-    )
+        row_parts = exchange(row_pass(col_parts, teacher_exp, planes), PLANE)
+        col_parts = exchange(column_pass(row_parts, teacher_exp, columns), "z")
+    sums = exchange(student_pass(col_parts, teacher_exp, z_s, v_s, planes), PLANE)
+    dzhat_part, dproto_part = gradient_pass(sums, col_parts, teacher_exp, z_s, z_s.T, v_s)
+    row_mass, expsum, cross = jnp.split(jnp.sum(sums, axis=0), 3, axis=0)
+    row_loss = jnp.sum(jnp.log(expsum) - cross / row_mass / TAU_S)
+    dproto = lax.psum_scatter(dproto_part, "z", scatter_dimension=0, tiled=True)
     dzhat = scatter_sum(dzhat_part, PLANE)
     dy = norm_backward(dzhat, unit_s, norm_s)
     dy_group = spread(dy, SHARD).reshape(-1, bot)

time: 308 us -> 282 us (0.916)
  blocking collectives: 49.5 us -> 101 us
  matrix products: 31.9 us -> 4.12 us
  other arithmetic: 45.3 us -> 18.4 us
  waiting for transfers between devices: 87.5 us -> 62 us
  Pallas kernels: 0 us -> 24.9 us
  starting transfers between devices: 54.5 us -> 31.8 us
    all_to_all x0 -> x6, blocking collectives: none -> 71.3 us  [the longest x4 50.1 us: exchange(): return lax.all_to_all(blocks, axes, 0, 0, tiled=True)]
    dot_general x4 -> x0, matrix products: 25.3 us -> none  [the longest x1 10.9 us: local(): scores = jnp.dot(z_s, v_s, preferred_element_type=jnp.float32)]
    pallas_call x0 -> x7, Pallas kernels: none -> 24.9 us  [the longest x1 11.1 us: gradient_pass(): pl.pallas_call(gradient_kernel, grid=(width // CHUNK,), in_specs=[whole(r...]
    all_to_all x6 -> x2, waiting for transfers between devices: 41.6 us -> 18 us  [spread(): lax.all_to_all(jnp.broadcast_to(block[None], (count,) + block.shape), axe...]
    all_to_all x6 -> x2, starting transfers between devices: 30.9 us -> 9.03 us  [spread(): lax.all_to_all(jnp.broadcast_to(block[None], (count,) + block.shape), axe...]
    all_to_all x4 -> x2, blocking collectives: 49.5 us -> 29.8 us  [spread(): lax.all_to_all(jnp.broadcast_to(block[None], (count,) + block.shape), axe...]
    reduce_sum x11 -> x2, other arithmetic: 18.1 us -> 0.65 us  [the longest x1 0.61 us: local(): row_loss = jnp.sum(jnp.log(expsum) - cross / row_mass / TAU_S)]
    unnamed x32 -> x28, local copies, waits for them, and re-layouts: 1.9 us -> 12.3 us
  transfers between devices with their start and end apart: 15 -> 11, of which waited for: 11 -> 6; matrix products, arithmetic and copies ran while one was open for 25% -> 9% of each run, Pallas kernels for 0% -> 9%
where the time goes in v3:
time: 282 us; the launch traced here: 281 us
  blocking collectives  101 us (36%)
  waiting for transfers between devices  62 us (22%)
  starting transfers between devices  31.8 us (11%)
  Pallas kernels  24.9 us (9%)
  local copies, waits for them, and re-layouts  22.6 us (8%)
  other arithmetic  18.4 us (7%)
  between operations  15.9 us (6%)
  matrix products  4.12 us (1%)
    all_to_all x4, blocking collectives, exchange(): return lax.all_to_all(blocks, axes, 0, 0, tiled=True)  50.1 us
    all_to_all x2, waiting for transfers between devices, scatter_sum(): return jnp.sum(lax.all_to_all(blocks, axes, 0, 0, tiled=True), axis=0)  33.3 us
    all_to_all x2, blocking collectives, spread(): lax.all_to_all(jnp.broadcast_to(block[None], (count,) + block.shape), axe...  29.8 us
    all_to_all x2, waiting for transfers between devices, spread(): lax.all_to_all(jnp.broadcast_to(block[None], (count,) + block.shape), axe...  18 us
    unnamed x28, local copies, waits for them, and re-layouts  12.3 us
    all_to_all x1, blocking collectives, scatter_sum(): return jnp.sum(lax.all_to_all(blocks, axes, 0, 0, tiled=True), axis=0)  12.1 us
    pallas_call x1, Pallas kernels, gradient_pass(): pl.pallas_call(gradient_kernel, grid=(width // CHUNK,), in_specs=[whole(r...  11.1 us
    all_to_all x2, starting transfers between devices, scatter_sum(): return jnp.sum(lax.all_to_all(blocks, axes, 0, 0, tiled=True), axis=0)  10.9 us
  transfers between devices with their start and end apart: 11, of which 6 were waited for; matrix products, arithmetic and copies ran while one was open for 9% of the time, Pallas kernels for 9%

profile of v3, /device:TPU:2, one launch (start us, length us, event | category | flops | bytes accessed | tf_op | source)
XLA Modules:
  0.0 280.8 jit_solution(2254801618713180760)
XLA Ops:
  9.1 9.2 %all_to_all.70 = bf16[4,32,512]{2,1,0:T(8,128)(2,1)S(1)} all-to-all(bf16[4,32,512]{2,1,0:T(8,128)(2,1)S(1)} %reshape.92), channel_id=1, replica_groups=mesh['z'=8,'yh'=2,'yl'=2,'x'=4,'c'=2] {'x'}, dimensions={0} | all-to-all | bytes 262144 | tf_op jit(solution)/shard_map/all_to_all | solution.py:61
  19.2 10.1 %all_to_all.71 = bf16[4,128,384]{2,1,0:T(8,128)(2,1)S(1)} all-to-all(bf16[4,128,384]{2,1,0:T(8,128)(2,1)S(1)} %broadcast_in_dim.10), channel_id=1, replica_groups=mesh['z'=8,'yh'=2,'yl'=2,'x'=4,'c'=2] {'yl','c'}, dimensions={0} | all-to-all | bytes 786432 | tf_op jit(solution)/shard_map/all_to_all | solution.py:44
  29.5 12.1 %all_to_all.72 = f32[4,32,384]{2,1,0:T(8,128)S(1)} all-to-all(f32[4,32,384]{2,1,0:T(8,128)S(1)} %fusion.12), channel_id=1, replica_groups=mesh['z'=8,'yh'=2,'yl'=2,'x'=4,'c'=2] {'x'}, dimensions={0} | all-to-all | bytes 393216 | tf_op jit(solution)/shard_map/all_to_all | solution.py:53
  41.8 19.8 %all_to_all.73 = bf16[32,32,384]{2,1,0:T(8,128)(2,1)S(1)} all-to-all(bf16[32,32,384]{2,1,0:T(8,128)(2,1)S(1)} %broadcast_in_dim.11), channel_id=1, replica_groups=mesh['z'=8,'yh'=2,'yl'=2,'x'=4,'c'=2] {'yh','yl','x','c'}, dimensions={0} | all-to-all | bytes 1572864 | tf_op jit(solution)/shard_map/all_to_all | solution.py:44
  61.6 3.0 %multiply_reduce_fusion.3 = (f32[32]{0:T(128)}, f32[32,384]{1,0:T(8,128)}) fusion(bf16[32,2048]{1,0:T(8,128)(2,1)S(1)} %copy-done.11, bf16[2048,384]{1,0:T(8,128)(2,1)} %all-gather.6.cloned.1.call-done), kind=kOutput, calls=%fused_computation.21 | convolution fusion | flops 50356192 | bytes 1753216 | tf_op jit(solution)/shard_map/dot_general | solution.py:372
  65.4 1.9 fusion.2
  67.3 2.6 fusion
  74.3 3.0 %shard_map.85 = (f32[1024,2048]{1,0:T(8,128)S(1)}, f32[8,16,128]{2,1,0:T(8,128)S(1)}) custom-call(bf16[1024,384]{1,0:T(8,128)(2,1)S(1)} %bitcast.30, bf16[384,2048]{1,0:T(8,128)(2,1)S(1)} %fusion.3.v_ref), custom_call_target="tpu_custom_call" | custom-call | flops 1610612736 | bytes 8388608 | tf_op jit(solution)/shard_map/pallas_call | solution.py:261
  77.3 16.4 %all_to_all.74.parts_ref = f32[8,16,128]{2,1,0:T(8,128)S(1)} all-to-all(f32[8,16,128]{2,1,0:T(8,128)S(1)} %get-tuple-element.13), channel_id=1, replica_groups=mesh['z'=8,'yh'=2,'yl'=2,'x'=4,'c'=2] {'z'}, dimensions={0} | all-to-all | bytes 131072 | tf_op jit(solution)/shard_map/all_to_all | solution.py:39
  94.8 11.7 %all_to_all.75.parts_ref = f32[32,8,128]{2,1,0:T(8,128)S(1)} all-to-all(f32[32,8,128]{2,1,0:T(8,128)S(1)} %shard_map.86), channel_id=1, replica_groups=mesh['z'=8,'yh'=2,'yl'=2,'x'=4,'c'=2] {'yh','yl','x','c'}, dimensions={0} | all-to-all | bytes 262144 | tf_op jit(solution)/shard_map/all_to_all | solution.py:39
  107.5 10.8 %all_to_all.76.parts_ref = f32[8,16,128]{2,1,0:T(8,128)S(1)} all-to-all(f32[8,16,128]{2,1,0:T(8,128)S(1)} %shard_map.87), channel_id=1, replica_groups=mesh['z'=8,'yh'=2,'yl'=2,'x'=4,'c'=2] {'z'}, dimensions={0} | all-to-all | bytes 131072 | tf_op jit(solution)/shard_map/all_to_all | solution.py:39
  119.4 11.3 %all_to_all.77.parts_ref = f32[32,8,128]{2,1,0:T(8,128)S(1)} all-to-all(f32[32,8,128]{2,1,0:T(8,128)S(1)} %shard_map.88), channel_id=1, replica_groups=mesh['z'=8,'yh'=2,'yl'=2,'x'=4,'c'=2] {'yh','yl','x','c'}, dimensions={0} | all-to-all | bytes 262144 | tf_op jit(solution)/shard_map/all_to_all | solution.py:39
  132.3 3.4 %all-to-all-start.8 = ((f32[8,16,128]{2,1,0:T(8,128)}), f32[8,16,128]{2,1,0:T(8,128)S(1)}, u32[]{:S(2)}, u32[]{:S(2)}) async-start(f32[8,16,128]{2,1,0:T(8,128)} %shard_map.89), calls=%async_computation.8 | async-start | bytes 131072 | tf_op jit(solution)/shard_map/all_to_all | solution.py:39
  135.7 1.9 copy.22
  137.6 2.2 multiply_reduce_fusion
  142.4 1.9 all-to-all-done.8.parts_ref.col_parts_ref
  144.3 3.5 %copy-done.1 = f32[1024,2048]{1,0:T(8,128)S(1)} copy-done((f32[1024,2048]{1,0:T(8,128)S(1)}, f32[1024,2048]{1,0:T(8,128)}, u32[]{:S(2)}) %copy-start.1) | copy-done | bytes 8388632
  147.7 5.9 %shard_map.90 = f32[32,24,128]{2,1,0:T(8,128)} custom-call(f32[8,16,128]{2,1,0:T(8,128)S(1)} %all-to-all-done.8.parts_ref.col_parts_ref, f32[1024,2048]{1,0:T(8,128)S(1)} %copy-done.1, bf16[1024,384]{1,0:T(8,128)(2,1)S(1)} %copy.23.z_ref, bf16[384,2048]{1,0:T(8,128)(2,1)S(1)} %constant_dynamic-slice_fusion.2.v_ref), custom_call_target="tpu_custom_call" | custom-call | flops 1610612736 | bytes 8388608 | tf_op jit(solution)/shard_map/pallas_call | solution.py:306
  153.7 4.7 %all-to-all-start.9 = ((f32[32,24,128]{2,1,0:T(8,128)}), f32[32,24,128]{2,1,0:T(8,128)S(1)}, u32[]{:S(2)}, u32[]{:S(2)}) async-start(f32[32,24,128]{2,1,0:T(8,128)} %shard_map.90), calls=%async_computation.9 | async-start | bytes 786432 | tf_op jit(solution)/shard_map/all_to_all | solution.py:39
  160.2 7.3 %all-to-all-done.9.row_parts_ref = f32[32,24,128]{2,1,0:T(8,128)S(1)} async-done(((f32[32,24,128]{2,1,0:T(8,128)}), f32[32,24,128]{2,1,0:T(8,128)S(1)}, u32[]{:S(2)}, u32[]{:S(2)}) %all-to-all-start.9) | async-done | bytes 393248 | tf_op jit(solution)/shard_map/all_to_all | solution.py:39
  167.6 3.4 %copy-done.2 = f32[1024,2048]{1,0:T(8,128)S(1)} copy-done((f32[1024,2048]{1,0:T(8,128)S(1)}, f32[1024,2048]{1,0:T(8,128)}, u32[]{:S(2)}) %copy-start.2) | copy-done | bytes 8388632
  171.8 11.1 %shard_map.91 = (f32[1024,384]{1,0:T(8,128)}, f32[384,2048]{1,0:T(8,128)S(1)}) custom-call(f32[32,24,128]{2,1,0:T(8,128)S(1)} %all-to-all-done.9.row_parts_ref, f32[8,16,128]{2,1,0:T(8,128)S(1)} %copy-done.5, f32[1024,2048]{1,0:T(8,128)S(1)} %copy-done.2, bf16[1024,384]{1,0:T(8,128)(2,1)S(1)} %copy.23.z_ref, bf16[384,1024]{1,0:T(8,128)(2,1)S(1)} %fusion.18.zt_ref, ...), custom_call_target="tpu_custom_call" | custom-call | flops 4831838208 | bytes 8388608 | tf_op jit(solution)/shard_map/pallas_call | solution.py:329
  184.5 5.1 %all-to-all-start.10 = ((f32[32,32,384]{2,1,0:T(8,128)}), f32[32,32,384]{2,1,0:T(8,128)S(1)}, u32[]{:S(2)}, u32[]{:S(2)}) async-start(f32[32,32,384]{2,1,0:T(8,128)} %bitcast.8), calls=%async_computation.10 | async-start | bytes 3145728 | tf_op jit(solution)/shard_map/all_to_all | solution.py:53
  190.8 21.0 %all-to-all-done.10 = f32[32,32,384]{2,1,0:T(8,128)S(1)} async-done(((f32[32,32,384]{2,1,0:T(8,128)}), f32[32,32,384]{2,1,0:T(8,128)S(1)}, u32[]{:S(2)}, u32[]{:S(2)}) %all-to-all-start.10) | async-done | bytes 1572896 | tf_op jit(solution)/shard_map/all_to_all | solution.py:53
  215.2 5.5 %all-to-all-start.11 = ((bf16[16,32,384]{2,1,0:T(8,128)(2,1)}), bf16[16,32,384]{2,1,0:T(8,128)(2,1)S(1)}, u32[]{:S(2)}, u32[]{:S(2)}) async-start(bf16[16,32,384]{2,1,0:T(8,128)(2,1)} %broadcast_in_dim.12), calls=%async_computation.11 | async-start | bytes 786432 | tf_op jit(solution)/shard_map/all_to_all | solution.py:44
  221.8 5.4 %all-to-all-done.11 = bf16[16,32,384]{2,1,0:T(8,128)(2,1)S(1)} async-done(((bf16[16,32,384]{2,1,0:T(8,128)(2,1)}), bf16[16,32,384]{2,1,0:T(8,128)(2,1)S(1)}, u32[]{:S(2)}, u32[]{:S(2)}) %all-to-all-start.11) | async-done | bytes 393248 | tf_op jit(solution)/shard_map/all_to_all | solution.py:44
  228.1 5.8 %all-to-all-start.12 = ((f32[16,8,384]{2,1,0:T(8,128)}), f32[16,8,384]{2,1,0:T(8,128)S(1)}, u32[]{:S(2)}, u32[]{:S(2)}) async-start(f32[16,8,384]{2,1,0:T(8,128)} %fusion.6), calls=%async_computation.12 | async-start | bytes 393216 | tf_op jit(solution)/shard_map/all_to_all | solution.py:53
  235.3 12.3 %all-to-all-done.12 = f32[16,8,384]{2,1,0:T(8,128)S(1)} async-done(((f32[16,8,384]{2,1,0:T(8,128)}), f32[16,8,384]{2,1,0:T(8,128)S(1)}, u32[]{:S(2)}, u32[]{:S(2)}) %all-to-all-start.12) | async-done | bytes 196640 | tf_op jit(solution)/shard_map/all_to_all | solution.py:53
  249.7 3.6 %all-to-all-start.13 = ((f32[16,48,128]{2,1,0:T(8,128)}), f32[16,48,128]{2,1,0:T(8,128)S(1)}, u32[]{:S(2)}, u32[]{:S(2)}) async-start(f32[16,48,128]{2,1,0:T(8,128)} %broadcast_in_dim.14), calls=%async_computation.14 | async-start | bytes 786432 | tf_op jit(solution)/shard_map/all_to_all | solution.py:44
  253.3 3.4 %collective-permute-start = (f32[24,2048]{1,0:T(8,128)S(1)}, f32[24,2048]{1,0:T(8,128)S(1)}, u32[]{:S(2)}, u32[]{:S(2)}) collective-permute-start(f32[24,2048]{1,0:T(8,128)S(1)} %get-tuple-element.20), channel_id=1, source_target_pairs={{0,16},{16,0},{1,17},{17,1},{2,18},{18,2},{3,19},{19,3},{4,20},{20... | collective-permute-start | bytes 589832 | tf_op jit(solution)/shard_map/ppermute | solution.py:71
  256.7 12.6 %all-to-all-done.13 = f32[16,48,128]{2,1,0:T(8,128)S(1)} async-done(((f32[16,48,128]{2,1,0:T(8,128)}), f32[16,48,128]{2,1,0:T(8,128)S(1)}, u32[]{:S(2)}, u32[]{:S(2)}) %all-to-all-start.13) | async-done | bytes 393248 | tf_op jit(solution)/shard_map/all_to_all | solution.py:44
  271.4 1.8 fusion.5
  (85 shorter events, 31.6 us)
Async XLA Ops:
  7.2 54.4 %all-gather.6.cloned.1.call-start = ((), (), s32[]{:S(2)}) async-start(), calls=%async_computation.16 | async-start | bytes 1671168 | tf_op jit(solution)/shard_map/all_gather | solution.py:370
  7.9 127.8 %all-gather.8.cloned.1.call-start = ((), (), s32[]{:S(2)}) async-start(), calls=%async_computation.17 | async-start | bytes 1622016 | tf_op jit(solution)/shard_map/all_gather | solution.py:374
  29.2 32.4 %copy-start.11 = (bf16[32,2048]{1,0:T(8,128)(2,1)S(1)}, bf16[32,2048]{1,0:T(8,128)(2,1)}, u32[]{:S(2)}) copy-start(bf16[32,2048]{1,0:T(8,128)(2,1)} %param.7) | copy-start | bytes 393220
  64.6 156.1 %all-gather.4.cloned.1.call-start = ((), (), s32[]{:S(2)}) async-start(), calls=%async_computation.15 | async-start | bytes 2228224 | tf_op jit(solution)/shard_map/all_gather | solution.py:376
  65.4 4.5 %copy-start.7 = (bf16[384,4096]{1,0:T(8,128)(2,1)S(1)}, bf16[384,4096]{1,0:T(8,128)(2,1)}, u32[]{:S(2)}) copy-start(bf16[384,4096]{1,0:T(8,128)(2,1)} %param.11) | copy-start | bytes 9437188
  70.8 1.8 copy-start.8
  70.8 3.0 %copy-start.9 = (bf16[384,4096]{1,0:T(8,128)(2,1)S(1)}, bf16[384,4096]{1,0:T(8,128)(2,1)}, u32[]{:S(2)}) copy-start(bf16[384,4096]{1,0:T(8,128)(2,1)} %param.10) | copy-start | bytes 9437188
  77.2 53.4 %copy-start = (f32[1024,2048]{1,0:T(8,128)}, f32[1024,2048]{1,0:T(8,128)S(1)}, u32[]{:S(2)}) copy-start(f32[1024,2048]{1,0:T(8,128)S(1)} %get-tuple-element.14.exp_ref) | copy-start | bytes 25165828
  132.3 12.0 %all-to-all-start.8 = ((f32[8,16,128]{2,1,0:T(8,128)}), f32[8,16,128]{2,1,0:T(8,128)S(1)}, u32[]{:S(2)}, u32[]{:S(2)}) async-start(f32[8,16,128]{2,1,0:T(8,128)} %shard_map.89), calls=%async_computation.8 | async-start | bytes 131072 | tf_op jit(solution)/shard_map/all_to_all | solution.py:39
  137.6 2.2 copy-start.6
  139.8 13.8 %copy-start.12 = (f32[1024]{0:T(1024)}, f32[1024]{0:T(1024)S(1)}, u32[]{:S(2)}) copy-start(f32[1024]{0:T(1024)S(1)} %add_sqrt_fusion.2) | copy-start | bytes 12292
  144.3 3.5 %copy-start.1 = (f32[1024,2048]{1,0:T(8,128)S(1)}, f32[1024,2048]{1,0:T(8,128)}, u32[]{:S(2)}) copy-start(f32[1024,2048]{1,0:T(8,128)} %copy-done) | copy-start | bytes 25165828
  147.7 5.9 %copy-start.4 = (f32[8,16,128]{2,1,0:T(8,128)}, f32[8,16,128]{2,1,0:T(8,128)S(1)}, u32[]{:S(2)}) copy-start(f32[8,16,128]{2,1,0:T(8,128)S(1)} %all-to-all-done.8.parts_ref.col_parts_ref) | copy-start | bytes 196612
  153.7 13.9 %all-to-all-start.9 = ((f32[32,24,128]{2,1,0:T(8,128)}), f32[32,24,128]{2,1,0:T(8,128)S(1)}, u32[]{:S(2)}, u32[]{:S(2)}) async-start(f32[32,24,128]{2,1,0:T(8,128)} %shard_map.90), calls=%async_computation.9 | async-start | bytes 786432 | tf_op jit(solution)/shard_map/all_to_all | solution.py:39
  158.4 89.3 %reduce-scatter.2.cloned.1.call-start = ((), (), s32[]{:S(2)}) async-start(), calls=%async_computation.18 | async-start | bytes 3538944 | tf_op jit(solution)/shard_map/reduce_scatter | solution.py:388
  167.6 3.4 %copy-start.2 = (f32[1024,2048]{1,0:T(8,128)S(1)}, f32[1024,2048]{1,0:T(8,128)}, u32[]{:S(2)}) copy-start(f32[1024,2048]{1,0:T(8,128)} %copy-done) | copy-start | bytes 25165828
  170.9 0.8 copy-start.5
  182.9 1.7 copy-start.3
  184.5 27.2 %all-to-all-start.10 = ((f32[32,32,384]{2,1,0:T(8,128)}), f32[32,32,384]{2,1,0:T(8,128)S(1)}, u32[]{:S(2)}, u32[]{:S(2)}) async-start(f32[32,32,384]{2,1,0:T(8,128)} %bitcast.8), calls=%async_computation.10 | async-start | bytes 3145728 | tf_op jit(solution)/shard_map/all_to_all | solution.py:53
  215.2 12.0 %all-to-all-start.11 = ((bf16[16,32,384]{2,1,0:T(8,128)(2,1)}), bf16[16,32,384]{2,1,0:T(8,128)(2,1)S(1)}, u32[]{:S(2)}, u32[]{:S(2)}) async-start(bf16[16,32,384]{2,1,0:T(8,128)(2,1)} %broadcast_in_dim.12), calls=%async_computation.11 | async-start | bytes 786432 | tf_op jit(solution)/shard_map/all_to_all | solution.py:44
  228.1 19.5 %all-to-all-start.12 = ((f32[16,8,384]{2,1,0:T(8,128)}), f32[16,8,384]{2,1,0:T(8,128)S(1)}, u32[]{:S(2)}, u32[]{:S(2)}) async-start(f32[16,8,384]{2,1,0:T(8,128)} %fusion.6), calls=%async_computation.12 | async-start | bytes 393216 | tf_op jit(solution)/shard_map/all_to_all | solution.py:53
  247.7 5.6 %copy-start.10 = (f32[48,2048]{1,0:T(8,128)S(1)}, f32[48,2048]{1,0:T(8,128)}, u32[]{:S(2)}) copy-start(f32[48,2048]{1,0:T(8,128)} %reduce-scatter.2.cloned.1.call-done) | copy-start | bytes 1179652
  249.7 19.6 %all-to-all-start.13 = ((f32[16,48,128]{2,1,0:T(8,128)}), f32[16,48,128]{2,1,0:T(8,128)S(1)}, u32[]{:S(2)}, u32[]{:S(2)}) async-start(f32[16,48,128]{2,1,0:T(8,128)} %broadcast_in_dim.14), calls=%async_computation.14 | async-start | bytes 786432 | tf_op jit(solution)/shard_map/all_to_all | solution.py:44
  253.3 18.1 %collective-permute-start = (f32[24,2048]{1,0:T(8,128)S(1)}, f32[24,2048]{1,0:T(8,128)S(1)}, u32[]{:S(2)}, u32[]{:S(2)}) collective-permute-start(f32[24,2048]{1,0:T(8,128)S(1)} %get-tuple-element.20), channel_id=1, source_target_pairs={{0,16},{16,0},{1,17},{17,1},{2,18},{18,2},{3,19},{19,3},{4,20},{20... | collective-permute-start | bytes 589832 | tf_op jit(solution)/shard_map/ppermute | solution.py:71
Sparse Core Ops, SparseCore 0:
  9.8 39.7 all-gather.5
  64.8 48.9 all-gather.7
  115.6 34.8 all-gather.3
  184.7 43.9 reduce-scatter.1

commit v4 on v3

--- a/solution.py
+++ b/solution.py
@@ -15,7 +15,7 @@
 LANES = 128
 ROWS_BLOCK = 256
 CHUNK = 512
-VMEM_LIMIT = 32 * 1024 * 1024
+MIB = 1024 * 1024
 ROW_DIMS = (((0,), (0,)), ((), ()))
 COL_DIMS = (((1,), (1,)), ((), ()))
 
@@ -27,12 +27,6 @@
 def unit_rows(proj_out):
     norm = jnp.sqrt(jnp.sum(proj_out * proj_out, axis=1, keepdims=True) + EPS)
     return (proj_out / norm, norm)
-
-
-def unit_columns(weight):
-    wide = weight.astype(jnp.float32)
-    norm = jnp.sqrt(jnp.sum(wide * wide, axis=0) + EPS)
-    return ((wide / norm).astype(jnp.bfloat16), norm)
 
 
 def exchange(blocks, axes):
@@ -46,21 +40,25 @@
     )
 
 
+def over_cores(blocks):
+    return lax.ppermute(blocks, "c", [(0, 1), (1, 0)])
+
+
 def scatter_sum(parts, axes):
     count = lax.axis_size(axes)
     own = parts.shape[0] // count
     blocks = parts.reshape((count, own) + parts.shape[1:])
-    return jnp.sum(lax.all_to_all(blocks, axes, 0, 0, tiled=True), axis=0)
+    blocks = lax.all_to_all(blocks, axes, 0, 0, tiled=True)
+    return jnp.sum(blocks.astype(jnp.float32), axis=0)
 
 
 def project_split(hidden, weight):
-    rows, depth = hidden.shape[0], weight.shape[0]
-    yl, x, c = (lax.axis_size(axis) for axis in SHARD)
-    share = spread(weight, ("yl", "c")).reshape(yl * c * depth, -1)
-    pieces = hidden.reshape(rows, yl, x, c, depth).transpose(2, 0, 1, 3, 4)
-    pieces = lax.all_to_all(pieces.reshape(x, rows, -1), "x", 0, 0, tiled=True)
-    part = jnp.dot(pieces.reshape(x * rows, -1), share, preferred_element_type=jnp.float32)
-    return scatter_sum(part, "x")
+    rows = hidden.shape[0]
+    kept, sent = depth_halves(hidden)
+    both = jnp.concatenate([kept, over_cores(sent)], axis=0)
+    share = spread(weight, ("yl", "x")).reshape(-1, weight.shape[1])
+    part = jnp.dot(both, share, preferred_element_type=jnp.float32)
+    return part[:rows] + over_cores(part[rows:])
 
 
 def swap(block):
@@ -117,14 +115,51 @@
     out_ref[...] = jnp.broadcast_to(block[None], out_ref.shape)
 
 
+def unit_kernel(teacher_ref, student_ref, vt_ref, vs_ref, norm_ref):
+    def unit(ref, out_ref):
+        wide = ref[...].astype(jnp.float32)
+        norm = jnp.sqrt(jnp.sum(wide * wide, axis=0, keepdims=True) + EPS)
+        out_ref[...] = (wide / norm).astype(jnp.bfloat16)
+        return norm
+
+    unit(teacher_ref, vt_ref)
+    norm_ref[...] = unit(student_ref, vs_ref)
+
+
+def halves_kernel(core_ref, hidden_ref, kept_ref, sent_ref):
+    width = kept_ref.shape[1]
+
+    def split(even_ref, odd_ref):
+        for start in range(0, width, LANES):
+            cols = slice(start, start + LANES)
+            even_ref[:, cols] = hidden_ref[:, 2 * start : 2 * start + LANES]
+            odd_ref[:, cols] = hidden_ref[:, 2 * start + LANES : 2 * start + 2 * LANES]
+
+    @pl.when(core_ref[0] == 0)
+    def _():
+        split(kept_ref, sent_ref)
+
+    @pl.when(core_ref[0] != 0)
+    def _():
+        split(sent_ref, kept_ref)
+
+
+def project_kernel(hidden_ref, weight_ref, out_ref):
+    @pl.when(pl.program_id(0) == 0)
+    def _():
+        out_ref[...] = jnp.zeros_like(out_ref)
+
+    out_ref[...] += jnp.dot(hidden_ref[...], weight_ref[...], preferred_element_type=jnp.float32)
+
+
 def first_kernel(z_ref, v_ref, exp_ref, out_ref, acc):
     step = pl.program_id(0)
+    width = v_ref.shape[1]
 
     @pl.when(step == 0)
     def _():
         acc[...] = jnp.zeros_like(acc)
 
-    width = v_ref.shape[1]
     for start in range(0, width, CHUNK):
         cols = slice(start, start + CHUNK)
         product = jnp.dot(z_ref[...], v_ref[:, cols], preferred_element_type=jnp.float32)
@@ -175,7 +210,7 @@
         repeat_out(out_ref, lane_rows(jnp.sum(acc[...], axis=0, keepdims=True)))
 
 
-def student_kernel(parts_ref, exp_ref, z_ref, v_ref, out_ref, scale, acc):
+def student_kernel(parts_ref, exp_ref, y_ref, v_ref, out_ref, z_ref, zt_ref, scale, acc):
     step = pl.program_id(0)
 
     @pl.when(step == 0)
@@ -184,6 +219,10 @@
 
     rows, width = exp_ref.shape
     here = pl.ds(pl.multiple_of(step * rows, rows), rows)
+    y = y_ref[...]
+    z = y / jnp.sqrt(jnp.sum(y * y, axis=1, keepdims=True) + EPS)
+    z_ref[...] = z.astype(jnp.bfloat16)
+    zt_ref[...] = z.T.astype(jnp.bfloat16)
     mass = jnp.zeros((rows, LANES), jnp.float32)
     exps = jnp.zeros((rows, LANES), jnp.float32)
     cross = jnp.zeros((rows, LANES), jnp.float32)
@@ -205,7 +244,7 @@
 
 
 def gradient_kernel(
-    row_parts_ref, col_parts_ref, exp_ref, z_ref, zt_ref, v_ref, dz_ref, dp_ref,
+    row_parts_ref, col_parts_ref, exp_ref, z_ref, zt_ref, v_ref, dz_ref, dp_ref, dots_ref,
     scale, teacher, student, grad,
 ):
     step = pl.program_id(0)
@@ -234,12 +273,47 @@
         dz_ref[here, :] += lax.dot_general(
             grad[here, :], v_ref[...], COL_DIMS, preferred_element_type=jnp.float32
         )
-    dp_ref[...] = jnp.dot(zt_ref[...], grad[...], preferred_element_type=jnp.float32)
-
-
-def params():
+    dproto = jnp.dot(zt_ref[...], grad[...], preferred_element_type=jnp.float32)
+    dp_ref[...] = dproto
+    dots_ref[...] = jnp.sum(v_ref[...].astype(jnp.float32) * dproto, axis=0, keepdims=True)
+
+
+def collect_kernel(proj_ref, dots_ref, loss_ref, out_ref):
+    own, bot = proj_ref.shape[1:]
+    proj = jnp.sum(proj_ref[...], axis=0)
+    dots = dots_ref[...]
+    width = dots.shape[1]
+    rows = -(-(width + LANES) // bot)
+    loss = jnp.broadcast_to(loss_ref[...], (1, rows * bot - width))
+    row = jnp.concatenate([dots, loss], axis=1)
+    pieces = [row[:, i * bot : (i + 1) * bot] for i in range(rows)]
+    pieces.append(jnp.zeros((out_ref.shape[1] - own - rows, bot), jnp.float32))
+    repeat_out(out_ref, jnp.concatenate([proj] + pieces, axis=0))
+
+
+def finish_kernel(parts_ref, dproto_ref, v_ref, norm_ref, proj_ref, grad_ref, loss_ref):
+    copies, height, bot = parts_ref.shape
+    own = proj_ref.shape[0] // copies
+    width = dproto_ref.shape[1] // 2
+    rows = -(-(width + LANES) // bot)
+    for i in range(copies):
+        proj_ref[i * own : (i + 1) * own, :] = parts_ref[i, 0:own, :]
+    lines = []
+    for side in range(2):
+        block = parts_ref[side, own:height, :]
+        for i in range(2 + side, copies, 2):
+            block = block + parts_ref[i, own:height, :]
+        lines.append(jnp.concatenate([block[i : i + 1] for i in range(rows)], axis=1))
+    loss_ref[...] = lines[0][:, width : width + LANES]
+    for side in range(2):
+        cols = slice(side * width, (side + 1) * width)
+        dots = lines[side][:, 0:width]
+        grad_ref[:, cols] = (dproto_ref[:, cols] - v_ref[:, cols] * dots) / norm_ref[:, cols]
+
+
+def params(mib):
     return pltpu.CompilerParams(
-        dimension_semantics=("arbitrary",), vmem_limit_bytes=VMEM_LIMIT
+        dimension_semantics=("arbitrary",), vmem_limit_bytes=mib * MIB
     )
 
 
@@ -255,17 +329,71 @@
     return jax.ShapeDtypeStruct(shape, jnp.float32)
 
 
+def unit_columns(teacher, student):
+    bot, width = teacher.shape
+    step = width // CHUNK
+    wide = student.shape[1] // step
+    return pl.pallas_call(
+        unit_kernel,
+        grid=(step,),
+        in_specs=[
+            pl.BlockSpec((bot, CHUNK), lambda i: (0, i)),
+            pl.BlockSpec((bot, wide), lambda i: (0, i)),
+        ],
+        out_specs=[
+            pl.BlockSpec((bot, CHUNK), lambda i: (0, i)),
+            pl.BlockSpec((bot, wide), lambda i: (0, i)),
+            pl.BlockSpec((1, wide), lambda i: (0, i)),
+        ],
+        out_shape=[
+            jax.ShapeDtypeStruct(teacher.shape, jnp.bfloat16),
+            jax.ShapeDtypeStruct(student.shape, jnp.bfloat16),
+            f32(1, student.shape[1]),
+        ],
+        compiler_params=params(16),
+        cost_estimate=cost(4 * (teacher.size + student.size), 4 * (teacher.size + student.size)),
+    )(teacher, student)
+
+
+def depth_halves(hidden):
+    half = jax.ShapeDtypeStruct((hidden.shape[0], hidden.shape[1] // 2), hidden.dtype)
+    return pl.pallas_call(
+        halves_kernel,
+        in_specs=[pl.BlockSpec(memory_space=pltpu.SMEM), pl.BlockSpec(memory_space=pltpu.VMEM)],
+        out_shape=[half, half],
+        cost_estimate=cost(0, 4 * hidden.size),
+    )(lax.axis_index("c").reshape(1), hidden)
+
+
+def project(hidden, weight):
+    rows, depth = hidden.shape
+    bot = weight.shape[1]
+    return pl.pallas_call(
+        project_kernel,
+        grid=(depth // CHUNK,),
+        in_specs=[
+            pl.BlockSpec((rows, CHUNK), lambda i: (0, i)),
+            pl.BlockSpec((CHUNK, bot), lambda i: (i, 0)),
+        ],
+        out_specs=whole((rows, bot)),
+        out_shape=f32(rows, bot),
+        compiler_params=params(8),
+        cost_estimate=cost(2 * rows * weight.size, 2 * (hidden.size + weight.size)),
+    )(hidden, weight)
+
+
 def first_pass(z, v, copies):
-    rows, width = z.shape[0], v.shape[1]
-    spread_shape = (copies, width // LANES, LANES)
+    rows, bot = z.shape
+    width = v.shape[1]
+    out = (copies, width // LANES, LANES)
     return pl.pallas_call(
         first_kernel,
         grid=(rows // ROWS_BLOCK,),
-        in_specs=[pl.BlockSpec((ROWS_BLOCK, z.shape[1]), lambda i: (i, 0)), whole(v.shape)],
-        out_specs=[pl.BlockSpec((ROWS_BLOCK, width), lambda i: (i, 0)), whole(spread_shape)],
-        out_shape=[f32(rows, width), f32(*spread_shape)],
+        in_specs=[pl.BlockSpec((ROWS_BLOCK, bot), lambda i: (i, 0)), whole(v.shape)],
+        out_specs=[pl.BlockSpec((ROWS_BLOCK, width), lambda i: (i, 0)), whole(out)],
+        out_shape=[f32(rows, width), f32(*out)],
         scratch_shapes=[pltpu.VMEM((8, width), jnp.float32)],
-        compiler_params=params(),
+        compiler_params=params(16),
         cost_estimate=cost(2 * z.size * width, rows * width * 4, rows * width),
     )(z, v)
 
@@ -280,7 +408,7 @@
         out_specs=whole(out),
         out_shape=f32(*out),
         scratch_shapes=[pltpu.VMEM((1, width), jnp.float32), pltpu.VMEM((rows, LANES), jnp.float32)],
-        compiler_params=params(),
+        compiler_params=params(12),
         cost_estimate=cost(2 * exp.size, exp.size * 4),
     )(parts, exp)
 
@@ -295,13 +423,14 @@
         out_specs=whole(out),
         out_shape=f32(*out),
         scratch_shapes=[pltpu.VMEM((rows, LANES), jnp.float32), pltpu.VMEM((8, width), jnp.float32)],
-        compiler_params=params(),
+        compiler_params=params(12),
         cost_estimate=cost(2 * exp.size, exp.size * 4),
     )(parts, exp)
 
 
-def student_pass(parts, exp, z, v, copies):
+def student_pass(parts, exp, y, v, copies):
     rows, width = exp.shape
+    bot = y.shape[1]
     out = (copies, 3 * rows // LANES, LANES)
     return pl.pallas_call(
         student_kernel,
@@ -309,18 +438,26 @@
         in_specs=[
             whole(parts.shape),
             pl.BlockSpec((ROWS_BLOCK, width), lambda i: (i, 0)),
-            pl.BlockSpec((ROWS_BLOCK, z.shape[1]), lambda i: (i, 0)),
+            pl.BlockSpec((ROWS_BLOCK, bot), lambda i: (i, 0)),
             whole(v.shape),
         ],
-        out_specs=whole(out),
-        out_shape=f32(*out),
+        out_specs=[
+            whole(out),
+            pl.BlockSpec((ROWS_BLOCK, bot), lambda i: (i, 0)),
+            pl.BlockSpec((bot, ROWS_BLOCK), lambda i: (0, i)),
+        ],
+        out_shape=[
+            f32(*out),
+            jax.ShapeDtypeStruct((rows, bot), jnp.bfloat16),
+            jax.ShapeDtypeStruct((bot, rows), jnp.bfloat16),
+        ],
         scratch_shapes=[
             pltpu.VMEM((1, width), jnp.float32),
             pltpu.VMEM((3, rows, LANES), jnp.float32),
         ],
-        compiler_params=params(),
-        cost_estimate=cost(2 * z.size * width, exp.size * 4, exp.size),
-    )(parts, exp, z, v)
+        compiler_params=params(16),
+        cost_estimate=cost(2 * y.size * width, exp.size * 4, exp.size),
+    )(parts, exp, y, v)
 
 
 def gradient_pass(row_parts, col_parts, exp, z, zt, v):
@@ -337,15 +474,19 @@
             whole(zt.shape),
             pl.BlockSpec((bot, CHUNK), lambda i: (0, i)),
         ],
-        out_specs=[whole((rows, bot)), pl.BlockSpec((bot, CHUNK), lambda i: (0, i))],
-        out_shape=[f32(rows, bot), f32(bot, width)],
+        out_specs=[
+            whole((rows, bot)),
+            pl.BlockSpec((bot, CHUNK), lambda i: (0, i)),
+            pl.BlockSpec((1, CHUNK), lambda i: (0, i)),
+        ],
+        out_shape=[f32(rows, bot), f32(bot, width), f32(1, width)],
         scratch_shapes=[
             pltpu.VMEM((width // LANES, LANES), jnp.float32),
             pltpu.VMEM((rows, LANES), jnp.float32),
             pltpu.VMEM((rows, LANES), jnp.float32),
             pltpu.VMEM((rows, CHUNK), jnp.bfloat16),
         ],
-        compiler_params=params(),
+        compiler_params=params(24),
         cost_estimate=cost(6 * z.size * width, exp.size * 4, exp.size),
     )(row_parts, col_parts, exp, z, zt, v)
 
@@ -356,36 +497,48 @@
 
 
 def local(hid_teacher, hid_student, proj_teacher, proj_student, proto_teacher, proto_student):
-    rows, bot = hid_teacher.shape[0], proj_teacher.shape[1]
+    bot = proj_teacher.shape[1]
     half = proto_teacher.shape[1] // lax.axis_size("yh")
-    side = lax.axis_index("yh")
-    first = side * half
-    v_t, _ = unit_columns(lax.dynamic_slice_in_dim(proto_teacher, first, half, 1))
-    v_all, norm_all = unit_columns(proto_student)
+    first = lax.axis_index("yh") * half
+    columns, planes = lax.axis_size("z"), lax.axis_size(PLANE)
+
+    gathered = lax.all_gather(proj_student, SHARD, axis=0, tiled=True)
+    z_own = unit_rows(project_split(hid_teacher, proj_teacher))[0].astype(jnp.bfloat16)
+    z_own, proto_teacher, proto_student = lax.optimization_barrier(
+        (z_own, proto_teacher, proto_student)
+    )
+    z_t = spread(z_own, PLANE).reshape(-1, bot)
+    v_t, v_all, norm_all = unit_columns(
+        lax.dynamic_slice_in_dim(proto_teacher, first, half, 1), proto_student
+    )
     v_s = lax.dynamic_slice_in_dim(v_all, first, half, 1)
-    v_t, v_s = lax.optimization_barrier((v_t, v_s))
-
-    y_t = project_split(hid_teacher, proj_teacher)
-    z_t = spread(unit_rows(y_t)[0].astype(jnp.bfloat16), PLANE).reshape(-1, bot)
-    gathered = lax.all_gather(proj_student, SHARD, axis=0, tiled=True)
-    gathered, z_t = lax.optimization_barrier((gathered, z_t))
-    y_s = jnp.dot(hid_student, gathered, preferred_element_type=jnp.float32)
-    unit_s, norm_s = unit_rows(y_s)
+    z_t, v_t, v_s = lax.optimization_barrier((z_t, v_t, v_s))
+    y_s = project(hid_student, gathered)
+    z_t, y_s, hid_student = lax.optimization_barrier((z_t, y_s, hid_student))
     wide_s = lax.all_gather(y_s, PLANE, axis=0, tiled=True)
-    z_s = unit_rows(wide_s)[0].astype(jnp.bfloat16)
     hid_group = lax.all_gather(hid_student, SHARD, axis=0, tiled=True)
 
-    columns, planes = lax.axis_size("z"), lax.axis_size(PLANE)
     teacher_exp, mass = first_pass(z_t, v_t, columns)
     col_parts = exchange(mass, "z")
     for step in range(ITERS - 1):
         row_parts = exchange(row_pass(col_parts, teacher_exp, planes), PLANE)
         col_parts = exchange(column_pass(row_parts, teacher_exp, columns), "z")
-    sums = exchange(student_pass(col_parts, teacher_exp, z_s, v_s, planes), PLANE)
-    dzhat_part, dproto_part = gradient_pass(sums, col_parts, teacher_exp, z_s, z_s.T, v_s)
+    sums, z_s, z_s_t = student_pass(col_parts, teacher_exp, wide_s, v_s, planes)
+    sums = exchange(sums, PLANE)
+    dzhat_part, dproto_part, dots = gradient_pass(sums, col_parts, teacher_exp, z_s, z_s_t, v_s)
+
+    dzhat_part, y_s, hid_group, v_all, sums = lax.optimization_barrier(
+        (dzhat_part, y_s, hid_group, v_all, sums)
+    )
+    unit_s, norm_s = unit_rows(y_s)
     row_mass, expsum, cross = jnp.split(jnp.sum(sums, axis=0), 3, axis=0)
-    row_loss = jnp.sum(jnp.log(expsum) - cross / row_mass / TAU_S)
+    row_count = unit_s.shape[0] * lax.axis_size(DP + SHARD)
+    loss_part = jnp.sum(jnp.log(expsum) - cross / row_mass / TAU_S) / row_count
     dproto = lax.psum_scatter(dproto_part, "z", scatter_dimension=0, tiled=True)
+    last = dproto.shape[0] // lax.axis_size("yh")
+    v_last = lax.dynamic_slice_in_dim(v_all, lax.axis_index(DP) * last, last, 0).astype(jnp.float32)
+    swapped = swap(dproto)
+
     dzhat = scatter_sum(dzhat_part, PLANE)
     dy = norm_backward(dzhat, unit_s, norm_s)
     dy_group = spread(dy, SHARD).reshape(-1, bot)
@@ -394,30 +547,19 @@
         hid_group, lax.axis_index(SHARD) * depth, depth, 1
     )
     proj_term = lax.dot_general(hid_block, dy_group, ROW_DIMS, preferred_element_type=jnp.float32)
-    proj_part = scatter_sum(proj_term, DP)
-
-    own = dproto.shape[0]
-    v_own = lax.dynamic_slice_in_dim(v_s, lax.axis_index("z") * own, own, 0).astype(jnp.float32)
-    dots = jnp.sum(v_own * dproto, axis=0)
-    swapped = swap(dproto)
-    last = own // lax.axis_size("yh")
-    v_swapped = lax.dynamic_slice_in_dim(v_all, lax.axis_index(DP) * last, last, 0).astype(
-        jnp.float32
-    )
-    flat = jnp.concatenate(
-        [proj_part.reshape(-1, LANES), dots.reshape(-1, LANES), jnp.full((8, LANES), row_loss)]
-    )
-    parts = spread(flat, DP)
-    cut = proj_part.size // LANES
-    grad_proj = parts[:, :cut].reshape(-1, bot)
-    sides = jnp.sum(
-        parts[:, cut:].reshape(lax.axis_size("z"), lax.axis_size("yh"), -1), axis=0
-    )
-    dots = sides[:, :half].reshape(-1)
-    row_count = hid_teacher.shape[0] * lax.axis_size(DP + SHARD)
-    loss = sides[0, half] / row_count
-    grad_proto = (swapped - v_swapped * dots[None, :]) / norm_all[None, :]
-    return (loss, grad_proj, grad_proto)
+    proj_parts = exchange(proj_term.reshape(lax.axis_size(DP), -1, bot), DP)
+    height = proj_parts.shape[1] + 8 * -(-(half + LANES) // (8 * bot))
+    collected = pl.pallas_call(
+        collect_kernel,
+        out_shape=f32(proj_parts.shape[0], height, bot),
+        compiler_params=pltpu.CompilerParams(vmem_limit_bytes=8 * MIB),
+    )(proj_parts, dots, loss_part.reshape(1, 1))
+    grad_proj, grad_proto, loss = pl.pallas_call(
+        finish_kernel,
+        out_shape=[f32(depth, bot), f32(last, 2 * half), f32(1, LANES)],
+        compiler_params=pltpu.CompilerParams(vmem_limit_bytes=12 * MIB),
+    )(exchange(collected, DP), swapped, v_last, norm_all)
+    return (loss[0, 0], grad_proj, grad_proto)
 
 
 def solution(mesh):

time: 282 us -> 268 us (0.950)
  blocking collectives: 101 us -> 75.8 us
  local copies, waits for them, and re-layouts: 22.6 us -> 30.9 us
  other arithmetic: 18.4 us -> 10.2 us
  Pallas kernels: 24.9 us -> 31.8 us
  starting transfers between devices: 31.8 us -> 35.6 us
    all_to_all x4 -> x0, blocking collectives: 51.1 us -> none  [the longest x2 29.8 us: spread(): lax.all_to_all(jnp.broadcast_to(block[None], (count,) + block.shape), axe...]
    all_to_all x4 -> x6, blocking collectives: 50.1 us -> 75.8 us  [exchange(): return lax.all_to_all(blocks, axes, 0, 0, tiled=True)]
    all_to_all x2 -> x1, waiting for transfers between devices: 33.3 us -> 20.8 us  [scatter_sum(): blocks = lax.all_to_all(blocks, axes, 0, 0, tiled=True)]
    all_to_all x2 -> x3, starting transfers between devices: 9.03 us -> 18.3 us  [spread(): lax.all_to_all(jnp.broadcast_to(block[None], (count,) + block.shape), axe...]
    unnamed x28 -> x42, local copies, waits for them, and re-layouts: 12.3 us -> 21.4 us
    pallas_call x0 -> x5, Pallas kernels: none -> 7.27 us  [the longest x1 2.4 us: unit_columns(): pl.pallas_call(unit_kernel, grid=(step,), in_specs=[pl.BlockSpec((bot, CH...]
    all_to_all x2, waiting for transfers between devices: 9.24 us -> 15.6 us  [exchange(): return lax.all_to_all(blocks, axes, 0, 0, tiled=True)]
    all_to_all x2 -> x1, starting transfers between devices: 10.9 us -> 5.94 us  [scatter_sum(): blocks = lax.all_to_all(blocks, axes, 0, 0, tiled=True)]
  transfers between devices with their start and end apart: 11 -> 13, of which waited for: 6 -> 10; matrix products, arithmetic and copies ran while one was open for 9% -> 9% of each run, Pallas kernels for 9% -> 11%
where the time goes in v4:
time: 268 us; the launch traced here: 266 us
  blocking collectives  75.8 us (28%)
  waiting for transfers between devices  63.5 us (24%)
  starting transfers between devices  35.6 us (13%)
  Pallas kernels  31.8 us (12%)
  local copies, waits for them, and re-layouts  30.9 us (12%)
  between operations  14.7 us (5%)
  other arithmetic  10.2 us (4%)
  matrix products  3.4 us (1%)
    all_to_all x6, blocking collectives, exchange(): return lax.all_to_all(blocks, axes, 0, 0, tiled=True)  75.8 us
    unnamed x42, local copies, waits for them, and re-layouts  21.4 us
    all_to_all x1, waiting for transfers between devices, scatter_sum(): blocks = lax.all_to_all(blocks, axes, 0, 0, tiled=True)  20.8 us
    all_to_all x3, starting transfers between devices, spread(): lax.all_to_all(jnp.broadcast_to(block[None], (count,) + block.shape), axe...  18.3 us
    all_to_all x3, waiting for transfers between devices, spread(): lax.all_to_all(jnp.broadcast_to(block[None], (count,) + block.shape), axe...  18 us
    all_to_all x2, waiting for transfers between devices, exchange(): return lax.all_to_all(blocks, axes, 0, 0, tiled=True)  15.6 us
    pallas_call x1, Pallas kernels, gradient_pass(): pl.pallas_call(gradient_kernel, grid=(width // CHUNK,), in_specs=[whole(r...  10.5 us
    all_to_all x2, starting transfers between devices, exchange(): return lax.all_to_all(blocks, axes, 0, 0, tiled=True)  7.73 us
  transfers between devices with their start and end apart: 13, of which 10 were waited for; matrix products, arithmetic and copies ran while one was open for 9% of the time, Pallas kernels for 11%

profile of v4, /device:TPU:2, one launch (start us, length us, event | category | flops | bytes accessed | tf_op | source)
XLA Modules:
  0.0 265.8 jit_solution(8559049637945385070)
XLA Ops:
  7.9 2.0 broadcast_in_dim.6
  10.0 6.4 %all-to-all-start = ((bf16[8,128,384]{2,1,0:T(8,128)(2,1)}), bf16[8,128,384]{2,1,0:T(8,128)(2,1)}, u32[]{:S(2)}, u32[]{:S(2)}) async-start(bf16[8,128,384]{2,1,0:T(8,128)(2,1)} %broadcast_in_dim.6), calls=%async_computation | async-start | bytes 1572864 | tf_op jit(solution)/shard_map/all_to_all | solution.py:38
  19.4 8.3 %all-to-all-done = bf16[8,128,384]{2,1,0:T(8,128)(2,1)} async-done(((bf16[8,128,384]{2,1,0:T(8,128)(2,1)}), bf16[8,128,384]{2,1,0:T(8,128)(2,1)}, u32[]{:S(2)}, u32[]{:S(2)}) %all-to-all-start) | async-done | bytes 786464 | tf_op jit(solution)/shard_map/all_to_all | solution.py:38
  31.6 5.9 %all-to-all-start.1 = ((bf16[32,32,384]{2,1,0:T(8,128)(2,1)}), bf16[32,32,384]{2,1,0:T(8,128)(2,1)}, u32[]{:S(2)}, u32[]{:S(2)}) async-start(bf16[32,32,384]{2,1,0:T(8,128)(2,1)} %broadcast_in_dim.7), calls=%async_computation.1 | async-start | bytes 1572864 | tf_op jit(solution)/shard_map/all_to_all | solution.py:38
  37.7 1.8 copy-done.5
  39.5 2.4 shard_map.86
  43.0 1.6 copy-done.13
  45.9 6.3 %all-to-all-done.1 = bf16[32,32,384]{2,1,0:T(8,128)(2,1)} async-done(((bf16[32,32,384]{2,1,0:T(8,128)(2,1)}), bf16[32,32,384]{2,1,0:T(8,128)(2,1)}, u32[]{:S(2)}, u32[]{:S(2)}) %all-to-all-start.1) | async-done | bytes 786464 | tf_op jit(solution)/shard_map/all_to_all | solution.py:38
  57.8 4.1 %shard_map.88 = (f32[1024,2048]{1,0:T(8,128)S(1)}, f32[8,16,128]{2,1,0:T(8,128)S(1)}) custom-call(bf16[1024,384]{1,0:T(8,128)(2,1)} %bitcast.2.z_ref, bf16[384,2048]{1,0:T(8,128)(2,1)S(1)} %copy-done.20), custom_call_target="tpu_custom_call" | custom-call | flops 1610612736 | bytes 8388608 | tf_op jit(solution)/shard_map/pallas_call | solution.py:389
  62.0 17.0 %all_to_all.60.parts_ref = f32[8,16,128]{2,1,0:T(8,128)S(1)} all-to-all(f32[8,16,128]{2,1,0:T(8,128)S(1)} %get-tuple-element.43), channel_id=1, replica_groups=mesh['z'=8,'yh'=2,'yl'=2,'x'=4,'c'=2] {'z'}, dimensions={0} | all-to-all | bytes 131072 | tf_op jit(solution)/shard_map/all_to_all | solution.py:33
  80.2 12.2 %all_to_all.61.parts_ref = f32[32,8,128]{2,1,0:T(8,128)S(1)} all-to-all(f32[32,8,128]{2,1,0:T(8,128)S(1)} %shard_map.89), channel_id=1, replica_groups=mesh['z'=8,'yh'=2,'yl'=2,'x'=4,'c'=2] {'yh','yl','x','c'}, dimensions={0} | all-to-all | bytes 262144 | tf_op jit(solution)/shard_map/all_to_all | solution.py:33
  93.4 10.8 %all_to_all.62.parts_ref = f32[8,16,128]{2,1,0:T(8,128)S(1)} all-to-all(f32[8,16,128]{2,1,0:T(8,128)S(1)} %shard_map.90), channel_id=1, replica_groups=mesh['z'=8,'yh'=2,'yl'=2,'x'=4,'c'=2] {'z'}, dimensions={0} | all-to-all | bytes 131072 | tf_op jit(solution)/shard_map/all_to_all | solution.py:33
  105.3 11.3 %all_to_all.63.parts_ref = f32[32,8,128]{2,1,0:T(8,128)S(1)} all-to-all(f32[32,8,128]{2,1,0:T(8,128)S(1)} %shard_map.91), channel_id=1, replica_groups=mesh['z'=8,'yh'=2,'yl'=2,'x'=4,'c'=2] {'yh','yl','x','c'}, dimensions={0} | all-to-all | bytes 262144 | tf_op jit(solution)/shard_map/all_to_all | solution.py:33
  117.5 10.8 %all_to_all.64.parts_ref.col_parts_ref = f32[8,16,128]{2,1,0:T(8,128)S(1)} all-to-all(f32[8,16,128]{2,1,0:T(8,128)S(1)} %shard_map.92), channel_id=1, replica_groups=mesh['z'=8,'yh'=2,'yl'=2,'x'=4,'c'=2] {'z'}, dimensions={0} | all-to-all | bytes 131072 | tf_op jit(solution)/shard_map/all_to_all | solution.py:33
  128.3 3.5 %copy-done.2 = f32[1024,2048]{1,0:T(8,128)S(1)} copy-done((f32[1024,2048]{1,0:T(8,128)S(1)}, f32[1024,2048]{1,0:T(8,128)}, u32[]{:S(2)}) %copy-start.2) | copy-done | bytes 8388632
  134.6 5.6 %shard_map.93 = (f32[32,24,128]{2,1,0:T(8,128)S(1)}, bf16[1024,384]{1,0:T(8,128)(2,1)S(1)}, bf16[384,1024]{1,0:T(8,128)(2,1)S(1)}) custom-call(f32[8,16,128]{2,1,0:T(8,128)S(1)} %all_to_all.64.parts_ref.col_parts_ref, f32[1024,2048]{1,0:T(8,128)S(1)} %copy-done.2, f32[1024,384]{1,0:T(8,128)S(1)} %copy-done.12, bf16[384,2048]{1,0:T(8,128)(2,1)S(1)} %copy-done.4), custom_call_target="tpu_custom_call" | custom-call | flops 1610612736 | bytes 8388608 | tf_op jit(solution)/shard_map/pallas_call | solution.py:435
  140.3 13.8 %all_to_all.65.row_parts_ref = f32[32,24,128]{2,1,0:T(8,128)S(1)} all-to-all(f32[32,24,128]{2,1,0:T(8,128)S(1)} %get-tuple-element.47), channel_id=1, replica_groups=mesh['z'=8,'yh'=2,'yl'=2,'x'=4,'c'=2] {'yh','yl','x','c'}, dimensions={0} | all-to-all | bytes 786432 | tf_op jit(solution)/shard_map/all_to_all | solution.py:33
  154.9 10.5 %shard_map.94 = (f32[1024,384]{1,0:T(8,128)S(1)}, f32[384,2048]{1,0:T(8,128)S(1)}, f32[1,2048]{1,0:T(1,128)S(1)}) custom-call(f32[32,24,128]{2,1,0:T(8,128)S(1)} %all_to_all.65.row_parts_ref, f32[8,16,128]{2,1,0:T(8,128)S(1)} %copy-done.16, f32[1024,2048]{1,0:T(8,128)S(1)} %copy-done.3, bf16[1024,384]{1,0:T(8,128)(2,1)S(1)} %get-tuple-element.48.z_ref, ...), custom_call_target="tpu_custom_call" | custom-call | flops 4831838208 | bytes 8388608 | tf_op jit(solution)/shard_map/pallas_call | solution.py:466
  168.8 5.9 %all-to-all-start.8 = ((f32[32,32,384]{2,1,0:T(8,128)}), f32[32,32,384]{2,1,0:T(8,128)}, u32[]{:S(2)}, u32[]{:S(2)}) async-start(f32[32,32,384]{2,1,0:T(8,128)} %bitcast.17), calls=%async_computation.8 | async-start | bytes 3145728 | tf_op jit(solution)/shard_map/all_to_all | solution.py:51
  176.2 20.8 %all-to-all-done.8 = f32[32,32,384]{2,1,0:T(8,128)} async-done(((f32[32,32,384]{2,1,0:T(8,128)}), f32[32,32,384]{2,1,0:T(8,128)}, u32[]{:S(2)}, u32[]{:S(2)}) %all-to-all-start.8) | async-done | bytes 1572896 | tf_op jit(solution)/shard_map/all_to_all | solution.py:51
  197.0 2.1 reduce_sum.55
  201.9 6.1 %all-to-all-start.9 = ((bf16[16,32,384]{2,1,0:T(8,128)(2,1)}), bf16[16,32,384]{2,1,0:T(8,128)(2,1)}, u32[]{:S(2)}, u32[]{:S(2)}) async-start(bf16[16,32,384]{2,1,0:T(8,128)(2,1)} %broadcast_in_dim.8), calls=%async_computation.9 | async-start | bytes 786432 | tf_op jit(solution)/shard_map/all_to_all | solution.py:38
  209.5 1.7 copy.10
  211.2 3.4 %all-to-all-done.9 = bf16[16,32,384]{2,1,0:T(8,128)(2,1)} async-done(((bf16[16,32,384]{2,1,0:T(8,128)(2,1)}), bf16[16,32,384]{2,1,0:T(8,128)(2,1)}, u32[]{:S(2)}, u32[]{:S(2)}) %all-to-all-start.9) | async-done | bytes 393248 | tf_op jit(solution)/shard_map/all_to_all | solution.py:38
  214.5 2.0 fusion.4
  216.5 4.2 %all-to-all-start.10 = ((f32[16,8,384]{2,1,0:T(8,128)}), f32[16,8,384]{2,1,0:T(8,128)}, u32[]{:S(2)}, u32[]{:S(2)}) async-start(f32[16,8,384]{2,1,0:T(8,128)} %fusion.4), calls=%async_computation.10 | async-start | bytes 393216 | tf_op jit(solution)/shard_map/all_to_all | solution.py:33
  223.3 11.2 %all-to-all-done.10.proj_ref = f32[16,8,384]{2,1,0:T(8,128)} async-done(((f32[16,8,384]{2,1,0:T(8,128)}), f32[16,8,384]{2,1,0:T(8,128)}, u32[]{:S(2)}, u32[]{:S(2)}) %all-to-all-start.10) | async-done | bytes 196640 | tf_op jit(solution)/shard_map/all_to_all | solution.py:33
  236.9 3.6 %all-to-all-start.11 = ((f32[16,16,384]{2,1,0:T(8,128)}), f32[16,16,384]{2,1,0:T(8,128)S(1)}, u32[]{:S(2)}, u32[]{:S(2)}) async-start(f32[16,16,384]{2,1,0:T(8,128)} %copy-done.9), calls=%async_computation.11 | async-start | bytes 786432 | tf_op jit(solution)/shard_map/all_to_all | solution.py:33
  241.6 3.4 %collective-permute-start.2 = (f32[24,2048]{1,0:T(8,128)S(1)}, f32[24,2048]{1,0:T(8,128)S(1)}, u32[]{:S(2)}, u32[]{:S(2)}) collective-permute-start(f32[24,2048]{1,0:T(8,128)S(1)} %get-tuple-element.64), channel_id=1, source_target_pairs={{0,16},{16,0},{1,17},{17,1},{2,18},{18,2},{3,19},{19,3},{4,20},{20... | collective-permute-start | bytes 589832 | tf_op jit(solution)/shard_map/ppermute | solution.py:69
  245.0 1.7 dynamic-slice_convert_fusion.v_ref
  246.7 4.5 %collective-permute-done.2 = f32[24,2048]{1,0:T(8,128)S(1)} collective-permute-done((f32[24,2048]{1,0:T(8,128)S(1)}, f32[24,2048]{1,0:T(8,128)S(1)}, u32[]{:S(2)}, u32[]{:S(2)}) %collective-permute-start.2) | collective-permute-done | bytes 196640 | tf_op jit(solution)/shard_map/ppermute | solution.py:69
  251.9 4.5 %all-to-all-done.11.parts_ref = f32[16,16,384]{2,1,0:T(8,128)S(1)} async-done(((f32[16,16,384]{2,1,0:T(8,128)}), f32[16,16,384]{2,1,0:T(8,128)S(1)}, u32[]{:S(2)}, u32[]{:S(2)}) %all-to-all-start.11) | async-done | bytes 393248 | tf_op jit(solution)/shard_map/all_to_all | solution.py:33
  (81 shorter events, 42.0 us)
Async XLA Ops:
  7.2 30.4 %copy-start = (bf16[384,4096]{1,0:T(8,128)(2,1)S(1)}, bf16[384,4096]{1,0:T(8,128)(2,1)}, u32[]{:S(2)}) copy-start(bf16[384,4096]{1,0:T(8,128)(2,1)} %param.10) | copy-start | bytes 9437188
  7.2 45.6 %all-gather.4.cloned.1.call-start = ((), (), s32[]{:S(2)}) async-start(), calls=%async_computation.13 | async-start | bytes 1671168 | tf_op jit(solution)/shard_map/all_gather | solution.py:505
  10.0 17.7 %all-to-all-start = ((bf16[8,128,384]{2,1,0:T(8,128)(2,1)}), bf16[8,128,384]{2,1,0:T(8,128)(2,1)}, u32[]{:S(2)}, u32[]{:S(2)}) async-start(bf16[8,128,384]{2,1,0:T(8,128)(2,1)} %broadcast_in_dim.6), calls=%async_computation | async-start | bytes 1572864 | tf_op jit(solution)/shard_map/all_to_all | solution.py:38
  17.9 1.5 collective-permute-start
  29.1 1.3 collective-permute-start.1
  31.6 20.7 %all-to-all-start.1 = ((bf16[32,32,384]{2,1,0:T(8,128)(2,1)}), bf16[32,32,384]{2,1,0:T(8,128)(2,1)}, u32[]{:S(2)}, u32[]{:S(2)}) async-start(bf16[32,32,384]{2,1,0:T(8,128)(2,1)} %broadcast_in_dim.7), calls=%async_computation.1 | async-start | bytes 1572864 | tf_op jit(solution)/shard_map/all_to_all | solution.py:38
  37.5 90.8 %all-gather.6.cloned.1.call-start = ((), (), s32[]{:S(2)}) async-start(), calls=%async_computation.14 | async-start | bytes 1622016 | tf_op jit(solution)/shard_map/all_gather | solution.py:518
  37.5 2.0 copy-start.5
  41.9 1.2 copy-start.19
  43.0 1.6 copy-start.13
  43.0 9.8 %copy-start.14 = (bf16[32,2048]{1,0:T(8,128)(2,1)S(1)}, bf16[32,2048]{1,0:T(8,128)(2,1)}, u32[]{:S(2)}) copy-start(bf16[32,2048]{1,0:T(8,128)(2,1)} %hidden_ref.3) | copy-start | bytes 393220
  52.8 1.4 copy-start.8
  55.6 113.2 %all-gather.8.cloned.1.call-start = ((), (), s32[]{:S(2)}) async-start(), calls=%async_computation.15 | async-start | bytes 2228224 | tf_op jit(solution)/shard_map/all_gather | solution.py:519
  56.4 184.2 %reduce-scatter.2.cloned.1.call-start = ((), (), s32[]{:S(2)}) async-start(), calls=%async_computation.16 | async-start | bytes 3538944 | tf_op jit(solution)/shard_map/reduce_scatter | solution.py:537
  56.4 1.4 copy-start.20
  62.0 54.6 %copy-start.1 = (f32[1024,2048]{1,0:T(8,128)}, f32[1024,2048]{1,0:T(8,128)S(1)}, u32[]{:S(2)}) copy-start(f32[1024,2048]{1,0:T(8,128)S(1)} %get-tuple-element.44.exp_ref) | copy-start | bytes 25165828
  128.3 12.0 %copy-start.15 = (f32[8,16,128]{2,1,0:T(8,128)}, f32[8,16,128]{2,1,0:T(8,128)S(1)}, u32[]{:S(2)}) copy-start(f32[8,16,128]{2,1,0:T(8,128)S(1)} %all_to_all.64.parts_ref.col_parts_ref) | copy-start | bytes 196612
  128.3 3.5 %copy-start.2 = (f32[1024,2048]{1,0:T(8,128)S(1)}, f32[1024,2048]{1,0:T(8,128)}, u32[]{:S(2)}) copy-start(f32[1024,2048]{1,0:T(8,128)} %copy-done.1) | copy-start | bytes 25165828
  131.8 1.4 copy-start.4
  133.2 1.4 copy-start.12
  134.6 19.4 %copy-start.3 = (f32[1024,2048]{1,0:T(8,128)S(1)}, f32[1024,2048]{1,0:T(8,128)}, u32[]{:S(2)}) copy-start(f32[1024,2048]{1,0:T(8,128)} %copy-done.1) | copy-start | bytes 25165828
  154.0 0.8 copy-start.16
  165.4 1.6 copy-start.6
  167.0 1.2 copy-start.7
  168.8 28.2 %all-to-all-start.8 = ((f32[32,32,384]{2,1,0:T(8,128)}), f32[32,32,384]{2,1,0:T(8,128)}, u32[]{:S(2)}, u32[]{:S(2)}) async-start(f32[32,32,384]{2,1,0:T(8,128)} %bitcast.17), calls=%async_computation.8 | async-start | bytes 3145728 | tf_op jit(solution)/shard_map/all_to_all | solution.py:51
  201.9 12.7 %all-to-all-start.9 = ((bf16[16,32,384]{2,1,0:T(8,128)(2,1)}), bf16[16,32,384]{2,1,0:T(8,128)(2,1)}, u32[]{:S(2)}, u32[]{:S(2)}) async-start(bf16[16,32,384]{2,1,0:T(8,128)(2,1)} %broadcast_in_dim.8), calls=%async_computation.9 | async-start | bytes 786432 | tf_op jit(solution)/shard_map/all_to_all | solution.py:38
  216.5 18.0 %all-to-all-start.10 = ((f32[16,8,384]{2,1,0:T(8,128)}), f32[16,8,384]{2,1,0:T(8,128)}, u32[]{:S(2)}, u32[]{:S(2)}) async-start(f32[16,8,384]{2,1,0:T(8,128)} %fusion.4), calls=%async_computation.10 | async-start | bytes 393216 | tf_op jit(solution)/shard_map/all_to_all | solution.py:33
  236.2 0.7 copy-start.9
  236.9 19.5 %all-to-all-start.11 = ((f32[16,16,384]{2,1,0:T(8,128)}), f32[16,16,384]{2,1,0:T(8,128)S(1)}, u32[]{:S(2)}, u32[]{:S(2)}) async-start(f32[16,16,384]{2,1,0:T(8,128)} %copy-done.9), calls=%async_computation.11 | async-start | bytes 786432 | tf_op jit(solution)/shard_map/all_to_all | solution.py:33
  241.6 9.5 %collective-permute-start.2 = (f32[24,2048]{1,0:T(8,128)S(1)}, f32[24,2048]{1,0:T(8,128)S(1)}, u32[]{:S(2)}, u32[]{:S(2)}) collective-permute-start(f32[24,2048]{1,0:T(8,128)S(1)} %get-tuple-element.64), channel_id=1, source_target_pairs={{0,16},{16,0},{1,17},{17,1},{2,18},{18,2},{3,19},{19,3},{4,20},{20... | collective-permute-start | bytes 589832 | tf_op jit(solution)/shard_map/ppermute | solution.py:69
  256.4 1.0 copy-start.10
  257.4 1.0 copy-start.11
  (2 other events, 1.3 us)
Sparse Core Ops, SparseCore 0:
  9.9 42.8 all-gather.3
  55.9 49.4 all-gather.5
  107.3 35.7 all-gather.7
  168.9 40.3 reduce-scatter.1

commit v5 on v4

--- a/solution.py
+++ b/solution.py
@@ -24,41 +24,31 @@
 PLANE = ("yh", "yl", "x", "c")
 
 
-def unit_rows(proj_out):
-    norm = jnp.sqrt(jnp.sum(proj_out * proj_out, axis=1, keepdims=True) + EPS)
-    return (proj_out / norm, norm)
-
-
 def exchange(blocks, axes):
     return lax.all_to_all(blocks, axes, 0, 0, tiled=True)
 
 
-def spread(block, axes):
-    count = lax.axis_size(axes)
-    return lax.all_to_all(
-        jnp.broadcast_to(block[None], (count,) + block.shape), axes, 0, 0, tiled=True
-    )
-
-
 def over_cores(blocks):
     return lax.ppermute(blocks, "c", [(0, 1), (1, 0)])
 
 
-def scatter_sum(parts, axes):
-    count = lax.axis_size(axes)
-    own = parts.shape[0] // count
-    blocks = parts.reshape((count, own) + parts.shape[1:])
-    blocks = lax.all_to_all(blocks, axes, 0, 0, tiled=True)
-    return jnp.sum(blocks.astype(jnp.float32), axis=0)
-
-
-def project_split(hidden, weight):
-    rows = hidden.shape[0]
-    kept, sent = depth_halves(hidden)
+def features_kernel(part_ref, got_ref, out_ref):
+    y = part_ref[0 : got_ref.shape[0], :] + got_ref[...]
+    unit = y / jnp.sqrt(jnp.sum(y * y, axis=1, keepdims=True) + EPS)
+    repeat_out(out_ref, unit.astype(jnp.bfloat16))
+
+
+def unit_split(hidden, weight, copies):
+    rows, bot = hidden.shape[0], weight.shape[1]
+    kept, sent, repeated = depth_halves(hidden, weight, lax.axis_size(("yl", "x")))
+    share = exchange(repeated, ("yl", "x")).reshape(-1, bot)
     both = jnp.concatenate([kept, over_cores(sent)], axis=0)
-    share = spread(weight, ("yl", "x")).reshape(-1, weight.shape[1])
     part = jnp.dot(both, share, preferred_element_type=jnp.float32)
-    return part[:rows] + over_cores(part[rows:])
+    return pl.pallas_call(
+        features_kernel,
+        out_shape=pltpu.HBM((copies, rows, bot), jnp.bfloat16),
+        compiler_params=pltpu.CompilerParams(vmem_limit_bytes=8 * MIB),
+    )(part, over_cores(part[rows:]))
 
 
 def swap(block):
@@ -126,8 +116,9 @@
     norm_ref[...] = unit(student_ref, vs_ref)
 
 
-def halves_kernel(core_ref, hidden_ref, kept_ref, sent_ref):
+def halves_kernel(core_ref, hidden_ref, weight_ref, kept_ref, sent_ref, out_ref):
     width = kept_ref.shape[1]
+    repeat_out(out_ref, weight_ref[...])
 
     def split(even_ref, odd_ref):
         for start in range(0, width, LANES):
@@ -329,6 +320,10 @@
     return jax.ShapeDtypeStruct(shape, jnp.float32)
 
 
+def hbm(array):
+    return pltpu.with_memory_space_constraint(array, pltpu.HBM)
+
+
 def unit_columns(teacher, student):
     bot, width = teacher.shape
     step = width // CHUNK
@@ -355,14 +350,16 @@
     )(teacher, student)
 
 
-def depth_halves(hidden):
+def depth_halves(hidden, weight, copies):
     half = jax.ShapeDtypeStruct((hidden.shape[0], hidden.shape[1] // 2), hidden.dtype)
     return pl.pallas_call(
         halves_kernel,
-        in_specs=[pl.BlockSpec(memory_space=pltpu.SMEM), pl.BlockSpec(memory_space=pltpu.VMEM)],
-        out_shape=[half, half],
-        cost_estimate=cost(0, 4 * hidden.size),
-    )(lax.axis_index("c").reshape(1), hidden)
+        in_specs=[pl.BlockSpec(memory_space=pltpu.SMEM)]
+        + [pl.BlockSpec(memory_space=pltpu.VMEM)] * 2,
+        out_shape=[half, half, pltpu.HBM((copies,) + weight.shape, weight.dtype)],
+        compiler_params=pltpu.CompilerParams(vmem_limit_bytes=8 * MIB),
+        cost_estimate=cost(0, 4 * hidden.size + 2 * copies * weight.size),
+    )(lax.axis_index("c").reshape(1), hbm(hidden), hbm(weight))
 
 
 def project(hidden, weight):
@@ -379,7 +376,7 @@
         out_shape=f32(rows, bot),
         compiler_params=params(8),
         cost_estimate=cost(2 * rows * weight.size, 2 * (hidden.size + weight.size)),
-    )(hidden, weight)
+    )(hidden, hbm(weight))
 
 
 def first_pass(z, v, copies):
@@ -395,7 +392,7 @@
         scratch_shapes=[pltpu.VMEM((8, width), jnp.float32)],
         compiler_params=params(16),
         cost_estimate=cost(2 * z.size * width, rows * width * 4, rows * width),
-    )(z, v)
+    )(z, hbm(v))
 
 
 def row_pass(parts, exp, copies):
@@ -457,7 +454,7 @@
         ],
         compiler_params=params(16),
         cost_estimate=cost(2 * y.size * width, exp.size * 4, exp.size),
-    )(parts, exp, y, v)
+    )(parts, hbm(exp), hbm(y), hbm(v))
 
 
 def gradient_pass(row_parts, col_parts, exp, z, zt, v):
@@ -479,7 +476,11 @@
             pl.BlockSpec((bot, CHUNK), lambda i: (0, i)),
             pl.BlockSpec((1, CHUNK), lambda i: (0, i)),
         ],
-        out_shape=[f32(rows, bot), f32(bot, width), f32(1, width)],
+        out_shape=[
+            pltpu.HBM((rows, bot), jnp.float32),
+            pltpu.HBM((bot, width), jnp.float32),
+            pltpu.HBM((1, width), jnp.float32),
+        ],
         scratch_shapes=[
             pltpu.VMEM((width // LANES, LANES), jnp.float32),
             pltpu.VMEM((rows, LANES), jnp.float32),
@@ -488,12 +489,24 @@
         ],
         compiler_params=params(24),
         cost_estimate=cost(6 * z.size * width, exp.size * 4, exp.size),
-    )(row_parts, col_parts, exp, z, zt, v)
-
-
-def norm_backward(dzhat, unit_s, norm_s):
-    inner = jnp.sum(unit_s * dzhat, axis=1, keepdims=True)
-    return ((dzhat - unit_s * inner) / norm_s).astype(jnp.bfloat16)
+    )(row_parts, col_parts, hbm(exp), z, zt, hbm(v))
+
+
+def backward_kernel(parts_ref, y_ref, out_ref):
+    dzhat = jnp.sum(parts_ref[...], axis=0)
+    y = y_ref[...]
+    norm = jnp.sqrt(jnp.sum(y * y, axis=1, keepdims=True) + EPS)
+    unit = y / norm
+    inner = jnp.sum(unit * dzhat, axis=1, keepdims=True)
+    repeat_out(out_ref, ((dzhat - unit * inner) / norm).astype(jnp.bfloat16))
+
+
+def norm_backward(parts, y, copies):
+    return pl.pallas_call(
+        backward_kernel,
+        out_shape=pltpu.HBM((copies,) + y.shape, jnp.bfloat16),
+        compiler_params=pltpu.CompilerParams(vmem_limit_bytes=8 * MIB),
+    )(parts, hbm(y))
 
 
 def local(hid_teacher, hid_student, proj_teacher, proj_student, proto_teacher, proto_student):
@@ -503,11 +516,11 @@
     columns, planes = lax.axis_size("z"), lax.axis_size(PLANE)
 
     gathered = lax.all_gather(proj_student, SHARD, axis=0, tiled=True)
-    z_own = unit_rows(project_split(hid_teacher, proj_teacher))[0].astype(jnp.bfloat16)
+    z_own = unit_split(hid_teacher, proj_teacher, planes)
     z_own, proto_teacher, proto_student = lax.optimization_barrier(
         (z_own, proto_teacher, proto_student)
     )
-    z_t = spread(z_own, PLANE).reshape(-1, bot)
+    z_t = exchange(z_own, PLANE).reshape(-1, bot)
     v_t, v_all, norm_all = unit_columns(
         lax.dynamic_slice_in_dim(proto_teacher, first, half, 1), proto_student
     )
@@ -530,18 +543,18 @@
     dzhat_part, y_s, hid_group, v_all, sums = lax.optimization_barrier(
         (dzhat_part, y_s, hid_group, v_all, sums)
     )
-    unit_s, norm_s = unit_rows(y_s)
     row_mass, expsum, cross = jnp.split(jnp.sum(sums, axis=0), 3, axis=0)
-    row_count = unit_s.shape[0] * lax.axis_size(DP + SHARD)
+    row_count = y_s.shape[0] * lax.axis_size(DP + SHARD)
     loss_part = jnp.sum(jnp.log(expsum) - cross / row_mass / TAU_S) / row_count
     dproto = lax.psum_scatter(dproto_part, "z", scatter_dimension=0, tiled=True)
     last = dproto.shape[0] // lax.axis_size("yh")
     v_last = lax.dynamic_slice_in_dim(v_all, lax.axis_index(DP) * last, last, 0).astype(jnp.float32)
     swapped = swap(dproto)
 
-    dzhat = scatter_sum(dzhat_part, PLANE)
-    dy = norm_backward(dzhat, unit_s, norm_s)
-    dy_group = spread(dy, SHARD).reshape(-1, bot)
+    dzhat_parts = exchange(dzhat_part.reshape((planes,) + y_s.shape), PLANE)
+    dy_group = exchange(
+        norm_backward(dzhat_parts, y_s, lax.axis_size(SHARD)), SHARD
+    ).reshape(-1, bot)
     depth = proj_student.shape[0]
     hid_block = lax.dynamic_slice_in_dim(
         hid_group, lax.axis_index(SHARD) * depth, depth, 1
@@ -551,14 +564,14 @@
     height = proj_parts.shape[1] + 8 * -(-(half + LANES) // (8 * bot))
     collected = pl.pallas_call(
         collect_kernel,
-        out_shape=f32(proj_parts.shape[0], height, bot),
+        out_shape=pltpu.HBM((proj_parts.shape[0], height, bot), jnp.float32),
         compiler_params=pltpu.CompilerParams(vmem_limit_bytes=8 * MIB),
-    )(proj_parts, dots, loss_part.reshape(1, 1))
+    )(proj_parts, hbm(dots), loss_part.reshape(1, 1))
     grad_proj, grad_proto, loss = pl.pallas_call(
         finish_kernel,
         out_shape=[f32(depth, bot), f32(last, 2 * half), f32(1, LANES)],
         compiler_params=pltpu.CompilerParams(vmem_limit_bytes=12 * MIB),
-    )(exchange(collected, DP), swapped, v_last, norm_all)
+    )(exchange(collected, DP), hbm(swapped), hbm(v_last), hbm(norm_all))
     return (loss[0, 0], grad_proj, grad_proto)
 
 

time: 268 us -> 255 us (0.951)
  blocking collectives: 75.8 us -> 103 us
  local copies, waits for them, and re-layouts: 30.9 us -> 11.8 us
  waiting for transfers between devices: 63.5 us -> 44.9 us
  Pallas kernels: 31.8 us -> 44.2 us
  other arithmetic: 10.2 us -> 3.15 us
  starting transfers between devices: 35.6 us -> 29.1 us
    all_to_all x4 -> x0, waiting for transfers between devices: 38.7 us -> none  [the longest x1 20.8 us: scatter_sum(): blocks = lax.all_to_all(blocks, axes, 0, 0, tiled=True)]
    all_to_all x6 -> x7, blocking collectives: 75.8 us -> 103 us  [exchange(): return lax.all_to_all(blocks, axes, 0, 0, tiled=True)]
    all_to_all x4 -> x0, starting transfers between devices: 24.2 us -> none  [the longest x3 18.3 us: spread(): lax.all_to_all(jnp.broadcast_to(block[None], (count,) + block.shape), axe...]
    all_to_all x2 -> x5, waiting for transfers between devices: 15.6 us -> 36.4 us  [exchange(): return lax.all_to_all(blocks, axes, 0, 0, tiled=True)]
    all_to_all x2 -> x5, starting transfers between devices: 7.73 us -> 25.4 us  [exchange(): return lax.all_to_all(blocks, axes, 0, 0, tiled=True)]
    unnamed x42 -> x18, local copies, waits for them, and re-layouts: 21.4 us -> 6.15 us
    reduce_sum x4 -> x0, other arithmetic: 4.18 us -> none  [the longest x1 2.14 us: scatter_sum(): return jnp.sum(blocks.astype(jnp.float32), axis=0)]
    broadcast_in_dim x3 -> x0, local copies, waits for them, and re-layouts: 3.79 us -> none  [spread(): jnp.broadcast_to(block[None], (count,) + block.shape)]
  transfers between devices with their start and end apart: 13 -> 12, of which waited for: 10 -> 9; matrix products, arithmetic and copies ran while one was open for 9% -> 5% of each run, Pallas kernels for 11% -> 15%
where the time goes in v5:
time: 255 us; the launch traced here: 254 us
  blocking collectives  103 us (40%)
  waiting for transfers between devices  44.9 us (18%)
  Pallas kernels  44.2 us (17%)
  starting transfers between devices  29.1 us (11%)
  between operations  14.6 us (6%)
  local copies, waits for them, and re-layouts  11.8 us (5%)
  matrix products  3.37 us (1%)
  other arithmetic  3.15 us (1%)
    all_to_all x7, blocking collectives, exchange(): return lax.all_to_all(blocks, axes, 0, 0, tiled=True)  103 us
    all_to_all x5, waiting for transfers between devices, exchange(): return lax.all_to_all(blocks, axes, 0, 0, tiled=True)  36.4 us
    all_to_all x5, starting transfers between devices, exchange(): return lax.all_to_all(blocks, axes, 0, 0, tiled=True)  25.4 us
    pallas_call x1, Pallas kernels, gradient_pass(): pl.pallas_call(gradient_kernel, grid=(width // CHUNK,), in_specs=[whole(r...  12.3 us
    pallas_call x1, Pallas kernels, student_pass(): pl.pallas_call(student_kernel, grid=(rows // ROWS_BLOCK,), in_specs=[whol...  8.64 us
    unnamed x18, local copies, waits for them, and re-layouts  6.15 us
  transfers between devices with their start and end apart: 12, of which 9 were waited for; matrix products, arithmetic and copies ran while one was open for 5% of the time, Pallas kernels for 15%

profile of v5, /device:TPU:2, one launch (start us, length us, event | category | flops | bytes accessed | tf_op | source)
XLA Modules:
  0.0 253.8 jit_solution(157000801610030539)
XLA Ops:
  7.9 2.1 shard_map.85
  10.0 6.4 %all-to-all-start = ((bf16[8,128,384]{2,1,0:T(8,128)(2,1)}), bf16[8,128,384]{2,1,0:T(8,128)(2,1)}, u32[]{:S(2)}, u32[]{:S(2)}) async-start(bf16[8,128,384]{2,1,0:T(8,128)(2,1)} %get-tuple-element.36), calls=%async_computation | async-start | bytes 1572864 | tf_op jit(solution)/shard_map/all_to_all | solution.py:28
  17.7 10.1 %all-to-all-done = bf16[8,128,384]{2,1,0:T(8,128)(2,1)} async-done(((bf16[8,128,384]{2,1,0:T(8,128)(2,1)}), bf16[8,128,384]{2,1,0:T(8,128)(2,1)}, u32[]{:S(2)}, u32[]{:S(2)}) %all-to-all-start) | async-done | bytes 786464 | tf_op jit(solution)/shard_map/all_to_all | solution.py:28
  31.5 5.9 %all-to-all-start.1 = ((bf16[32,32,384]{2,1,0:T(8,128)(2,1)}), bf16[32,32,384]{2,1,0:T(8,128)(2,1)}, u32[]{:S(2)}, u32[]{:S(2)}) async-start(bf16[32,32,384]{2,1,0:T(8,128)(2,1)} %shard_map.86), calls=%async_computation.1 | async-start | bytes 1572864 | tf_op jit(solution)/shard_map/all_to_all | solution.py:28
  37.6 1.8 copy-done.2
  39.4 2.4 shard_map.87
  46.6 6.0 %all-to-all-done.1 = bf16[32,32,384]{2,1,0:T(8,128)(2,1)} async-done(((bf16[32,32,384]{2,1,0:T(8,128)(2,1)}), bf16[32,32,384]{2,1,0:T(8,128)(2,1)}, u32[]{:S(2)}, u32[]{:S(2)}) %all-to-all-start.1) | async-done | bytes 786464 | tf_op jit(solution)/shard_map/all_to_all | solution.py:28
  52.7 3.2 %shard_map.88.y_ref = f32[32,384]{1,0:T(8,128)} custom-call(bf16[32,2048]{1,0:T(8,128)(2,1)S(1)} %copy-done.4, bf16[2048,384]{1,0:T(8,128)(2,1)} %all-gather.4.cloned.1.call-done.weight_ref), custom_call_target="tpu_custom_call" | custom-call | flops 50331648 | bytes 1703936 | tf_op jit(solution)/shard_map/pallas_call | solution.py:368
  56.7 4.7 %shard_map.89 = (f32[1024,2048]{1,0:T(8,128)S(1)}, f32[8,16,128]{2,1,0:T(8,128)S(1)}) custom-call(bf16[1024,384]{1,0:T(8,128)(2,1)} %bitcast.2.z_ref, bf16[384,2048]{1,0:T(8,128)(2,1)} %copy-done.8), custom_call_target="tpu_custom_call" | custom-call | flops 1610612736 | bytes 8388608 | tf_op jit(solution)/shard_map/pallas_call | solution.py:386
  61.5 17.3 %all_to_all.60.parts_ref = f32[8,16,128]{2,1,0:T(8,128)S(1)} all-to-all(f32[8,16,128]{2,1,0:T(8,128)S(1)} %get-tuple-element.45), channel_id=1, replica_groups=mesh['z'=8,'yh'=2,'yl'=2,'x'=4,'c'=2] {'z'}, dimensions={0} | all-to-all | bytes 131072 | tf_op jit(solution)/shard_map/all_to_all | solution.py:28
  80.0 12.0 %all_to_all.61.parts_ref = f32[32,8,128]{2,1,0:T(8,128)S(1)} all-to-all(f32[32,8,128]{2,1,0:T(8,128)S(1)} %shard_map.90), channel_id=1, replica_groups=mesh['z'=8,'yh'=2,'yl'=2,'x'=4,'c'=2] {'yh','yl','x','c'}, dimensions={0} | all-to-all | bytes 262144 | tf_op jit(solution)/shard_map/all_to_all | solution.py:28
  92.9 10.8 %all_to_all.62.parts_ref = f32[8,16,128]{2,1,0:T(8,128)S(1)} all-to-all(f32[8,16,128]{2,1,0:T(8,128)S(1)} %shard_map.91), channel_id=1, replica_groups=mesh['z'=8,'yh'=2,'yl'=2,'x'=4,'c'=2] {'z'}, dimensions={0} | all-to-all | bytes 131072 | tf_op jit(solution)/shard_map/all_to_all | solution.py:28
  104.9 11.3 %all_to_all.63.parts_ref = f32[32,8,128]{2,1,0:T(8,128)S(1)} all-to-all(f32[32,8,128]{2,1,0:T(8,128)S(1)} %shard_map.92), channel_id=1, replica_groups=mesh['z'=8,'yh'=2,'yl'=2,'x'=4,'c'=2] {'yh','yl','x','c'}, dimensions={0} | all-to-all | bytes 262144 | tf_op jit(solution)/shard_map/all_to_all | solution.py:28
  117.1 10.8 %all_to_all.64.parts_ref.col_parts_ref = f32[8,16,128]{2,1,0:T(8,128)S(1)} all-to-all(f32[8,16,128]{2,1,0:T(8,128)S(1)} %shard_map.93), channel_id=1, replica_groups=mesh['z'=8,'yh'=2,'yl'=2,'x'=4,'c'=2] {'z'}, dimensions={0} | all-to-all | bytes 131072 | tf_op jit(solution)/shard_map/all_to_all | solution.py:28
  127.9 8.6 %shard_map.94 = (f32[32,24,128]{2,1,0:T(8,128)S(1)}, bf16[1024,384]{1,0:T(8,128)(2,1)S(1)}, bf16[384,1024]{1,0:T(8,128)(2,1)S(1)}) custom-call(f32[8,16,128]{2,1,0:T(8,128)S(1)} %all_to_all.64.parts_ref.col_parts_ref, f32[1024,2048]{1,0:T(8,128)} %copy-done.1, f32[1024,384]{1,0:T(8,128)} %all-gather.6.cloned.1.call-done.y_ref, ...), custom_call_target="tpu_custom_call" | custom-call | flops 1610612736 | bytes 8388608 | tf_op jit(solution)/shard_map/pallas_call | solution.py:432
  136.5 13.6 %all_to_all.65.row_parts_ref = f32[32,24,128]{2,1,0:T(8,128)S(1)} all-to-all(f32[32,24,128]{2,1,0:T(8,128)S(1)} %get-tuple-element.49), channel_id=1, replica_groups=mesh['z'=8,'yh'=2,'yl'=2,'x'=4,'c'=2] {'yh','yl','x','c'}, dimensions={0} | all-to-all | bytes 786432 | tf_op jit(solution)/shard_map/all_to_all | solution.py:28
  151.0 12.3 %shard_map.95 = (f32[1024,384]{1,0:T(8,128)}, f32[384,2048]{1,0:T(8,128)}, f32[1,2048]{1,0:T(1,128)}) custom-call(f32[32,24,128]{2,1,0:T(8,128)S(1)} %all_to_all.65.row_parts_ref, f32[8,16,128]{2,1,0:T(8,128)S(1)} %copy-done.6, f32[1024,2048]{1,0:T(8,128)} %copy-done.1, bf16[1024,384]{1,0:T(8,128)(2,1)S(1)} %get-tuple-element.50.z_ref, ...), custom_call_target="tpu_custom_call" | custom-call | flops 4831838208 | bytes 8388608 | tf_op jit(solution)/shard_map/pallas_call | solution.py:463
  163.3 26.9 %all_to_all.66.parts_ref = f32[32,32,384]{2,1,0:T(8,128)S(1)} all-to-all(f32[32,32,384]{2,1,0:T(8,128)} %bitcast.17), channel_id=1, replica_groups=mesh['z'=8,'yh'=2,'yl'=2,'x'=4,'c'=2] {'yh','yl','x','c'}, dimensions={0} | all-to-all | bytes 3145728 | tf_op jit(solution)/shard_map/all_to_all | solution.py:28
  190.3 1.8 shard_map.96
  192.0 5.5 %all-to-all-start.9 = ((bf16[16,32,384]{2,1,0:T(8,128)(2,1)}), bf16[16,32,384]{2,1,0:T(8,128)(2,1)}, u32[]{:S(2)}, u32[]{:S(2)}) async-start(bf16[16,32,384]{2,1,0:T(8,128)(2,1)} %shard_map.96), calls=%async_computation.9 | async-start | bytes 786432 | tf_op jit(solution)/shard_map/all_to_all | solution.py:28
  199.1 1.7 copy.10
  200.7 3.4 %all-to-all-done.9 = bf16[16,32,384]{2,1,0:T(8,128)(2,1)} async-done(((bf16[16,32,384]{2,1,0:T(8,128)(2,1)}), bf16[16,32,384]{2,1,0:T(8,128)(2,1)}, u32[]{:S(2)}, u32[]{:S(2)}) %all-to-all-start.9) | async-done | bytes 393248 | tf_op jit(solution)/shard_map/all_to_all | solution.py:28
  204.1 2.0 fusion.4
  206.1 4.2 %all-to-all-start.10 = ((f32[16,8,384]{2,1,0:T(8,128)}), f32[16,8,384]{2,1,0:T(8,128)}, u32[]{:S(2)}, u32[]{:S(2)}) async-start(f32[16,8,384]{2,1,0:T(8,128)} %fusion.4), calls=%async_computation.10 | async-start | bytes 393216 | tf_op jit(solution)/shard_map/all_to_all | solution.py:28
  211.6 12.5 %all-to-all-done.10.proj_ref = f32[16,8,384]{2,1,0:T(8,128)} async-done(((f32[16,8,384]{2,1,0:T(8,128)}), f32[16,8,384]{2,1,0:T(8,128)}, u32[]{:S(2)}, u32[]{:S(2)}) %all-to-all-start.10) | async-done | bytes 196640 | tf_op jit(solution)/shard_map/all_to_all | solution.py:28
  224.0 1.8 shard_map.97
  225.8 3.6 %all-to-all-start.11 = ((f32[16,16,384]{2,1,0:T(8,128)}), f32[16,16,384]{2,1,0:T(8,128)S(1)}, u32[]{:S(2)}, u32[]{:S(2)}) async-start(f32[16,16,384]{2,1,0:T(8,128)} %shard_map.97), calls=%async_computation.11 | async-start | bytes 786432 | tf_op jit(solution)/shard_map/all_to_all | solution.py:28
  230.4 3.4 %collective-permute-start.2 = (f32[24,2048]{1,0:T(8,128)S(1)}, f32[24,2048]{1,0:T(8,128)S(1)}, u32[]{:S(2)}, u32[]{:S(2)}) collective-permute-start(f32[24,2048]{1,0:T(8,128)S(1)} %get-tuple-element.66), channel_id=1, source_target_pairs={{0,16},{16,0},{1,17},{17,1},{2,18},{18,2},{3,19},{19,3},{4,20},{20... | collective-permute-start | bytes 589832 | tf_op jit(solution)/shard_map/ppermute | solution.py:59
  233.8 1.7 dynamic-slice_convert_fusion.v_ref
  235.5 4.4 %collective-permute-done.2 = f32[24,2048]{1,0:T(8,128)S(1)} collective-permute-done((f32[24,2048]{1,0:T(8,128)S(1)}, f32[24,2048]{1,0:T(8,128)S(1)}, u32[]{:S(2)}, u32[]{:S(2)}) %collective-permute-start.2) | collective-permute-done | bytes 196640 | tf_op jit(solution)/shard_map/ppermute | solution.py:59
  240.8 4.5 %all-to-all-done.11.parts_ref = f32[16,16,384]{2,1,0:T(8,128)S(1)} async-done(((f32[16,16,384]{2,1,0:T(8,128)}), f32[16,16,384]{2,1,0:T(8,128)S(1)}, u32[]{:S(2)}, u32[]{:S(2)}) %all-to-all-start.11) | async-done | bytes 393248 | tf_op jit(solution)/shard_map/all_to_all | solution.py:28
  245.3 2.0 shard_map.98
  (47 shorter events, 20.8 us)
Async XLA Ops:
  7.2 30.3 %copy-start = (bf16[384,4096]{1,0:T(8,128)(2,1)S(1)}, bf16[384,4096]{1,0:T(8,128)(2,1)}, u32[]{:S(2)}) copy-start(bf16[384,4096]{1,0:T(8,128)(2,1)} %param.10) | copy-start | bytes 9437188
  7.2 45.5 %all-gather.4.cloned.1.call-start = ((), (), s32[]{:S(2)}) async-start(), calls=%async_computation.13 | async-start | bytes 1671168 | tf_op jit(solution)/shard_map/all_gather | solution.py:518
  10.0 17.7 %all-to-all-start = ((bf16[8,128,384]{2,1,0:T(8,128)(2,1)}), bf16[8,128,384]{2,1,0:T(8,128)(2,1)}, u32[]{:S(2)}, u32[]{:S(2)}) async-start(bf16[8,128,384]{2,1,0:T(8,128)(2,1)} %get-tuple-element.36), calls=%async_computation | async-start | bytes 1572864 | tf_op jit(solution)/shard_map/all_to_all | solution.py:28
  16.4 1.3 collective-permute-start
  29.2 1.3 collective-permute-start.1
  31.5 21.1 %all-to-all-start.1 = ((bf16[32,32,384]{2,1,0:T(8,128)(2,1)}), bf16[32,32,384]{2,1,0:T(8,128)(2,1)}, u32[]{:S(2)}, u32[]{:S(2)}) async-start(bf16[32,32,384]{2,1,0:T(8,128)(2,1)} %shard_map.86), calls=%async_computation.1 | async-start | bytes 1572864 | tf_op jit(solution)/shard_map/all_to_all | solution.py:28
  37.4 90.5 %all-gather.6.cloned.1.call-start = ((), (), s32[]{:S(2)}) async-start(), calls=%async_computation.14 | async-start | bytes 1622016 | tf_op jit(solution)/shard_map/all_gather | solution.py:531
  37.5 1.9 copy-start.2
  41.8 0.6 copy-start.7
  42.4 1.2 copy-start.8
  43.6 1.7 copy-start.3
  43.6 9.1 %copy-start.4 = (bf16[32,2048]{1,0:T(8,128)(2,1)S(1)}, bf16[32,2048]{1,0:T(8,128)(2,1)}, u32[]{:S(2)}) copy-start(bf16[32,2048]{1,0:T(8,128)(2,1)} %hidden_ref.3) | copy-start | bytes 393220
  55.9 107.4 %all-gather.8.cloned.1.call-start = ((), (), s32[]{:S(2)}) async-start(), calls=%async_computation.15 | async-start | bytes 2228224 | tf_op jit(solution)/shard_map/all_gather | solution.py:532
  56.7 172.7 %reduce-scatter.2.cloned.1.call-start = ((), (), s32[]{:S(2)}) async-start(), calls=%async_computation.16 | async-start | bytes 3538944 | tf_op jit(solution)/shard_map/reduce_scatter | solution.py:549
  61.5 54.7 %copy-start.1 = (f32[1024,2048]{1,0:T(8,128)}, f32[1024,2048]{1,0:T(8,128)S(1)}, u32[]{:S(2)}) copy-start(f32[1024,2048]{1,0:T(8,128)S(1)} %get-tuple-element.46.exp_ref) | copy-start | bytes 25165828
  127.9 8.7 %copy-start.5 = (f32[8,16,128]{2,1,0:T(8,128)}, f32[8,16,128]{2,1,0:T(8,128)S(1)}, u32[]{:S(2)}) copy-start(f32[8,16,128]{2,1,0:T(8,128)S(1)} %all_to_all.64.parts_ref.col_parts_ref) | copy-start | bytes 196612
  150.2 0.8 copy-start.6
  192.0 12.1 %all-to-all-start.9 = ((bf16[16,32,384]{2,1,0:T(8,128)(2,1)}), bf16[16,32,384]{2,1,0:T(8,128)(2,1)}, u32[]{:S(2)}, u32[]{:S(2)}) async-start(bf16[16,32,384]{2,1,0:T(8,128)(2,1)} %shard_map.96), calls=%async_computation.9 | async-start | bytes 786432 | tf_op jit(solution)/shard_map/all_to_all | solution.py:28
  206.1 18.0 %all-to-all-start.10 = ((f32[16,8,384]{2,1,0:T(8,128)}), f32[16,8,384]{2,1,0:T(8,128)}, u32[]{:S(2)}, u32[]{:S(2)}) async-start(f32[16,8,384]{2,1,0:T(8,128)} %fusion.4), calls=%async_computation.10 | async-start | bytes 393216 | tf_op jit(solution)/shard_map/all_to_all | solution.py:28
  225.8 19.5 %all-to-all-start.11 = ((f32[16,16,384]{2,1,0:T(8,128)}), f32[16,16,384]{2,1,0:T(8,128)S(1)}, u32[]{:S(2)}, u32[]{:S(2)}) async-start(f32[16,16,384]{2,1,0:T(8,128)} %shard_map.97), calls=%async_computation.11 | async-start | bytes 786432 | tf_op jit(solution)/shard_map/all_to_all | solution.py:28
  230.4 9.5 %collective-permute-start.2 = (f32[24,2048]{1,0:T(8,128)S(1)}, f32[24,2048]{1,0:T(8,128)S(1)}, u32[]{:S(2)}, u32[]{:S(2)}) collective-permute-start(f32[24,2048]{1,0:T(8,128)S(1)} %get-tuple-element.66), channel_id=1, source_target_pairs={{0,16},{16,0},{1,17},{17,1},{2,18},{18,2},{3,19},{19,3},{4,20},{20... | collective-permute-start | bytes 589832 | tf_op jit(solution)/shard_map/ppermute | solution.py:59
Sparse Core Ops, SparseCore 0:
  9.9 42.7 all-gather.3
  56.1 49.4 all-gather.5
  107.4 35.8 all-gather.7
  163.4 41.0 reduce-scatter.1

commit v6 on v5

--- a/solution.py
+++ b/solution.py
@@ -14,8 +14,11 @@
 EPS = 1e-06
 LANES = 128
 ROWS_BLOCK = 256
+TALL_BLOCK = 512
+DEPTH_BLOCK = 1024
 CHUNK = 512
 MIB = 1024 * 1024
+WIRE_SCALE = 4.0
 ROW_DIMS = (((0,), (0,)), ((), ()))
 COL_DIMS = (((1,), (1,)), ((), ()))
 
@@ -235,8 +238,8 @@
 
 
 def gradient_kernel(
-    row_parts_ref, col_parts_ref, exp_ref, z_ref, zt_ref, v_ref, dz_ref, dp_ref, dots_ref,
-    scale, teacher, student, grad,
+    row_parts_ref, col_parts_ref, exp_ref, z_ref, zt_ref, v_ref, y_ref, dy_ref, dp_ref, dots_ref,
+    scale, teacher, student, grad, dz,
 ):
     step = pl.program_id(0)
     rows, width = exp_ref.shape
@@ -249,7 +252,7 @@
         teacher[...] = down(factor / sums[0:tall])
         student[...] = down(factor / sums[tall : 2 * tall])
         scale[...] = 1.0 / jnp.sum(col_parts_ref[...], axis=0)
-        dz_ref[...] = jnp.zeros_like(dz_ref)
+        dz[...] = jnp.zeros_like(dz)
 
     groups = width // LANES
     col = one_row(scale[pl.ds(pl.multiple_of(step * groups, groups), groups), :])
@@ -261,12 +264,22 @@
             cols = slice(piece, piece + LANES)
             target = exp_ref[here, cols] * col[:, cols] * teacher[here, :]
             grad[here, cols] = (prob[:, cols] * student[here, :] - target).astype(jnp.bfloat16)
-        dz_ref[here, :] += lax.dot_general(
+        dz[here, :] += lax.dot_general(
             grad[here, :], v_ref[...], COL_DIMS, preferred_element_type=jnp.float32
         )
     dproto = jnp.dot(zt_ref[...], grad[...], preferred_element_type=jnp.float32)
     dp_ref[...] = dproto
     dots_ref[...] = jnp.sum(v_ref[...].astype(jnp.float32) * dproto, axis=0, keepdims=True)
+
+    @pl.when(step == pl.num_programs(0) - 1)
+    def _():
+        for start in range(0, rows, ROWS_BLOCK):
+            here = slice(start, start + ROWS_BLOCK)
+            y = y_ref[here, :]
+            part = dz[here, :]
+            square = jnp.sum(y * y, axis=1, keepdims=True) + EPS
+            inner = jnp.sum(y * part, axis=1, keepdims=True)
+            dy_ref[here, :] = part - y * (inner / square)
 
 
 def collect_kernel(proj_ref, dots_ref, loss_ref, out_ref):
@@ -345,7 +358,7 @@
             jax.ShapeDtypeStruct(student.shape, jnp.bfloat16),
             f32(1, student.shape[1]),
         ],
-        compiler_params=params(16),
+        compiler_params=params(20),
         cost_estimate=cost(4 * (teacher.size + student.size), 4 * (teacher.size + student.size)),
     )(teacher, student)
 
@@ -367,10 +380,10 @@
     bot = weight.shape[1]
     return pl.pallas_call(
         project_kernel,
-        grid=(depth // CHUNK,),
+        grid=(depth // DEPTH_BLOCK,),
         in_specs=[
-            pl.BlockSpec((rows, CHUNK), lambda i: (0, i)),
-            pl.BlockSpec((CHUNK, bot), lambda i: (i, 0)),
+            pl.BlockSpec((rows, DEPTH_BLOCK), lambda i: (0, i)),
+            pl.BlockSpec((DEPTH_BLOCK, bot), lambda i: (i, 0)),
         ],
         out_specs=whole((rows, bot)),
         out_shape=f32(rows, bot),
@@ -385,12 +398,12 @@
     out = (copies, width // LANES, LANES)
     return pl.pallas_call(
         first_kernel,
-        grid=(rows // ROWS_BLOCK,),
-        in_specs=[pl.BlockSpec((ROWS_BLOCK, bot), lambda i: (i, 0)), whole(v.shape)],
-        out_specs=[pl.BlockSpec((ROWS_BLOCK, width), lambda i: (i, 0)), whole(out)],
+        grid=(rows // TALL_BLOCK,),
+        in_specs=[pl.BlockSpec((TALL_BLOCK, bot), lambda i: (i, 0)), whole(v.shape)],
+        out_specs=[pl.BlockSpec((TALL_BLOCK, width), lambda i: (i, 0)), whole(out)],
         out_shape=[f32(rows, width), f32(*out)],
         scratch_shapes=[pltpu.VMEM((8, width), jnp.float32)],
-        compiler_params=params(16),
+        compiler_params=params(20),
         cost_estimate=cost(2 * z.size * width, rows * width * 4, rows * width),
     )(z, hbm(v))
 
@@ -405,7 +418,7 @@
         out_specs=whole(out),
         out_shape=f32(*out),
         scratch_shapes=[pltpu.VMEM((1, width), jnp.float32), pltpu.VMEM((rows, LANES), jnp.float32)],
-        compiler_params=params(12),
+        compiler_params=params(20),
         cost_estimate=cost(2 * exp.size, exp.size * 4),
     )(parts, exp)
 
@@ -420,7 +433,7 @@
         out_specs=whole(out),
         out_shape=f32(*out),
         scratch_shapes=[pltpu.VMEM((rows, LANES), jnp.float32), pltpu.VMEM((8, width), jnp.float32)],
-        compiler_params=params(12),
+        compiler_params=params(20),
         cost_estimate=cost(2 * exp.size, exp.size * 4),
     )(parts, exp)
 
@@ -452,12 +465,12 @@
             pltpu.VMEM((1, width), jnp.float32),
             pltpu.VMEM((3, rows, LANES), jnp.float32),
         ],
-        compiler_params=params(16),
+        compiler_params=params(20),
         cost_estimate=cost(2 * y.size * width, exp.size * 4, exp.size),
     )(parts, hbm(exp), hbm(y), hbm(v))
 
 
-def gradient_pass(row_parts, col_parts, exp, z, zt, v):
+def gradient_pass(row_parts, col_parts, exp, z, zt, v, y):
     rows, width = exp.shape
     bot = z.shape[1]
     return pl.pallas_call(
@@ -470,6 +483,7 @@
             whole(z.shape),
             whole(zt.shape),
             pl.BlockSpec((bot, CHUNK), lambda i: (0, i)),
+            whole(y.shape),
         ],
         out_specs=[
             whole((rows, bot)),
@@ -486,27 +500,25 @@
             pltpu.VMEM((rows, LANES), jnp.float32),
             pltpu.VMEM((rows, LANES), jnp.float32),
             pltpu.VMEM((rows, CHUNK), jnp.bfloat16),
-        ],
-        compiler_params=params(24),
+            pltpu.VMEM((rows, bot), jnp.float32),
+        ],
+        compiler_params=params(20),
         cost_estimate=cost(6 * z.size * width, exp.size * 4, exp.size),
-    )(row_parts, col_parts, hbm(exp), z, zt, hbm(v))
-
-
-def backward_kernel(parts_ref, y_ref, out_ref):
-    dzhat = jnp.sum(parts_ref[...], axis=0)
+    )(row_parts, col_parts, exp, z, zt, v, y)
+
+
+def backward_kernel(sum_ref, y_ref, out_ref):
     y = y_ref[...]
     norm = jnp.sqrt(jnp.sum(y * y, axis=1, keepdims=True) + EPS)
-    unit = y / norm
-    inner = jnp.sum(unit * dzhat, axis=1, keepdims=True)
-    repeat_out(out_ref, ((dzhat - unit * inner) / norm).astype(jnp.bfloat16))
-
-
-def norm_backward(parts, y, copies):
+    repeat_out(out_ref, (sum_ref[...] / norm).astype(jnp.bfloat16))
+
+
+def norm_backward(total, y, copies):
     return pl.pallas_call(
         backward_kernel,
         out_shape=pltpu.HBM((copies,) + y.shape, jnp.bfloat16),
         compiler_params=pltpu.CompilerParams(vmem_limit_bytes=8 * MIB),
-    )(parts, hbm(y))
+    )(total, hbm(y))
 
 
 def local(hid_teacher, hid_student, proj_teacher, proj_student, proto_teacher, proto_student):
@@ -535,14 +547,17 @@
     col_parts = exchange(mass, "z")
     for step in range(ITERS - 1):
         row_parts = exchange(row_pass(col_parts, teacher_exp, planes), PLANE)
-        col_parts = exchange(column_pass(row_parts, teacher_exp, columns), "z")
+        mass = column_pass(row_parts, teacher_exp, columns)
+        if step == ITERS - 2:
+            mass, wide_s = lax.optimization_barrier((mass, wide_s))
+        col_parts = exchange(mass, "z")
     sums, z_s, z_s_t = student_pass(col_parts, teacher_exp, wide_s, v_s, planes)
     sums = exchange(sums, PLANE)
-    dzhat_part, dproto_part, dots = gradient_pass(sums, col_parts, teacher_exp, z_s, z_s_t, v_s)
-
-    dzhat_part, y_s, hid_group, v_all, sums = lax.optimization_barrier(
-        (dzhat_part, y_s, hid_group, v_all, sums)
-    )
+    dy_part, dproto_part, dots = gradient_pass(
+        sums, col_parts, teacher_exp, z_s, z_s_t, v_s, wide_s
+    )
+
+    dy_part, hid_group, v_all, sums = lax.optimization_barrier((dy_part, hid_group, v_all, sums))
     row_mass, expsum, cross = jnp.split(jnp.sum(sums, axis=0), 3, axis=0)
     row_count = y_s.shape[0] * lax.axis_size(DP + SHARD)
     loss_part = jnp.sum(jnp.log(expsum) - cross / row_mass / TAU_S) / row_count
@@ -551,9 +566,10 @@
     v_last = lax.dynamic_slice_in_dim(v_all, lax.axis_index(DP) * last, last, 0).astype(jnp.float32)
     swapped = swap(dproto)
 
-    dzhat_parts = exchange(dzhat_part.reshape((planes,) + y_s.shape), PLANE)
+    parts = (dy_part * WIRE_SCALE).astype(jnp.float16).reshape((planes,) + y_s.shape)
+    tangent = jnp.sum(exchange(parts, PLANE).astype(jnp.float32), axis=0) * (1.0 / WIRE_SCALE)
     dy_group = exchange(
-        norm_backward(dzhat_parts, y_s, lax.axis_size(SHARD)), SHARD
+        norm_backward(tangent, y_s, lax.axis_size(SHARD)), SHARD
     ).reshape(-1, bot)
     depth = proj_student.shape[0]
     hid_block = lax.dynamic_slice_in_dim(

time: 255 us -> 247 us (0.969)
  blocking collectives: 103 us -> 93.7 us
    all_to_all x7, blocking collectives: 103 us -> 93.7 us  [exchange(): return lax.all_to_all(blocks, axes, 0, 0, tiled=True)]
    unnamed x18 -> x20, local copies, waits for them, and re-layouts: 6.15 us -> 5.16 us
  transfers between devices with their start and end apart: 12 -> 12, of which waited for: 9 -> 9; matrix products, arithmetic and copies ran while one was open for 5% -> 6% of each run, Pallas kernels for 15% -> 16%
where the time goes in v6:
time: 247 us; the launch traced here: 245 us
  blocking collectives  93.7 us (38%)
  waiting for transfers between devices  45.6 us (18%)
  Pallas kernels  43.3 us (18%)
  starting transfers between devices  29 us (12%)
  between operations  14.7 us (6%)
  local copies, waits for them, and re-layouts  11 us (4%)
  other arithmetic  4.84 us (2%)
  matrix products  3.37 us (1%)
    all_to_all x7, blocking collectives, exchange(): return lax.all_to_all(blocks, axes, 0, 0, tiled=True)  93.7 us
    all_to_all x5, waiting for transfers between devices, exchange(): return lax.all_to_all(blocks, axes, 0, 0, tiled=True)  36.4 us
    all_to_all x5, starting transfers between devices, exchange(): return lax.all_to_all(blocks, axes, 0, 0, tiled=True)  25.4 us
    pallas_call x1, Pallas kernels, gradient_pass(): pl.pallas_call(gradient_kernel, grid=(width // CHUNK,), in_specs=[whole(r...  12.2 us
    pallas_call x1, Pallas kernels, student_pass(): pl.pallas_call(student_kernel, grid=(rows // ROWS_BLOCK,), in_specs=[whol...  9.45 us
    unnamed x20, local copies, waits for them, and re-layouts  5.16 us
  transfers between devices with their start and end apart: 12, of which 9 were waited for; matrix products, arithmetic and copies ran while one was open for 6% of the time, Pallas kernels for 16%

profile of v6, /device:TPU:2, one launch (start us, length us, event | category | flops | bytes accessed | tf_op | source)
XLA Modules:
  0.0 245.5 jit_solution(17378928270957586555)
XLA Ops:
  7.9 2.1 shard_map.85
  10.0 6.4 %all-to-all-start = ((bf16[8,128,384]{2,1,0:T(8,128)(2,1)}), bf16[8,128,384]{2,1,0:T(8,128)(2,1)}, u32[]{:S(2)}, u32[]{:S(2)}) async-start(bf16[8,128,384]{2,1,0:T(8,128)(2,1)} %get-tuple-element.37), calls=%async_computation | async-start | bytes 1572864 | tf_op jit(solution)/shard_map/all_to_all | solution.py:31
  17.7 10.1 %all-to-all-done = bf16[8,128,384]{2,1,0:T(8,128)(2,1)} async-done(((bf16[8,128,384]{2,1,0:T(8,128)(2,1)}), bf16[8,128,384]{2,1,0:T(8,128)(2,1)}, u32[]{:S(2)}, u32[]{:S(2)}) %all-to-all-start) | async-done | bytes 786464 | tf_op jit(solution)/shard_map/all_to_all | solution.py:31
  31.5 5.9 %all-to-all-start.1 = ((bf16[32,32,384]{2,1,0:T(8,128)(2,1)}), bf16[32,32,384]{2,1,0:T(8,128)(2,1)}, u32[]{:S(2)}, u32[]{:S(2)}) async-start(bf16[32,32,384]{2,1,0:T(8,128)(2,1)} %shard_map.86), calls=%async_computation.1 | async-start | bytes 1572864 | tf_op jit(solution)/shard_map/all_to_all | solution.py:31
  37.7 1.8 copy-done.4
  39.4 2.4 shard_map.87
  46.5 5.9 %all-to-all-done.1 = bf16[32,32,384]{2,1,0:T(8,128)(2,1)} async-done(((bf16[32,32,384]{2,1,0:T(8,128)(2,1)}), bf16[32,32,384]{2,1,0:T(8,128)(2,1)}, u32[]{:S(2)}, u32[]{:S(2)}) %all-to-all-start.1) | async-done | bytes 786464 | tf_op jit(solution)/shard_map/all_to_all | solution.py:31
  52.8 2.2 shard_map.88.y_ref
  55.8 4.2 %shard_map.89 = (f32[1024,2048]{1,0:T(8,128)S(1)}, f32[8,16,128]{2,1,0:T(8,128)S(1)}) custom-call(bf16[1024,384]{1,0:T(8,128)(2,1)} %bitcast.2.z_ref, bf16[384,2048]{1,0:T(8,128)(2,1)} %copy-done.9), custom_call_target="tpu_custom_call" | custom-call | flops 1610612736 | bytes 8388608 | tf_op jit(solution)/shard_map/pallas_call | solution.py:399
  60.0 17.3 %all_to_all.60.parts_ref = f32[8,16,128]{2,1,0:T(8,128)S(1)} all-to-all(f32[8,16,128]{2,1,0:T(8,128)S(1)} %get-tuple-element.46), channel_id=1, replica_groups=mesh['z'=8,'yh'=2,'yl'=2,'x'=4,'c'=2] {'z'}, dimensions={0} | all-to-all | bytes 131072 | tf_op jit(solution)/shard_map/all_to_all | solution.py:31
  78.5 11.9 %all_to_all.61.parts_ref = f32[32,8,128]{2,1,0:T(8,128)S(1)} all-to-all(f32[32,8,128]{2,1,0:T(8,128)S(1)} %shard_map.90), channel_id=1, replica_groups=mesh['z'=8,'yh'=2,'yl'=2,'x'=4,'c'=2] {'yh','yl','x','c'}, dimensions={0} | all-to-all | bytes 262144 | tf_op jit(solution)/shard_map/all_to_all | solution.py:31
  91.4 10.8 %all_to_all.62.parts_ref = f32[8,16,128]{2,1,0:T(8,128)S(1)} all-to-all(f32[8,16,128]{2,1,0:T(8,128)S(1)} %shard_map.91), channel_id=1, replica_groups=mesh['z'=8,'yh'=2,'yl'=2,'x'=4,'c'=2] {'z'}, dimensions={0} | all-to-all | bytes 131072 | tf_op jit(solution)/shard_map/all_to_all | solution.py:31
  103.3 11.3 %all_to_all.63.parts_ref = f32[32,8,128]{2,1,0:T(8,128)S(1)} all-to-all(f32[32,8,128]{2,1,0:T(8,128)S(1)} %shard_map.92), channel_id=1, replica_groups=mesh['z'=8,'yh'=2,'yl'=2,'x'=4,'c'=2] {'yh','yl','x','c'}, dimensions={0} | all-to-all | bytes 262144 | tf_op jit(solution)/shard_map/all_to_all | solution.py:31
  115.6 10.8 %all_to_all.64.parts_ref.col_parts_ref = f32[8,16,128]{2,1,0:T(8,128)S(1)} all-to-all(f32[8,16,128]{2,1,0:T(8,128)S(1)} %shard_map.93), channel_id=1, replica_groups=mesh['z'=8,'yh'=2,'yl'=2,'x'=4,'c'=2] {'z'}, dimensions={0} | all-to-all | bytes 131072 | tf_op jit(solution)/shard_map/all_to_all | solution.py:31
  126.4 9.4 %shard_map.94 = (f32[32,24,128]{2,1,0:T(8,128)S(1)}, bf16[1024,384]{1,0:T(8,128)(2,1)S(1)}, bf16[384,1024]{1,0:T(8,128)(2,1)S(1)}) custom-call(f32[8,16,128]{2,1,0:T(8,128)S(1)} %all_to_all.64.parts_ref.col_parts_ref, f32[1024,2048]{1,0:T(8,128)} %copy-done.1, f32[1024,384]{1,0:T(8,128)} %all-gather.6.cloned.1.call-done.y_ref, ...), custom_call_target="tpu_custom_call" | custom-call | flops 1610612736 | bytes 8388608 | tf_op jit(solution)/shard_map/pallas_call | solution.py:445
  135.8 13.8 %all_to_all.65.row_parts_ref = f32[32,24,128]{2,1,0:T(8,128)S(1)} all-to-all(f32[32,24,128]{2,1,0:T(8,128)S(1)} %get-tuple-element.52), channel_id=1, replica_groups=mesh['z'=8,'yh'=2,'yl'=2,'x'=4,'c'=2] {'yh','yl','x','c'}, dimensions={0} | all-to-all | bytes 786432 | tf_op jit(solution)/shard_map/all_to_all | solution.py:31
  149.6 12.2 %shard_map.95 = (f32[1024,384]{1,0:T(8,128)}, f32[384,2048]{1,0:T(8,128)}, f32[1,2048]{1,0:T(1,128)}) custom-call(f32[32,24,128]{2,1,0:T(8,128)S(1)} %all_to_all.65.row_parts_ref, f32[8,16,128]{2,1,0:T(8,128)S(1)} %all_to_all.64.parts_ref.col_parts_ref, f32[1024,2048]{1,0:T(8,128)S(1)} %copy-done.2, bf16[1024,384]{1,0:T(8,128)(2,1)S(1)} %get-tuple-element.53.z_ref, ...), custom_call_target="tpu_custom_call" | custom-call | flops 4831838208 | bytes 8388608 | tf_op jit(solution)/shard_map/pallas_call | solution.py:476
  163.4 18.0 %all_to_all.66 = f16[32,32,384]{2,1,0:T(8,128)(2,1)S(1)} all-to-all(f16[32,32,384]{2,1,0:T(8,128)(2,1)S(1)} %bitcast.17), channel_id=1, replica_groups=mesh['z'=8,'yh'=2,'yl'=2,'x'=4,'c'=2] {'yh','yl','x','c'}, dimensions={0} | all-to-all | bytes 1572864 | tf_op jit(solution)/shard_map/all_to_all | solution.py:31
  181.4 1.7 shard_map.96
  183.1 5.4 %all-to-all-start.9 = ((bf16[16,32,384]{2,1,0:T(8,128)(2,1)}), bf16[16,32,384]{2,1,0:T(8,128)(2,1)}, u32[]{:S(2)}, u32[]{:S(2)}) async-start(bf16[16,32,384]{2,1,0:T(8,128)(2,1)} %shard_map.96), calls=%async_computation.9 | async-start | bytes 786432 | tf_op jit(solution)/shard_map/all_to_all | solution.py:31
  190.1 1.7 copy.10
  191.8 3.4 %all-to-all-done.9 = bf16[16,32,384]{2,1,0:T(8,128)(2,1)} async-done(((bf16[16,32,384]{2,1,0:T(8,128)(2,1)}), bf16[16,32,384]{2,1,0:T(8,128)(2,1)}, u32[]{:S(2)}, u32[]{:S(2)}) %all-to-all-start.9) | async-done | bytes 393248 | tf_op jit(solution)/shard_map/all_to_all | solution.py:31
  195.2 2.0 fusion.4
  197.2 4.2 %all-to-all-start.10 = ((f32[16,8,384]{2,1,0:T(8,128)}), f32[16,8,384]{2,1,0:T(8,128)}, u32[]{:S(2)}, u32[]{:S(2)}) async-start(f32[16,8,384]{2,1,0:T(8,128)} %fusion.4), calls=%async_computation.10 | async-start | bytes 393216 | tf_op jit(solution)/shard_map/all_to_all | solution.py:31
  202.7 12.6 %all-to-all-done.10.proj_ref = f32[16,8,384]{2,1,0:T(8,128)} async-done(((f32[16,8,384]{2,1,0:T(8,128)}), f32[16,8,384]{2,1,0:T(8,128)}, u32[]{:S(2)}, u32[]{:S(2)}) %all-to-all-start.10) | async-done | bytes 196640 | tf_op jit(solution)/shard_map/all_to_all | solution.py:31
  215.2 1.8 shard_map.97
  217.0 3.6 %all-to-all-start.11 = ((f32[16,16,384]{2,1,0:T(8,128)}), f32[16,16,384]{2,1,0:T(8,128)S(1)}, u32[]{:S(2)}, u32[]{:S(2)}) async-start(f32[16,16,384]{2,1,0:T(8,128)} %shard_map.97), calls=%async_computation.11 | async-start | bytes 786432 | tf_op jit(solution)/shard_map/all_to_all | solution.py:31
  221.6 3.4 %collective-permute-start.2 = (f32[24,2048]{1,0:T(8,128)S(1)}, f32[24,2048]{1,0:T(8,128)S(1)}, u32[]{:S(2)}, u32[]{:S(2)}) collective-permute-start(f32[24,2048]{1,0:T(8,128)S(1)} %get-tuple-element.68), channel_id=1, source_target_pairs={{0,16},{16,0},{1,17},{17,1},{2,18},{18,2},{3,19},{19,3},{4,20},{20... | collective-permute-start | bytes 589832 | tf_op jit(solution)/shard_map/ppermute | solution.py:62
  225.0 1.7 dynamic-slice_convert_fusion.v_ref
  226.7 4.9 %collective-permute-done.2 = f32[24,2048]{1,0:T(8,128)S(1)} collective-permute-done((f32[24,2048]{1,0:T(8,128)S(1)}, f32[24,2048]{1,0:T(8,128)S(1)}, u32[]{:S(2)}, u32[]{:S(2)}) %collective-permute-start.2) | collective-permute-done | bytes 196640 | tf_op jit(solution)/shard_map/ppermute | solution.py:62
  232.5 4.5 %all-to-all-done.11.parts_ref = f32[16,16,384]{2,1,0:T(8,128)S(1)} async-done(((f32[16,16,384]{2,1,0:T(8,128)}), f32[16,16,384]{2,1,0:T(8,128)S(1)}, u32[]{:S(2)}, u32[]{:S(2)}) %all-to-all-start.11) | async-done | bytes 393248 | tf_op jit(solution)/shard_map/all_to_all | solution.py:31
  236.9 2.0 shard_map.98
  (52 shorter events, 21.9 us)
Async XLA Ops:
  7.2 30.3 %copy-start = (bf16[384,4096]{1,0:T(8,128)(2,1)S(1)}, bf16[384,4096]{1,0:T(8,128)(2,1)}, u32[]{:S(2)}) copy-start(bf16[384,4096]{1,0:T(8,128)(2,1)} %param.10) | copy-start | bytes 9437188
  7.2 45.6 %all-gather.4.cloned.1.call-start = ((), (), s32[]{:S(2)}) async-start(), calls=%async_computation.13 | async-start | bytes 1671168 | tf_op jit(solution)/shard_map/all_gather | solution.py:530
  10.0 17.7 %all-to-all-start = ((bf16[8,128,384]{2,1,0:T(8,128)(2,1)}), bf16[8,128,384]{2,1,0:T(8,128)(2,1)}, u32[]{:S(2)}, u32[]{:S(2)}) async-start(bf16[8,128,384]{2,1,0:T(8,128)(2,1)} %get-tuple-element.37), calls=%async_computation | async-start | bytes 1572864 | tf_op jit(solution)/shard_map/all_to_all | solution.py:31
  16.4 1.3 collective-permute-start
  29.2 1.3 collective-permute-start.1
  31.5 20.9 %all-to-all-start.1 = ((bf16[32,32,384]{2,1,0:T(8,128)(2,1)}), bf16[32,32,384]{2,1,0:T(8,128)(2,1)}, u32[]{:S(2)}, u32[]{:S(2)}) async-start(bf16[32,32,384]{2,1,0:T(8,128)(2,1)} %shard_map.86), calls=%async_computation.1 | async-start | bytes 1572864 | tf_op jit(solution)/shard_map/all_to_all | solution.py:31
  37.4 78.2 %all-gather.6.cloned.1.call-start = ((), (), s32[]{:S(2)}) async-start(), calls=%async_computation.14 | async-start | bytes 1622016 | tf_op jit(solution)/shard_map/all_gather | solution.py:543
  37.5 1.9 copy-start.4
  41.8 0.6 copy-start.8
  42.4 1.1 copy-start.9
  43.6 1.7 copy-start.6
  45.2 7.5 %copy-start.7 = (bf16[32,2048]{1,0:T(8,128)(2,1)S(1)}, bf16[32,2048]{1,0:T(8,128)(2,1)}, u32[]{:S(2)}) copy-start(bf16[32,2048]{1,0:T(8,128)(2,1)} %hidden_ref.3) | copy-start | bytes 393220
  55.0 106.8 %all-gather.8.cloned.1.call-start = ((), (), s32[]{:S(2)}) async-start(), calls=%async_computation.15 | async-start | bytes 2228224 | tf_op jit(solution)/shard_map/all_gather | solution.py:544
  55.8 164.8 %reduce-scatter.2.cloned.1.call-start = ((), (), s32[]{:S(2)}) async-start(), calls=%async_computation.16 | async-start | bytes 3538944 | tf_op jit(solution)/shard_map/reduce_scatter | solution.py:564
  60.0 54.6 %copy-start.1 = (f32[1024,2048]{1,0:T(8,128)}, f32[1024,2048]{1,0:T(8,128)S(1)}, u32[]{:S(2)}) copy-start(f32[1024,2048]{1,0:T(8,128)S(1)} %get-tuple-element.47.exp_ref) | copy-start | bytes 25165828
  126.4 23.2 %copy-start.2 = (f32[1024,2048]{1,0:T(8,128)S(1)}, f32[1024,2048]{1,0:T(8,128)}, u32[]{:S(2)}) copy-start(f32[1024,2048]{1,0:T(8,128)} %copy-done.1) | copy-start | bytes 25165828
  126.4 23.2 %copy-start.3 = (bf16[384,2048]{1,0:T(8,128)(2,1)S(1)}, bf16[384,2048]{1,0:T(8,128)(2,1)}, u32[]{:S(2)}) copy-start(bf16[384,2048]{1,0:T(8,128)(2,1)} %constant_dynamic-slice_fusion.2.v_ref) | copy-start | bytes 4718596
  126.4 23.2 %copy-start.5 = (f32[1024,384]{1,0:T(8,128)S(1)}, f32[1024,384]{1,0:T(8,128)}, u32[]{:S(2)}) copy-start(f32[1024,384]{1,0:T(8,128)} %all-gather.6.cloned.1.call-done.y_ref) | copy-start | bytes 4718596
  183.1 12.1 %all-to-all-start.9 = ((bf16[16,32,384]{2,1,0:T(8,128)(2,1)}), bf16[16,32,384]{2,1,0:T(8,128)(2,1)}, u32[]{:S(2)}, u32[]{:S(2)}) async-start(bf16[16,32,384]{2,1,0:T(8,128)(2,1)} %shard_map.96), calls=%async_computation.9 | async-start | bytes 786432 | tf_op jit(solution)/shard_map/all_to_all | solution.py:31
  197.2 18.1 %all-to-all-start.10 = ((f32[16,8,384]{2,1,0:T(8,128)}), f32[16,8,384]{2,1,0:T(8,128)}, u32[]{:S(2)}, u32[]{:S(2)}) async-start(f32[16,8,384]{2,1,0:T(8,128)} %fusion.4), calls=%async_computation.10 | async-start | bytes 393216 | tf_op jit(solution)/shard_map/all_to_all | solution.py:31
  217.0 20.0 %all-to-all-start.11 = ((f32[16,16,384]{2,1,0:T(8,128)}), f32[16,16,384]{2,1,0:T(8,128)S(1)}, u32[]{:S(2)}, u32[]{:S(2)}) async-start(f32[16,16,384]{2,1,0:T(8,128)} %shard_map.97), calls=%async_computation.11 | async-start | bytes 786432 | tf_op jit(solution)/shard_map/all_to_all | solution.py:31
  221.6 10.0 %collective-permute-start.2 = (f32[24,2048]{1,0:T(8,128)S(1)}, f32[24,2048]{1,0:T(8,128)S(1)}, u32[]{:S(2)}, u32[]{:S(2)}) collective-permute-start(f32[24,2048]{1,0:T(8,128)S(1)} %get-tuple-element.68), channel_id=1, source_target_pairs={{0,16},{16,0},{1,17},{17,1},{2,18},{18,2},{3,19},{19,3},{4,20},{20... | collective-permute-start | bytes 589832 | tf_op jit(solution)/shard_map/ppermute | solution.py:62
Sparse Core Ops, SparseCore 0:
  9.9 42.8 all-gather.3
  55.9 49.4 all-gather.5
  107.2 35.8 all-gather.7
  161.9 41.0 reduce-scatter.1

commit v7 on v6

--- a/solution.py
+++ b/solution.py
@@ -204,36 +204,48 @@
         repeat_out(out_ref, lane_rows(jnp.sum(acc[...], axis=0, keepdims=True)))
 
 
-def student_kernel(parts_ref, exp_ref, y_ref, v_ref, out_ref, z_ref, zt_ref, scale, acc):
+def student_kernel(y_ref, v_ref, z_ref, zt_ref, scores_ref, out_ref, acc):
     step = pl.program_id(0)
-
-    @pl.when(step == 0)
-    def _():
-        scale[...] = one_row(1.0 / jnp.sum(parts_ref[...], axis=0))
-
-    rows, width = exp_ref.shape
-    here = pl.ds(pl.multiple_of(step * rows, rows), rows)
+    rows, width = scores_ref.shape
     y = y_ref[...]
     z = y / jnp.sqrt(jnp.sum(y * y, axis=1, keepdims=True) + EPS)
     z_ref[...] = z.astype(jnp.bfloat16)
     zt_ref[...] = z.T.astype(jnp.bfloat16)
-    mass = jnp.zeros((rows, LANES), jnp.float32)
     exps = jnp.zeros((rows, LANES), jnp.float32)
-    cross = jnp.zeros((rows, LANES), jnp.float32)
     for start in range(0, width, CHUNK):
         cols = slice(start, start + CHUNK)
         scores = jnp.dot(z_ref[...], v_ref[:, cols], preferred_element_type=jnp.float32)
+        scores_ref[:, cols] = scores.astype(jnp.bfloat16)
+        exps += fold_lanes(jnp.exp(scores * (1.0 / TAU_S)))
+    acc[pl.ds(pl.multiple_of(step * rows, rows), rows), :] = exps
+
+    @pl.when(step == pl.num_programs(0) - 1)
+    def _():
+        out_ref[...] = lane_sums(acc[...])
+
+
+def last_kernel(parts_ref, exps_ref, exp_ref, scores_ref, out_ref, scale, acc):
+    step = pl.program_id(0)
+
+    @pl.when(step == 0)
+    def _():
+        scale[...] = one_row(1.0 / jnp.sum(parts_ref[...], axis=0))
+
+    rows, width = exp_ref.shape
+    here = pl.ds(pl.multiple_of(step * rows, rows), rows)
+    mass = jnp.zeros((rows, LANES), jnp.float32)
+    cross = jnp.zeros((rows, LANES), jnp.float32)
+    for start in range(0, width, LANES):
+        cols = slice(start, start + LANES)
         weighted = exp_ref[:, cols] * scale[:, cols]
-        mass += fold_lanes(weighted)
-        exps += fold_lanes(jnp.exp(scores * (1.0 / TAU_S)))
-        cross += fold_lanes(weighted * scores)
+        mass += weighted
+        cross += weighted * scores_ref[:, cols].astype(jnp.float32)
     acc[0, here, :] = mass
-    acc[1, here, :] = exps
-    acc[2, here, :] = cross
+    acc[1, here, :] = cross
 
     @pl.when(step == pl.num_programs(0) - 1)
     def _():
-        sums = [lane_sums(acc[i]) for i in range(3)]
+        sums = [lane_sums(acc[0]), exps_ref[...], lane_sums(acc[1])]
         repeat_out(out_ref, jnp.concatenate(sums, axis=0))
 
 
@@ -438,36 +450,52 @@
     )(parts, exp)
 
 
-def student_pass(parts, exp, y, v, copies):
+def student_pass(y, v):
+    rows, bot = y.shape
+    width = v.shape[1]
+    return pl.pallas_call(
+        student_kernel,
+        grid=(rows // ROWS_BLOCK,),
+        in_specs=[pl.BlockSpec((ROWS_BLOCK, bot), lambda i: (i, 0)), whole(v.shape)],
+        out_specs=[
+            pl.BlockSpec((ROWS_BLOCK, bot), lambda i: (i, 0)),
+            pl.BlockSpec((bot, ROWS_BLOCK), lambda i: (0, i)),
+            pl.BlockSpec((ROWS_BLOCK, width), lambda i: (i, 0)),
+            whole((rows // LANES, LANES)),
+        ],
+        out_shape=[
+            jax.ShapeDtypeStruct((rows, bot), jnp.bfloat16),
+            jax.ShapeDtypeStruct((bot, rows), jnp.bfloat16),
+            pltpu.HBM((rows, width), jnp.bfloat16),
+            f32(rows // LANES, LANES),
+        ],
+        scratch_shapes=[pltpu.VMEM((rows, LANES), jnp.float32)],
+        compiler_params=params(20),
+        cost_estimate=cost(2 * y.size * width, rows * width * 4, rows * width),
+    )(hbm(y), hbm(v))
+
+
+def last_pass(parts, exps, exp, scores, copies):
     rows, width = exp.shape
-    bot = y.shape[1]
     out = (copies, 3 * rows // LANES, LANES)
     return pl.pallas_call(
-        student_kernel,
+        last_kernel,
         grid=(rows // ROWS_BLOCK,),
         in_specs=[
             whole(parts.shape),
+            whole(exps.shape),
             pl.BlockSpec((ROWS_BLOCK, width), lambda i: (i, 0)),
-            pl.BlockSpec((ROWS_BLOCK, bot), lambda i: (i, 0)),
-            whole(v.shape),
-        ],
-        out_specs=[
-            whole(out),
-            pl.BlockSpec((ROWS_BLOCK, bot), lambda i: (i, 0)),
-            pl.BlockSpec((bot, ROWS_BLOCK), lambda i: (0, i)),
-        ],
-        out_shape=[
-            f32(*out),
-            jax.ShapeDtypeStruct((rows, bot), jnp.bfloat16),
-            jax.ShapeDtypeStruct((bot, rows), jnp.bfloat16),
-        ],
+            pl.BlockSpec((ROWS_BLOCK, width), lambda i: (i, 0)),
+        ],
+        out_specs=whole(out),
+        out_shape=f32(*out),
         scratch_shapes=[
             pltpu.VMEM((1, width), jnp.float32),
-            pltpu.VMEM((3, rows, LANES), jnp.float32),
+            pltpu.VMEM((2, rows, LANES), jnp.float32),
         ],
         compiler_params=params(20),
-        cost_estimate=cost(2 * y.size * width, exp.size * 4, exp.size),
-    )(parts, hbm(exp), hbm(y), hbm(v))
+        cost_estimate=cost(4 * exp.size, exp.size * 6),
+    )(parts, exps, hbm(exp), hbm(scores))
 
 
 def gradient_pass(row_parts, col_parts, exp, z, zt, v, y):
@@ -537,7 +565,9 @@
         lax.dynamic_slice_in_dim(proto_teacher, first, half, 1), proto_student
     )
     v_s = lax.dynamic_slice_in_dim(v_all, first, half, 1)
-    z_t, v_t, v_s = lax.optimization_barrier((z_t, v_t, v_s))
+    last = bot // lax.axis_size(DP)
+    v_last = lax.dynamic_slice_in_dim(v_all, lax.axis_index(DP) * last, last, 0).astype(jnp.float32)
+    z_t, v_t, v_s, v_last = lax.optimization_barrier((z_t, v_t, v_s, v_last))
     y_s = project(hid_student, gathered)
     z_t, y_s, hid_student = lax.optimization_barrier((z_t, y_s, hid_student))
     wide_s = lax.all_gather(y_s, PLANE, axis=0, tiled=True)
@@ -550,21 +580,18 @@
         mass = column_pass(row_parts, teacher_exp, columns)
         if step == ITERS - 2:
             mass, wide_s = lax.optimization_barrier((mass, wide_s))
+            z_s, z_s_t, scores, exps = student_pass(wide_s, v_s)
         col_parts = exchange(mass, "z")
-    sums, z_s, z_s_t = student_pass(col_parts, teacher_exp, wide_s, v_s, planes)
-    sums = exchange(sums, PLANE)
+    sums = exchange(last_pass(col_parts, exps, teacher_exp, scores, planes), PLANE)
     dy_part, dproto_part, dots = gradient_pass(
         sums, col_parts, teacher_exp, z_s, z_s_t, v_s, wide_s
     )
 
-    dy_part, hid_group, v_all, sums = lax.optimization_barrier((dy_part, hid_group, v_all, sums))
+    dy_part, hid_group, sums = lax.optimization_barrier((dy_part, hid_group, sums))
     row_mass, expsum, cross = jnp.split(jnp.sum(sums, axis=0), 3, axis=0)
     row_count = y_s.shape[0] * lax.axis_size(DP + SHARD)
     loss_part = jnp.sum(jnp.log(expsum) - cross / row_mass / TAU_S) / row_count
     dproto = lax.psum_scatter(dproto_part, "z", scatter_dimension=0, tiled=True)
-    last = dproto.shape[0] // lax.axis_size("yh")
-    v_last = lax.dynamic_slice_in_dim(v_all, lax.axis_index(DP) * last, last, 0).astype(jnp.float32)
-    swapped = swap(dproto)
 
     parts = (dy_part * WIRE_SCALE).astype(jnp.float16).reshape((planes,) + y_s.shape)
     tangent = jnp.sum(exchange(parts, PLANE).astype(jnp.float32), axis=0) * (1.0 / WIRE_SCALE)
@@ -583,6 +610,7 @@
         out_shape=pltpu.HBM((proj_parts.shape[0], height, bot), jnp.float32),
         compiler_params=pltpu.CompilerParams(vmem_limit_bytes=8 * MIB),
     )(proj_parts, hbm(dots), loss_part.reshape(1, 1))
+    swapped = swap(dproto)
     grad_proj, grad_proto, loss = pl.pallas_call(
         finish_kernel,
         out_shape=[f32(depth, bot), f32(last, 2 * half), f32(1, LANES)],

time: 247 us -> 251 us (1.016)
  blocking collectives: 93.7 us -> 83.2 us
  starting transfers between devices: 29 us -> 35.5 us
  Pallas kernels: 43.3 us -> 49.2 us
    all_to_all x7 -> x6, blocking collectives: 93.7 us -> 83.2 us  [exchange(): return lax.all_to_all(blocks, axes, 0, 0, tiled=True)]
    all_to_all x5 -> x6, starting transfers between devices: 25.4 us -> 32 us  [exchange(): return lax.all_to_all(blocks, axes, 0, 0, tiled=True)]
    pallas_call x1 -> x2, Pallas kernels: 9.45 us -> 14.6 us  [the longest x1 7.48 us: last_pass(): pl.pallas_call(last_kernel, grid=(rows // ROWS_BLOCK,), in_specs=[whole(p...]
    unnamed x20 -> x30, local copies, waits for them, and re-layouts: 5.16 us -> 5.26 us
    all_to_all x5 -> x6, waiting for transfers between devices: 36.4 us -> 36.4 us  [exchange(): return lax.all_to_all(blocks, axes, 0, 0, tiled=True)]
  transfers between devices with their start and end apart: 12 -> 13, of which waited for: 9 -> 9; matrix products, arithmetic and copies ran while one was open for 6% -> 6% of each run, Pallas kernels for 16% -> 18%
where the time goes in v7:
time: 251 us; the launch traced here: 250 us
  blocking collectives  83.2 us (33%)
  Pallas kernels  49.2 us (20%)
  waiting for transfers between devices  47 us (19%)
  starting transfers between devices  35.5 us (14%)
  between operations  14.7 us (6%)
  local copies, waits for them, and re-layouts  11.9 us (5%)
  other arithmetic  5.11 us (2%)
  matrix products  3.37 us (1%)
    all_to_all x6, blocking collectives, exchange(): return lax.all_to_all(blocks, axes, 0, 0, tiled=True)  83.2 us
    all_to_all x6, waiting for transfers between devices, exchange(): return lax.all_to_all(blocks, axes, 0, 0, tiled=True)  36.4 us
    all_to_all x6, starting transfers between devices, exchange(): return lax.all_to_all(blocks, axes, 0, 0, tiled=True)  32 us
    pallas_call x1, Pallas kernels, gradient_pass(): pl.pallas_call(gradient_kernel, grid=(width // CHUNK,), in_specs=[whole(r...  12.2 us
    pallas_call x1, Pallas kernels, last_pass(): pl.pallas_call(last_kernel, grid=(rows // ROWS_BLOCK,), in_specs=[whole(p...  7.48 us
    pallas_call x1, Pallas kernels, student_pass(): pl.pallas_call(student_kernel, grid=(rows // ROWS_BLOCK,), in_specs=[pl.B...  7.12 us
    ppermute x1, waiting for transfers between devices, swap(): got = lax.ppermute(sent, 'yh', [(0, 1), (1, 0)])  6.62 us
    unnamed x30, local copies, waits for them, and re-layouts  5.26 us
  transfers between devices with their start and end apart: 13, of which 9 were waited for; matrix products, arithmetic and copies ran while one was open for 6% of the time, Pallas kernels for 18%

profile of v7, /device:TPU:2, one launch (start us, length us, event | category | flops | bytes accessed | tf_op | source)
XLA Modules:
  0.0 249.9 jit_solution(12292673190729538772)
XLA Ops:
  7.9 2.1 shard_map.85
  10.0 6.4 %all-to-all-start = ((bf16[8,128,384]{2,1,0:T(8,128)(2,1)}), bf16[8,128,384]{2,1,0:T(8,128)(2,1)}, u32[]{:S(2)}, u32[]{:S(2)}) async-start(bf16[8,128,384]{2,1,0:T(8,128)(2,1)} %get-tuple-element.38), calls=%async_computation | async-start | bytes 1572864 | tf_op jit(solution)/shard_map/all_to_all | solution.py:31
  17.7 10.1 %all-to-all-done = bf16[8,128,384]{2,1,0:T(8,128)(2,1)} async-done(((bf16[8,128,384]{2,1,0:T(8,128)(2,1)}), bf16[8,128,384]{2,1,0:T(8,128)(2,1)}, u32[]{:S(2)}, u32[]{:S(2)}) %all-to-all-start) | async-done | bytes 786464 | tf_op jit(solution)/shard_map/all_to_all | solution.py:31
  31.5 5.9 %all-to-all-start.1 = ((bf16[32,32,384]{2,1,0:T(8,128)(2,1)}), bf16[32,32,384]{2,1,0:T(8,128)(2,1)}, u32[]{:S(2)}, u32[]{:S(2)}) async-start(bf16[32,32,384]{2,1,0:T(8,128)(2,1)} %shard_map.86), calls=%async_computation.1 | async-start | bytes 1572864 | tf_op jit(solution)/shard_map/all_to_all | solution.py:31
  37.6 1.8 copy-done.3
  39.4 2.4 shard_map.87
  44.3 8.4 %all-to-all-done.1 = bf16[32,32,384]{2,1,0:T(8,128)(2,1)} async-done(((bf16[32,32,384]{2,1,0:T(8,128)(2,1)}), bf16[32,32,384]{2,1,0:T(8,128)(2,1)}, u32[]{:S(2)}, u32[]{:S(2)}) %all-to-all-start.1) | async-done | bytes 786464 | tf_op jit(solution)/shard_map/all_to_all | solution.py:31
  52.7 2.3 shard_map.88.y_ref
  55.7 4.2 %shard_map.89 = (f32[1024,2048]{1,0:T(8,128)S(1)}, f32[8,16,128]{2,1,0:T(8,128)S(1)}) custom-call(bf16[1024,384]{1,0:T(8,128)(2,1)} %bitcast.2.z_ref, bf16[384,2048]{1,0:T(8,128)(2,1)} %copy-done.10), custom_call_target="tpu_custom_call" | custom-call | flops 1610612736 | bytes 8388608 | tf_op jit(solution)/shard_map/pallas_call | solution.py:411
  59.9 17.3 %all_to_all.60.parts_ref = f32[8,16,128]{2,1,0:T(8,128)S(1)} all-to-all(f32[8,16,128]{2,1,0:T(8,128)S(1)} %get-tuple-element.47), channel_id=1, replica_groups=mesh['z'=8,'yh'=2,'yl'=2,'x'=4,'c'=2] {'z'}, dimensions={0} | all-to-all | bytes 131072 | tf_op jit(solution)/shard_map/all_to_all | solution.py:31
  78.4 12.0 %all_to_all.61.parts_ref = f32[32,8,128]{2,1,0:T(8,128)S(1)} all-to-all(f32[32,8,128]{2,1,0:T(8,128)S(1)} %shard_map.90), channel_id=1, replica_groups=mesh['z'=8,'yh'=2,'yl'=2,'x'=4,'c'=2] {'yh','yl','x','c'}, dimensions={0} | all-to-all | bytes 262144 | tf_op jit(solution)/shard_map/all_to_all | solution.py:31
  91.3 10.8 %all_to_all.62.parts_ref = f32[8,16,128]{2,1,0:T(8,128)S(1)} all-to-all(f32[8,16,128]{2,1,0:T(8,128)S(1)} %shard_map.91), channel_id=1, replica_groups=mesh['z'=8,'yh'=2,'yl'=2,'x'=4,'c'=2] {'z'}, dimensions={0} | all-to-all | bytes 131072 | tf_op jit(solution)/shard_map/all_to_all | solution.py:31
  103.3 11.3 %all_to_all.63.parts_ref = f32[32,8,128]{2,1,0:T(8,128)S(1)} all-to-all(f32[32,8,128]{2,1,0:T(8,128)S(1)} %shard_map.92), channel_id=1, replica_groups=mesh['z'=8,'yh'=2,'yl'=2,'x'=4,'c'=2] {'yh','yl','x','c'}, dimensions={0} | all-to-all | bytes 262144 | tf_op jit(solution)/shard_map/all_to_all | solution.py:31
  116.1 3.4 %all-to-all-start.6 = ((f32[8,16,128]{2,1,0:T(8,128)}), f32[8,16,128]{2,1,0:T(8,128)S(1)}, u32[]{:S(2)}, u32[]{:S(2)}) async-start(f32[8,16,128]{2,1,0:T(8,128)} %shard_map.93), calls=%async_computation.6 | async-start | bytes 131072 | tf_op jit(solution)/shard_map/all_to_all | solution.py:31
  119.5 7.1 %shard_map.94 = (bf16[1024,384]{1,0:T(8,128)(2,1)S(1)}, bf16[384,1024]{1,0:T(8,128)(2,1)S(1)}, bf16[1024,2048]{1,0:T(8,128)(2,1)}, f32[8,128]{1,0:T(8,128)S(1)}) custom-call(f32[1024,384]{1,0:T(8,128)} %all-gather.6.cloned.1.call-done.y_ref, bf16[384,2048]{1,0:T(8,128)(2,1)} %constant_dynamic-slice_fusion.2.v_ref), custom_call_target="tpu_custom_call" | custom-call | flops 1610612736 | bytes 8388608 | tf_op jit(solution)/shard_map/pallas_call | solution.py:456
  128.5 7.5 %shard_map.95 = f32[32,24,128]{2,1,0:T(8,128)S(1)} custom-call(f32[8,16,128]{2,1,0:T(8,128)S(1)} %all-to-all-done.6.parts_ref.col_parts_ref, f32[8,128]{1,0:T(8,128)S(1)} %get-tuple-element.53.exps_ref, f32[1024,2048]{1,0:T(8,128)} %copy-done.1, bf16[1024,2048]{1,0:T(8,128)(2,1)} %get-tuple-element.54.scores_ref), custom_call_target="tpu_custom_call" | custom-call | flops 8388608 | bytes 12582912 | tf_op jit(solution)/shard_map/pallas_call | solution.py:481
  136.6 13.9 %all_to_all.64.row_parts_ref = f32[32,24,128]{2,1,0:T(8,128)S(1)} all-to-all(f32[32,24,128]{2,1,0:T(8,128)S(1)} %shard_map.95), channel_id=1, replica_groups=mesh['z'=8,'yh'=2,'yl'=2,'x'=4,'c'=2] {'yh','yl','x','c'}, dimensions={0} | all-to-all | bytes 786432 | tf_op jit(solution)/shard_map/all_to_all | solution.py:31
  151.4 12.2 %shard_map.96 = (f32[1024,384]{1,0:T(8,128)}, f32[384,2048]{1,0:T(8,128)}, f32[1,2048]{1,0:T(1,128)}) custom-call(f32[32,24,128]{2,1,0:T(8,128)S(1)} %all_to_all.64.row_parts_ref, f32[8,16,128]{2,1,0:T(8,128)S(1)} %copy-done.7, f32[1024,2048]{1,0:T(8,128)S(1)} %copy-done.2, bf16[1024,384]{1,0:T(8,128)(2,1)S(1)} %copy-done.12, ...), custom_call_target="tpu_custom_call" | custom-call | flops 4831838208 | bytes 8388608 | tf_op jit(solution)/shard_map/pallas_call | solution.py:504
  165.2 18.0 %all_to_all.65 = f16[32,32,384]{2,1,0:T(8,128)(2,1)S(1)} all-to-all(f16[32,32,384]{2,1,0:T(8,128)(2,1)S(1)} %bitcast.17), channel_id=1, replica_groups=mesh['z'=8,'yh'=2,'yl'=2,'x'=4,'c'=2] {'yh','yl','x','c'}, dimensions={0} | all-to-all | bytes 1572864 | tf_op jit(solution)/shard_map/all_to_all | solution.py:31
  185.0 5.4 %all-to-all-start.9 = ((bf16[16,32,384]{2,1,0:T(8,128)(2,1)}), bf16[16,32,384]{2,1,0:T(8,128)(2,1)}, u32[]{:S(2)}, u32[]{:S(2)}) async-start(bf16[16,32,384]{2,1,0:T(8,128)(2,1)} %shard_map.97), calls=%async_computation.9 | async-start | bytes 786432 | tf_op jit(solution)/shard_map/all_to_all | solution.py:31
  193.7 3.4 %all-to-all-done.9 = bf16[16,32,384]{2,1,0:T(8,128)(2,1)} async-done(((bf16[16,32,384]{2,1,0:T(8,128)(2,1)}), bf16[16,32,384]{2,1,0:T(8,128)(2,1)}, u32[]{:S(2)}, u32[]{:S(2)}) %all-to-all-start.9) | async-done | bytes 393248 | tf_op jit(solution)/shard_map/all_to_all | solution.py:31
  197.1 2.0 fusion.4
  199.1 7.4 %all-to-all-start.10 = ((f32[16,8,384]{2,1,0:T(8,128)}), f32[16,8,384]{2,1,0:T(8,128)}, u32[]{:S(2)}, u32[]{:S(2)}) async-start(f32[16,8,384]{2,1,0:T(8,128)} %fusion.4), calls=%async_computation.10 | async-start | bytes 393216 | tf_op jit(solution)/shard_map/all_to_all | solution.py:31
  207.8 12.3 %all-to-all-done.10.proj_ref = f32[16,8,384]{2,1,0:T(8,128)} async-done(((f32[16,8,384]{2,1,0:T(8,128)}), f32[16,8,384]{2,1,0:T(8,128)}, u32[]{:S(2)}, u32[]{:S(2)}) %all-to-all-start.10) | async-done | bytes 196640 | tf_op jit(solution)/shard_map/all_to_all | solution.py:31
  220.0 1.8 shard_map.98
  221.8 3.6 %all-to-all-start.11 = ((f32[16,16,384]{2,1,0:T(8,128)}), f32[16,16,384]{2,1,0:T(8,128)S(1)}, u32[]{:S(2)}, u32[]{:S(2)}) async-start(f32[16,16,384]{2,1,0:T(8,128)} %shard_map.98), calls=%async_computation.11 | async-start | bytes 786432 | tf_op jit(solution)/shard_map/all_to_all | solution.py:31
  225.4 1.8 constant_dynamic-slice_fusion.1
  227.2 3.3 %collective-permute-start.2 = (f32[24,2048]{1,0:T(8,128)}, f32[24,2048]{1,0:T(8,128)}, u32[]{:S(2)}, u32[]{:S(2)}) collective-permute-start(f32[24,2048]{1,0:T(8,128)} %get-tuple-element.70), channel_id=1, source_target_pairs={{0,16},{16,0},{1,17},{17,1},{2,18},{18,2},{3,19},{19,3},{4,20},{20... | collective-permute-start | bytes 589832 | tf_op jit(solution)/shard_map/ppermute | solution.py:62
  230.5 6.6 %collective-permute-done.2 = f32[24,2048]{1,0:T(8,128)} collective-permute-done((f32[24,2048]{1,0:T(8,128)}, f32[24,2048]{1,0:T(8,128)}, u32[]{:S(2)}, u32[]{:S(2)}) %collective-permute-start.2) | collective-permute-done | bytes 196640 | tf_op jit(solution)/shard_map/ppermute | solution.py:62
  237.1 2.0 maximum_select_fusion.dproto_ref
  239.1 2.3 all-to-all-done.11.parts_ref
  241.4 2.0 shard_map.99
  (64 shorter events, 24.6 us)
Async XLA Ops:
  7.2 30.3 %copy-start = (bf16[384,4096]{1,0:T(8,128)(2,1)S(1)}, bf16[384,4096]{1,0:T(8,128)(2,1)}, u32[]{:S(2)}) copy-start(bf16[384,4096]{1,0:T(8,128)(2,1)} %param.10) | copy-start | bytes 9437188
  7.2 45.5 %all-gather.4.cloned.1.call-start = ((), (), s32[]{:S(2)}) async-start(), calls=%async_computation.13 | async-start | bytes 1671168 | tf_op jit(solution)/shard_map/all_gather | solution.py:558
  10.0 17.7 %all-to-all-start = ((bf16[8,128,384]{2,1,0:T(8,128)(2,1)}), bf16[8,128,384]{2,1,0:T(8,128)(2,1)}, u32[]{:S(2)}, u32[]{:S(2)}) async-start(bf16[8,128,384]{2,1,0:T(8,128)(2,1)} %get-tuple-element.38), calls=%async_computation | async-start | bytes 1572864 | tf_op jit(solution)/shard_map/all_to_all | solution.py:31
  16.4 1.3 collective-permute-start
  29.2 1.3 collective-permute-start.1
  31.5 21.1 %all-to-all-start.1 = ((bf16[32,32,384]{2,1,0:T(8,128)(2,1)}), bf16[32,32,384]{2,1,0:T(8,128)(2,1)}, u32[]{:S(2)}, u32[]{:S(2)}) async-start(bf16[32,32,384]{2,1,0:T(8,128)(2,1)} %shard_map.86), calls=%async_computation.1 | async-start | bytes 1572864 | tf_op jit(solution)/shard_map/all_to_all | solution.py:31
  37.4 78.7 %all-gather.6.cloned.1.call-start = ((), (), s32[]{:S(2)}) async-start(), calls=%async_computation.14 | async-start | bytes 1622016 | tf_op jit(solution)/shard_map/all_gather | solution.py:573
  37.5 1.9 copy-start.3
  41.8 1.5 copy-start.8
  41.8 1.7 copy-start.10
  41.8 10.9 %copy-start.5 = (bf16[32,2048]{1,0:T(8,128)(2,1)S(1)}, bf16[32,2048]{1,0:T(8,128)(2,1)}, u32[]{:S(2)}) copy-start(bf16[32,2048]{1,0:T(8,128)(2,1)} %hidden_ref.3) | copy-start | bytes 393220
  55.0 108.7 %all-gather.8.cloned.1.call-start = ((), (), s32[]{:S(2)}) async-start(), calls=%async_computation.15 | async-start | bytes 2228224 | tf_op jit(solution)/shard_map/all_gather | solution.py:574
  59.9 54.7 %copy-start.1 = (f32[1024,2048]{1,0:T(8,128)}, f32[1024,2048]{1,0:T(8,128)S(1)}, u32[]{:S(2)}) copy-start(f32[1024,2048]{1,0:T(8,128)S(1)} %get-tuple-element.48.exp_ref) | copy-start | bytes 25165828
  116.1 12.3 %all-to-all-start.6 = ((f32[8,16,128]{2,1,0:T(8,128)}), f32[8,16,128]{2,1,0:T(8,128)S(1)}, u32[]{:S(2)}, u32[]{:S(2)}) async-start(f32[8,16,128]{2,1,0:T(8,128)} %shard_map.93), calls=%async_computation.6 | async-start | bytes 131072 | tf_op jit(solution)/shard_map/all_to_all | solution.py:31
  119.5 105.9 %reduce-scatter.2.cloned.1.call-start = ((), (), s32[]{:S(2)}) async-start(), calls=%async_computation.16 | async-start | bytes 3538944 | tf_op jit(solution)/shard_map/reduce_scatter | solution.py:594
  126.7 0.9 copy-start.11
  127.6 0.9 copy-start.13
  128.4 22.1 %copy-start.2 = (f32[1024,2048]{1,0:T(8,128)S(1)}, f32[1024,2048]{1,0:T(8,128)}, u32[]{:S(2)}) copy-start(f32[1024,2048]{1,0:T(8,128)} %copy-done.1) | copy-start | bytes 25165828
  128.4 22.1 %copy-start.4 = (bf16[384,2048]{1,0:T(8,128)(2,1)S(1)}, bf16[384,2048]{1,0:T(8,128)(2,1)}, u32[]{:S(2)}) copy-start(bf16[384,2048]{1,0:T(8,128)(2,1)} %constant_dynamic-slice_fusion.2.v_ref) | copy-start | bytes 4718596
  128.4 22.1 %copy-start.9 = (f32[1024,384]{1,0:T(8,128)S(1)}, f32[1024,384]{1,0:T(8,128)}, u32[]{:S(2)}) copy-start(f32[1024,384]{1,0:T(8,128)} %all-gather.6.cloned.1.call-done.y_ref) | copy-start | bytes 4718596
  128.5 22.1 %copy-start.12 = (bf16[1024,384]{1,0:T(8,128)(2,1)S(1)}, bf16[1024,384]{1,0:T(8,128)(2,1)}, u32[]{:S(2)}) copy-start(bf16[1024,384]{1,0:T(8,128)(2,1)} %copy-done.11) | copy-start | bytes 2359300
  128.5 22.1 %copy-start.14 = (bf16[384,1024]{1,0:T(8,128)(2,1)S(1)}, bf16[384,1024]{1,0:T(8,128)(2,1)}, u32[]{:S(2)}) copy-start(bf16[384,1024]{1,0:T(8,128)(2,1)} %copy-done.13) | copy-start | bytes 2359300
  136.0 0.6 copy-start.6
  150.5 0.8 copy-start.7
  185.0 12.1 %all-to-all-start.9 = ((bf16[16,32,384]{2,1,0:T(8,128)(2,1)}), bf16[16,32,384]{2,1,0:T(8,128)(2,1)}, u32[]{:S(2)}, u32[]{:S(2)}) async-start(bf16[16,32,384]{2,1,0:T(8,128)(2,1)} %shard_map.97), calls=%async_computation.9 | async-start | bytes 786432 | tf_op jit(solution)/shard_map/all_to_all | solution.py:31
  199.1 21.0 %all-to-all-start.10 = ((f32[16,8,384]{2,1,0:T(8,128)}), f32[16,8,384]{2,1,0:T(8,128)}, u32[]{:S(2)}, u32[]{:S(2)}) async-start(f32[16,8,384]{2,1,0:T(8,128)} %fusion.4), calls=%async_computation.10 | async-start | bytes 393216 | tf_op jit(solution)/shard_map/all_to_all | solution.py:31
  221.8 19.6 %all-to-all-start.11 = ((f32[16,16,384]{2,1,0:T(8,128)}), f32[16,16,384]{2,1,0:T(8,128)S(1)}, u32[]{:S(2)}, u32[]{:S(2)}) async-start(f32[16,16,384]{2,1,0:T(8,128)} %shard_map.98), calls=%async_computation.11 | async-start | bytes 786432 | tf_op jit(solution)/shard_map/all_to_all | solution.py:31
  227.2 9.9 %collective-permute-start.2 = (f32[24,2048]{1,0:T(8,128)}, f32[24,2048]{1,0:T(8,128)}, u32[]{:S(2)}, u32[]{:S(2)}) collective-permute-start(f32[24,2048]{1,0:T(8,128)} %get-tuple-element.70), channel_id=1, source_target_pairs={{0,16},{16,0},{1,17},{17,1},{2,18},{18,2},{3,19},{19,3},{4,20},{20... | collective-permute-start | bytes 589832 | tf_op jit(solution)/shard_map/ppermute | solution.py:62
Sparse Core Ops, SparseCore 0:
  9.9 42.7 all-gather.3
  55.2 49.4 all-gather.5
  106.6 35.7 all-gather.7
  163.8 45.4 reduce-scatter.1

commit v8 on v6

--- a/solution.py
+++ b/solution.py
@@ -15,6 +15,7 @@
 LANES = 128
 ROWS_BLOCK = 256
 TALL_BLOCK = 512
+GRAD_BLOCK = 1024
 DEPTH_BLOCK = 1024
 CHUNK = 512
 MIB = 1024 * 1024
@@ -55,16 +56,11 @@
 
 
 def swap(block):
-    side, count = lax.axis_index("yh"), lax.axis_size("yh")
-    rows = block.shape[0] // count
+    side = lax.axis_index("yh")
+    rows = block.shape[0] // lax.axis_size("yh")
     kept = lax.dynamic_slice_in_dim(block, side * rows, rows, 0)
     sent = lax.dynamic_slice_in_dim(block, (1 - side) * rows, rows, 0)
-    got = lax.ppermute(sent, "yh", [(0, 1), (1, 0)])
-    return jnp.where(
-        side == 0,
-        jnp.concatenate([kept, got], axis=1),
-        jnp.concatenate([got, kept], axis=1),
-    )
+    return kept, lax.ppermute(sent, "yh", [(0, 1), (1, 0)])
 
 
 def lane_rows(row):
@@ -256,8 +252,8 @@
 
     groups = width // LANES
     col = one_row(scale[pl.ds(pl.multiple_of(step * groups, groups), groups), :])
-    for start in range(0, rows, ROWS_BLOCK):
-        here = slice(start, start + ROWS_BLOCK)
+    for start in range(0, rows, GRAD_BLOCK):
+        here = slice(start, start + GRAD_BLOCK)
         scores = jnp.dot(z_ref[here, :], v_ref[...], preferred_element_type=jnp.float32)
         prob = jnp.exp(scores * (1.0 / TAU_S))
         for piece in range(0, width, LANES):
@@ -295,10 +291,12 @@
     repeat_out(out_ref, jnp.concatenate([proj] + pieces, axis=0))
 
 
-def finish_kernel(parts_ref, dproto_ref, v_ref, norm_ref, proj_ref, grad_ref, loss_ref):
+def finish_kernel(
+    side_ref, parts_ref, kept_ref, got_ref, v_ref, norm_ref, proj_ref, grad_ref, loss_ref
+):
     copies, height, bot = parts_ref.shape
     own = proj_ref.shape[0] // copies
-    width = dproto_ref.shape[1] // 2
+    width = kept_ref.shape[1]
     rows = -(-(width + LANES) // bot)
     for i in range(copies):
         proj_ref[i * own : (i + 1) * own, :] = parts_ref[i, 0:own, :]
@@ -309,10 +307,20 @@
             block = block + parts_ref[i, own:height, :]
         lines.append(jnp.concatenate([block[i : i + 1] for i in range(rows)], axis=1))
     loss_ref[...] = lines[0][:, width : width + LANES]
-    for side in range(2):
-        cols = slice(side * width, (side + 1) * width)
-        dots = lines[side][:, 0:width]
-        grad_ref[:, cols] = (dproto_ref[:, cols] - v_ref[:, cols] * dots) / norm_ref[:, cols]
+
+    def write(halves):
+        for side in range(2):
+            cols = slice(side * width, (side + 1) * width)
+            dots = lines[side][:, 0:width]
+            grad_ref[:, cols] = (halves[side][...] - v_ref[:, cols] * dots) / norm_ref[:, cols]
+
+    @pl.when(side_ref[0] == 0)
+    def _():
+        write((kept_ref, got_ref))
+
+    @pl.when(side_ref[0] != 0)
+    def _():
+        write((got_ref, kept_ref))
 
 
 def params(mib):
@@ -502,7 +510,7 @@
             pltpu.VMEM((rows, CHUNK), jnp.bfloat16),
             pltpu.VMEM((rows, bot), jnp.float32),
         ],
-        compiler_params=params(20),
+        compiler_params=params(28),
         cost_estimate=cost(6 * z.size * width, exp.size * 4, exp.size),
     )(row_parts, col_parts, exp, z, zt, v, y)
 
@@ -537,7 +545,9 @@
         lax.dynamic_slice_in_dim(proto_teacher, first, half, 1), proto_student
     )
     v_s = lax.dynamic_slice_in_dim(v_all, first, half, 1)
-    z_t, v_t, v_s = lax.optimization_barrier((z_t, v_t, v_s))
+    last = bot // lax.axis_size(DP)
+    v_last = lax.dynamic_slice_in_dim(v_all, lax.axis_index(DP) * last, last, 0).astype(jnp.float32)
+    z_t, v_t, v_s, v_last = lax.optimization_barrier((z_t, v_t, v_s, v_last))
     y_s = project(hid_student, gathered)
     z_t, y_s, hid_student = lax.optimization_barrier((z_t, y_s, hid_student))
     wide_s = lax.all_gather(y_s, PLANE, axis=0, tiled=True)
@@ -557,14 +567,12 @@
         sums, col_parts, teacher_exp, z_s, z_s_t, v_s, wide_s
     )
 
-    dy_part, hid_group, v_all, sums = lax.optimization_barrier((dy_part, hid_group, v_all, sums))
+    dy_part, hid_group, sums = lax.optimization_barrier((dy_part, hid_group, sums))
     row_mass, expsum, cross = jnp.split(jnp.sum(sums, axis=0), 3, axis=0)
     row_count = y_s.shape[0] * lax.axis_size(DP + SHARD)
     loss_part = jnp.sum(jnp.log(expsum) - cross / row_mass / TAU_S) / row_count
     dproto = lax.psum_scatter(dproto_part, "z", scatter_dimension=0, tiled=True)
-    last = dproto.shape[0] // lax.axis_size("yh")
-    v_last = lax.dynamic_slice_in_dim(v_all, lax.axis_index(DP) * last, last, 0).astype(jnp.float32)
-    swapped = swap(dproto)
+    kept, got = swap(dproto)
 
     parts = (dy_part * WIRE_SCALE).astype(jnp.float16).reshape((planes,) + y_s.shape)
     tangent = jnp.sum(exchange(parts, PLANE).astype(jnp.float32), axis=0) * (1.0 / WIRE_SCALE)
@@ -585,9 +593,18 @@
     )(proj_parts, hbm(dots), loss_part.reshape(1, 1))
     grad_proj, grad_proto, loss = pl.pallas_call(
         finish_kernel,
+        in_specs=[pl.BlockSpec(memory_space=pltpu.SMEM)]
+        + [pl.BlockSpec(memory_space=pltpu.VMEM)] * 5,
         out_shape=[f32(depth, bot), f32(last, 2 * half), f32(1, LANES)],
         compiler_params=pltpu.CompilerParams(vmem_limit_bytes=12 * MIB),
-    )(exchange(collected, DP), hbm(swapped), hbm(v_last), hbm(norm_all))
+    )(
+        lax.axis_index("yh").reshape(1),
+        exchange(collected, DP),
+        hbm(kept),
+        hbm(got),
+        hbm(v_last),
+        hbm(norm_all),
+    )
     return (loss[0, 0], grad_proj, grad_proto)
 
 

time: 247 us -> 245 us (level)
  waiting for transfers between devices: 45.6 us -> 49.8 us
    all_to_all x5, waiting for transfers between devices: 36.4 us -> 45.8 us  [exchange(): return lax.all_to_all(blocks, axes, 0, 0, tiled=True)]
    ppermute x1, waiting for transfers between devices: 4.93 us -> 0.01 us  [swap(): return (kept, lax.ppermute(sent, 'yh', [(0, 1), (1, 0)]))]
    unnamed x20 -> x18, local copies, waits for them, and re-layouts: 5.16 us -> 1.98 us
  transfers between devices with their start and end apart: 12 -> 12, of which waited for: 9 -> 8; matrix products, arithmetic and copies ran while one was open for 6% -> 5% of each run, Pallas kernels for 16% -> 15%
where the time goes in v8:
time: 245 us; the launch traced here: 244 us
  blocking collectives  93.8 us (38%)
  waiting for transfers between devices  49.8 us (20%)
  Pallas kernels  41.6 us (17%)
  starting transfers between devices  28.9 us (12%)
  between operations  14.7 us (6%)
  local copies, waits for them, and re-layouts  8.56 us (3%)
  matrix products  3.37 us (1%)
  other arithmetic  3.11 us (1%)
    all_to_all x7, blocking collectives, exchange(): return lax.all_to_all(blocks, axes, 0, 0, tiled=True)  93.8 us
    all_to_all x5, waiting for transfers between devices, exchange(): return lax.all_to_all(blocks, axes, 0, 0, tiled=True)  45.8 us
    all_to_all x5, starting transfers between devices, exchange(): return lax.all_to_all(blocks, axes, 0, 0, tiled=True)  25.4 us
    pallas_call x1, Pallas kernels, gradient_pass(): pl.pallas_call(gradient_kernel, grid=(width // CHUNK,), in_specs=[whole(r...  10.4 us
    pallas_call x1, Pallas kernels, student_pass(): pl.pallas_call(student_kernel, grid=(rows // ROWS_BLOCK,), in_specs=[whol...  9.45 us
  transfers between devices with their start and end apart: 12, of which 8 were waited for; matrix products, arithmetic and copies ran while one was open for 5% of the time, Pallas kernels for 15%

profile of v8, /device:TPU:2, one launch (start us, length us, event | category | flops | bytes accessed | tf_op | source)
XLA Modules:
  0.0 243.8 jit_solution(6722313958091560808)
XLA Ops:
  7.9 2.1 shard_map.85
  10.0 6.4 %all-to-all-start = ((bf16[8,128,384]{2,1,0:T(8,128)(2,1)}), bf16[8,128,384]{2,1,0:T(8,128)(2,1)}, u32[]{:S(2)}, u32[]{:S(2)}) async-start(bf16[8,128,384]{2,1,0:T(8,128)(2,1)} %get-tuple-element.37), calls=%async_computation | async-start | bytes 1572864 | tf_op jit(solution)/shard_map/all_to_all | solution.py:32
  17.7 10.1 %all-to-all-done = bf16[8,128,384]{2,1,0:T(8,128)(2,1)} async-done(((bf16[8,128,384]{2,1,0:T(8,128)(2,1)}), bf16[8,128,384]{2,1,0:T(8,128)(2,1)}, u32[]{:S(2)}, u32[]{:S(2)}) %all-to-all-start) | async-done | bytes 786464 | tf_op jit(solution)/shard_map/all_to_all | solution.py:32
  31.5 5.9 %all-to-all-start.1 = ((bf16[32,32,384]{2,1,0:T(8,128)(2,1)}), bf16[32,32,384]{2,1,0:T(8,128)(2,1)}, u32[]{:S(2)}, u32[]{:S(2)}) async-start(bf16[32,32,384]{2,1,0:T(8,128)(2,1)} %shard_map.86), calls=%async_computation.1 | async-start | bytes 1572864 | tf_op jit(solution)/shard_map/all_to_all | solution.py:32
  37.6 1.8 copy-done.4
  39.4 2.4 shard_map.87
  44.2 8.4 %all-to-all-done.1 = bf16[32,32,384]{2,1,0:T(8,128)(2,1)} async-done(((bf16[32,32,384]{2,1,0:T(8,128)(2,1)}), bf16[32,32,384]{2,1,0:T(8,128)(2,1)}, u32[]{:S(2)}, u32[]{:S(2)}) %all-to-all-start.1) | async-done | bytes 786464 | tf_op jit(solution)/shard_map/all_to_all | solution.py:32
  52.7 2.2 shard_map.88.y_ref
  55.8 4.2 %shard_map.89 = (f32[1024,2048]{1,0:T(8,128)S(1)}, f32[8,16,128]{2,1,0:T(8,128)S(1)}) custom-call(bf16[1024,384]{1,0:T(8,128)(2,1)} %bitcast.3.z_ref, bf16[384,2048]{1,0:T(8,128)(2,1)} %copy-done.8), custom_call_target="tpu_custom_call" | custom-call | flops 1610612736 | bytes 8388608 | tf_op jit(solution)/shard_map/pallas_call | solution.py:407
  59.9 17.3 %all_to_all.60.parts_ref = f32[8,16,128]{2,1,0:T(8,128)S(1)} all-to-all(f32[8,16,128]{2,1,0:T(8,128)S(1)} %get-tuple-element.46), channel_id=1, replica_groups=mesh['z'=8,'yh'=2,'yl'=2,'x'=4,'c'=2] {'z'}, dimensions={0} | all-to-all | bytes 131072 | tf_op jit(solution)/shard_map/all_to_all | solution.py:32
  78.4 12.0 %all_to_all.61.parts_ref = f32[32,8,128]{2,1,0:T(8,128)S(1)} all-to-all(f32[32,8,128]{2,1,0:T(8,128)S(1)} %shard_map.90), channel_id=1, replica_groups=mesh['z'=8,'yh'=2,'yl'=2,'x'=4,'c'=2] {'yh','yl','x','c'}, dimensions={0} | all-to-all | bytes 262144 | tf_op jit(solution)/shard_map/all_to_all | solution.py:32
  91.4 10.8 %all_to_all.62.parts_ref = f32[8,16,128]{2,1,0:T(8,128)S(1)} all-to-all(f32[8,16,128]{2,1,0:T(8,128)S(1)} %shard_map.91), channel_id=1, replica_groups=mesh['z'=8,'yh'=2,'yl'=2,'x'=4,'c'=2] {'z'}, dimensions={0} | all-to-all | bytes 131072 | tf_op jit(solution)/shard_map/all_to_all | solution.py:32
  103.3 11.3 %all_to_all.63.parts_ref = f32[32,8,128]{2,1,0:T(8,128)S(1)} all-to-all(f32[32,8,128]{2,1,0:T(8,128)S(1)} %shard_map.92), channel_id=1, replica_groups=mesh['z'=8,'yh'=2,'yl'=2,'x'=4,'c'=2] {'yh','yl','x','c'}, dimensions={0} | all-to-all | bytes 262144 | tf_op jit(solution)/shard_map/all_to_all | solution.py:32
  115.6 10.8 %all_to_all.64.parts_ref.col_parts_ref = f32[8,16,128]{2,1,0:T(8,128)S(1)} all-to-all(f32[8,16,128]{2,1,0:T(8,128)S(1)} %shard_map.93), channel_id=1, replica_groups=mesh['z'=8,'yh'=2,'yl'=2,'x'=4,'c'=2] {'z'}, dimensions={0} | all-to-all | bytes 131072 | tf_op jit(solution)/shard_map/all_to_all | solution.py:32
  126.3 9.5 %shard_map.94 = (f32[32,24,128]{2,1,0:T(8,128)S(1)}, bf16[1024,384]{1,0:T(8,128)(2,1)S(1)}, bf16[384,1024]{1,0:T(8,128)(2,1)S(1)}) custom-call(f32[8,16,128]{2,1,0:T(8,128)S(1)} %all_to_all.64.parts_ref.col_parts_ref, f32[1024,2048]{1,0:T(8,128)} %copy-done.1, f32[1024,384]{1,0:T(8,128)} %all-gather.6.cloned.1.call-done.y_ref, ...), custom_call_target="tpu_custom_call" | custom-call | flops 1610612736 | bytes 8388608 | tf_op jit(solution)/shard_map/pallas_call | solution.py:453
  135.8 13.7 %all_to_all.65.row_parts_ref = f32[32,24,128]{2,1,0:T(8,128)S(1)} all-to-all(f32[32,24,128]{2,1,0:T(8,128)S(1)} %get-tuple-element.52), channel_id=1, replica_groups=mesh['z'=8,'yh'=2,'yl'=2,'x'=4,'c'=2] {'yh','yl','x','c'}, dimensions={0} | all-to-all | bytes 786432 | tf_op jit(solution)/shard_map/all_to_all | solution.py:32
  149.6 10.4 %shard_map.95 = (f32[1024,384]{1,0:T(8,128)}, f32[384,2048]{1,0:T(8,128)}, f32[1,2048]{1,0:T(1,128)}) custom-call(f32[32,24,128]{2,1,0:T(8,128)S(1)} %all_to_all.65.row_parts_ref, f32[8,16,128]{2,1,0:T(8,128)S(1)} %all_to_all.64.parts_ref.col_parts_ref, f32[1024,2048]{1,0:T(8,128)S(1)} %copy-done.2, bf16[1024,384]{1,0:T(8,128)(2,1)S(1)} %get-tuple-element.53.z_ref, ...), custom_call_target="tpu_custom_call" | custom-call | flops 4831838208 | bytes 8388608 | tf_op jit(solution)/shard_map/pallas_call | solution.py:484
  161.6 18.0 %all_to_all.66 = f16[32,32,384]{2,1,0:T(8,128)(2,1)S(1)} all-to-all(f16[32,32,384]{2,1,0:T(8,128)(2,1)S(1)} %bitcast.18), channel_id=1, replica_groups=mesh['z'=8,'yh'=2,'yl'=2,'x'=4,'c'=2] {'yh','yl','x','c'}, dimensions={0} | all-to-all | bytes 1572864 | tf_op jit(solution)/shard_map/all_to_all | solution.py:32
  179.7 1.7 shard_map.96
  181.4 5.4 %all-to-all-start.9 = ((bf16[16,32,384]{2,1,0:T(8,128)(2,1)}), bf16[16,32,384]{2,1,0:T(8,128)(2,1)}, u32[]{:S(2)}, u32[]{:S(2)}) async-start(bf16[16,32,384]{2,1,0:T(8,128)(2,1)} %shard_map.96), calls=%async_computation.9 | async-start | bytes 786432 | tf_op jit(solution)/shard_map/all_to_all | solution.py:32
  186.8 1.6 dynamic-slice_bitcast_fusion
  188.4 1.6 copy.10
  190.0 3.4 %all-to-all-done.9 = bf16[16,32,384]{2,1,0:T(8,128)(2,1)} async-done(((bf16[16,32,384]{2,1,0:T(8,128)(2,1)}), bf16[16,32,384]{2,1,0:T(8,128)(2,1)}, u32[]{:S(2)}, u32[]{:S(2)}) %all-to-all-start.9) | async-done | bytes 393248 | tf_op jit(solution)/shard_map/all_to_all | solution.py:32
  193.4 2.0 fusion.4
  195.4 4.2 %all-to-all-start.10 = ((f32[16,8,384]{2,1,0:T(8,128)}), f32[16,8,384]{2,1,0:T(8,128)}, u32[]{:S(2)}, u32[]{:S(2)}) async-start(f32[16,8,384]{2,1,0:T(8,128)} %fusion.4), calls=%async_computation.10 | async-start | bytes 393216 | tf_op jit(solution)/shard_map/all_to_all | solution.py:32
  200.9 12.6 %all-to-all-done.10.proj_ref = f32[16,8,384]{2,1,0:T(8,128)} async-done(((f32[16,8,384]{2,1,0:T(8,128)}), f32[16,8,384]{2,1,0:T(8,128)}, u32[]{:S(2)}, u32[]{:S(2)}) %all-to-all-start.10) | async-done | bytes 196640 | tf_op jit(solution)/shard_map/all_to_all | solution.py:32
  213.5 1.8 shard_map.97
  215.2 3.6 %all-to-all-start.11 = ((f32[16,16,384]{2,1,0:T(8,128)}), f32[16,16,384]{2,1,0:T(8,128)S(1)}, u32[]{:S(2)}, u32[]{:S(2)}) async-start(f32[16,16,384]{2,1,0:T(8,128)} %shard_map.97), calls=%async_computation.11 | async-start | bytes 786432 | tf_op jit(solution)/shard_map/all_to_all | solution.py:32
  218.8 1.8 constant_dynamic-slice_fusion
  220.6 3.3 %collective-permute-start.2 = (f32[24,2048]{1,0:T(8,128)}, f32[24,2048]{1,0:T(8,128)}, u32[]{:S(2)}, u32[]{:S(2)}) collective-permute-start(f32[24,2048]{1,0:T(8,128)} %get-tuple-element.67), channel_id=1, source_target_pairs={{0,16},{16,0},{1,17},{17,1},{2,18},{18,2},{3,19},{19,3},{4,20},{20... | collective-permute-start | bytes 589832 | tf_op jit(solution)/shard_map/ppermute | solution.py:63
  223.9 11.3 %all-to-all-done.11.parts_ref = f32[16,16,384]{2,1,0:T(8,128)S(1)} async-done(((f32[16,16,384]{2,1,0:T(8,128)}), f32[16,16,384]{2,1,0:T(8,128)S(1)}, u32[]{:S(2)}, u32[]{:S(2)}) %all-to-all-start.11) | async-done | bytes 393248 | tf_op jit(solution)/shard_map/all_to_all | solution.py:32
  235.2 2.1 shard_map.98
  (49 shorter events, 15.8 us)
Async XLA Ops:
  7.2 30.3 %copy-start = (bf16[384,4096]{1,0:T(8,128)(2,1)S(1)}, bf16[384,4096]{1,0:T(8,128)(2,1)}, u32[]{:S(2)}) copy-start(bf16[384,4096]{1,0:T(8,128)(2,1)} %param.10) | copy-start | bytes 9437188
  7.2 45.5 %all-gather.4.cloned.1.call-start = ((), (), s32[]{:S(2)}) async-start(), calls=%async_computation.13 | async-start | bytes 1671168 | tf_op jit(solution)/shard_map/all_gather | solution.py:538
  10.0 17.7 %all-to-all-start = ((bf16[8,128,384]{2,1,0:T(8,128)(2,1)}), bf16[8,128,384]{2,1,0:T(8,128)(2,1)}, u32[]{:S(2)}, u32[]{:S(2)}) async-start(bf16[8,128,384]{2,1,0:T(8,128)(2,1)} %get-tuple-element.37), calls=%async_computation | async-start | bytes 1572864 | tf_op jit(solution)/shard_map/all_to_all | solution.py:32
  16.4 1.3 collective-permute-start
  29.2 1.3 collective-permute-start.1
  31.5 21.1 %all-to-all-start.1 = ((bf16[32,32,384]{2,1,0:T(8,128)(2,1)}), bf16[32,32,384]{2,1,0:T(8,128)(2,1)}, u32[]{:S(2)}, u32[]{:S(2)}) async-start(bf16[32,32,384]{2,1,0:T(8,128)(2,1)} %shard_map.86), calls=%async_computation.1 | async-start | bytes 1572864 | tf_op jit(solution)/shard_map/all_to_all | solution.py:32
  37.4 78.2 %all-gather.6.cloned.1.call-start = ((), (), s32[]{:S(2)}) async-start(), calls=%async_computation.14 | async-start | bytes 1622016 | tf_op jit(solution)/shard_map/all_gather | solution.py:553
  37.4 1.9 copy-start.4
  41.8 1.5 copy-start.7
  41.8 1.6 copy-start.8
  41.8 10.9 %copy-start.6 = (bf16[32,2048]{1,0:T(8,128)(2,1)S(1)}, bf16[32,2048]{1,0:T(8,128)(2,1)}, u32[]{:S(2)}) copy-start(bf16[32,2048]{1,0:T(8,128)(2,1)} %hidden_ref.3) | copy-start | bytes 393220
  55.0 105.0 %all-gather.8.cloned.1.call-start = ((), (), s32[]{:S(2)}) async-start(), calls=%async_computation.15 | async-start | bytes 2228224 | tf_op jit(solution)/shard_map/all_gather | solution.py:554
  55.7 163.1 %reduce-scatter.2.cloned.1.call-start = ((), (), s32[]{:S(2)}) async-start(), calls=%async_computation.16 | async-start | bytes 3538944 | tf_op jit(solution)/shard_map/reduce_scatter | solution.py:574
  59.9 54.7 %copy-start.1 = (f32[1024,2048]{1,0:T(8,128)}, f32[1024,2048]{1,0:T(8,128)S(1)}, u32[]{:S(2)}) copy-start(f32[1024,2048]{1,0:T(8,128)S(1)} %get-tuple-element.47.exp_ref) | copy-start | bytes 25165828
  126.3 23.2 %copy-start.2 = (f32[1024,2048]{1,0:T(8,128)S(1)}, f32[1024,2048]{1,0:T(8,128)}, u32[]{:S(2)}) copy-start(f32[1024,2048]{1,0:T(8,128)} %copy-done.1) | copy-start | bytes 25165828
  126.3 23.2 %copy-start.3 = (bf16[384,2048]{1,0:T(8,128)(2,1)S(1)}, bf16[384,2048]{1,0:T(8,128)(2,1)}, u32[]{:S(2)}) copy-start(bf16[384,2048]{1,0:T(8,128)(2,1)} %constant_dynamic-slice_fusion.2.v_ref) | copy-start | bytes 4718596
  126.3 23.2 %copy-start.5 = (f32[1024,384]{1,0:T(8,128)S(1)}, f32[1024,384]{1,0:T(8,128)}, u32[]{:S(2)}) copy-start(f32[1024,384]{1,0:T(8,128)} %all-gather.6.cloned.1.call-done.y_ref) | copy-start | bytes 4718596
  181.4 12.1 %all-to-all-start.9 = ((bf16[16,32,384]{2,1,0:T(8,128)(2,1)}), bf16[16,32,384]{2,1,0:T(8,128)(2,1)}, u32[]{:S(2)}, u32[]{:S(2)}) async-start(bf16[16,32,384]{2,1,0:T(8,128)(2,1)} %shard_map.96), calls=%async_computation.9 | async-start | bytes 786432 | tf_op jit(solution)/shard_map/all_to_all | solution.py:32
  195.4 18.1 %all-to-all-start.10 = ((f32[16,8,384]{2,1,0:T(8,128)}), f32[16,8,384]{2,1,0:T(8,128)}, u32[]{:S(2)}, u32[]{:S(2)}) async-start(f32[16,8,384]{2,1,0:T(8,128)} %fusion.4), calls=%async_computation.10 | async-start | bytes 393216 | tf_op jit(solution)/shard_map/all_to_all | solution.py:32
  215.2 20.0 %all-to-all-start.11 = ((f32[16,16,384]{2,1,0:T(8,128)}), f32[16,16,384]{2,1,0:T(8,128)S(1)}, u32[]{:S(2)}, u32[]{:S(2)}) async-start(f32[16,16,384]{2,1,0:T(8,128)} %shard_map.97), calls=%async_computation.11 | async-start | bytes 786432 | tf_op jit(solution)/shard_map/all_to_all | solution.py:32
  220.6 14.6 %collective-permute-start.2 = (f32[24,2048]{1,0:T(8,128)}, f32[24,2048]{1,0:T(8,128)}, u32[]{:S(2)}, u32[]{:S(2)}) collective-permute-start(f32[24,2048]{1,0:T(8,128)} %get-tuple-element.67), channel_id=1, source_target_pairs={{0,16},{16,0},{1,17},{17,1},{2,18},{18,2},{3,19},{19,3},{4,20},{20... | collective-permute-start | bytes 589832 | tf_op jit(solution)/shard_map/ppermute | solution.py:63
Sparse Core Ops, SparseCore 0:
  9.9 42.7 all-gather.3
  55.8 49.4 all-gather.5
  107.2 35.8 all-gather.7
  160.1 41.0 reduce-scatter.1

commit v9 on v8

--- a/solution.py
+++ b/solution.py
@@ -278,35 +278,61 @@
             dy_ref[here, :] = part - y * (inner / square)
 
 
-def collect_kernel(proj_ref, dots_ref, loss_ref, out_ref):
-    own, bot = proj_ref.shape[1:]
-    proj = jnp.sum(proj_ref[...], axis=0)
-    dots = dots_ref[...]
-    width = dots.shape[1]
-    rows = -(-(width + LANES) // bot)
-    loss = jnp.broadcast_to(loss_ref[...], (1, rows * bot - width))
-    row = jnp.concatenate([dots, loss], axis=1)
-    pieces = [row[:, i * bot : (i + 1) * bot] for i in range(rows)]
-    pieces.append(jnp.zeros((out_ref.shape[1] - own - rows, bot), jnp.float32))
-    repeat_out(out_ref, jnp.concatenate([proj] + pieces, axis=0))
+def rows_kernel(hidden_ref, dy_ref, dots_ref, out_ref):
+    copies, height = out_ref.shape[:2]
+    product = lax.dot_general(
+        hidden_ref[...], dy_ref[...], ROW_DIMS, preferred_element_type=jnp.float32
+    )
+    own, bot = product.shape[0] // copies, product.shape[1]
+    for i in range(copies):
+        for piece in range(0, bot, LANES):
+            row = piece // LANES * own
+            out_ref[i, row : row + own, :] = product[
+                i * own : (i + 1) * own, piece : piece + LANES
+            ]
+        dots = dots_ref[:, i * LANES : (i + 1) * LANES]
+        tail = height - own * bot // LANES
+        out_ref[i, height - tail : height, :] = jnp.broadcast_to(dots, (tail, LANES))
+
+
+def collect_kernel(parts_ref, loss_ref, out_ref):
+    copies, height = parts_ref.shape[:2]
+    sides = []
+    for side in range(2):
+        block = parts_ref[side]
+        for i in range(2 + side, copies, 2):
+            block = block + parts_ref[i]
+        sides.append(block)
+    head = height - 8
+    loss = jnp.broadcast_to(loss_ref[...], (6, LANES))
+    tail = [sides[0][head : head + 1], sides[1][head : head + 1], loss]
+    repeat_out(
+        out_ref, jnp.concatenate([sides[0][0:head] + sides[1][0:head]] + tail, axis=0)
+    )
 
 
 def finish_kernel(
     side_ref, parts_ref, kept_ref, got_ref, v_ref, norm_ref, proj_ref, grad_ref, loss_ref
 ):
-    copies, height, bot = parts_ref.shape
-    own = proj_ref.shape[0] // copies
-    width = kept_ref.shape[1]
-    rows = -(-(width + LANES) // bot)
+    copies, height = parts_ref.shape[:2]
+    rows, bot = proj_ref.shape
+    own, width, head = rows // copies, kept_ref.shape[1], height - 8
     for i in range(copies):
-        proj_ref[i * own : (i + 1) * own, :] = parts_ref[i, 0:own, :]
-    lines = []
-    for side in range(2):
-        block = parts_ref[side, own:height, :]
-        for i in range(2 + side, copies, 2):
-            block = block + parts_ref[i, own:height, :]
-        lines.append(jnp.concatenate([block[i : i + 1] for i in range(rows)], axis=1))
-    loss_ref[...] = lines[0][:, width : width + LANES]
+        for piece in range(0, bot, LANES):
+            row = piece // LANES * own
+            proj_ref[i * own : (i + 1) * own, piece : piece + LANES] = parts_ref[
+                i, row : row + own, :
+            ]
+    lines = [
+        jnp.concatenate(
+            [parts_ref[i, head + side : head + side + 1, :] for i in range(copies)], axis=1
+        )
+        for side in range(2)
+    ]
+    loss = parts_ref[0, head + 2 : head + 3, :]
+    for i in range(2, copies, 2):
+        loss = loss + parts_ref[i, head + 2 : head + 3, :]
+    loss_ref[...] = loss
 
     def write(halves):
         for side in range(2):
@@ -452,17 +478,17 @@
     out = (copies, 3 * rows // LANES, LANES)
     return pl.pallas_call(
         student_kernel,
-        grid=(rows // ROWS_BLOCK,),
+        grid=(rows // TALL_BLOCK,),
         in_specs=[
             whole(parts.shape),
-            pl.BlockSpec((ROWS_BLOCK, width), lambda i: (i, 0)),
-            pl.BlockSpec((ROWS_BLOCK, bot), lambda i: (i, 0)),
+            pl.BlockSpec((TALL_BLOCK, width), lambda i: (i, 0)),
+            pl.BlockSpec((TALL_BLOCK, bot), lambda i: (i, 0)),
             whole(v.shape),
         ],
         out_specs=[
             whole(out),
-            pl.BlockSpec((ROWS_BLOCK, bot), lambda i: (i, 0)),
-            pl.BlockSpec((bot, ROWS_BLOCK), lambda i: (0, i)),
+            pl.BlockSpec((TALL_BLOCK, bot), lambda i: (i, 0)),
+            pl.BlockSpec((bot, TALL_BLOCK), lambda i: (0, i)),
         ],
         out_shape=[
             f32(*out),
@@ -473,7 +499,7 @@
             pltpu.VMEM((1, width), jnp.float32),
             pltpu.VMEM((3, rows, LANES), jnp.float32),
         ],
-        compiler_params=params(20),
+        compiler_params=params(28),
         cost_estimate=cost(2 * y.size * width, exp.size * 4, exp.size),
     )(parts, hbm(exp), hbm(y), hbm(v))
 
@@ -572,7 +598,6 @@
     row_count = y_s.shape[0] * lax.axis_size(DP + SHARD)
     loss_part = jnp.sum(jnp.log(expsum) - cross / row_mass / TAU_S) / row_count
     dproto = lax.psum_scatter(dproto_part, "z", scatter_dimension=0, tiled=True)
-    kept, got = swap(dproto)
 
     parts = (dy_part * WIRE_SCALE).astype(jnp.float16).reshape((planes,) + y_s.shape)
     tangent = jnp.sum(exchange(parts, PLANE).astype(jnp.float32), axis=0) * (1.0 / WIRE_SCALE)
@@ -583,14 +608,19 @@
     hid_block = lax.dynamic_slice_in_dim(
         hid_group, lax.axis_index(SHARD) * depth, depth, 1
     )
-    proj_term = lax.dot_general(hid_block, dy_group, ROW_DIMS, preferred_element_type=jnp.float32)
-    proj_parts = exchange(proj_term.reshape(lax.axis_size(DP), -1, bot), DP)
-    height = proj_parts.shape[1] + 8 * -(-(half + LANES) // (8 * bot))
+    copies = lax.axis_size(DP)
+    height = depth // copies * bot // LANES + 8
+    proj_rows = pl.pallas_call(
+        rows_kernel,
+        out_shape=pltpu.HBM((copies, height, LANES), jnp.float32),
+        compiler_params=pltpu.CompilerParams(vmem_limit_bytes=8 * MIB),
+    )(hbm(hid_block), hbm(dy_group), hbm(dots))
     collected = pl.pallas_call(
         collect_kernel,
-        out_shape=pltpu.HBM((proj_parts.shape[0], height, bot), jnp.float32),
+        out_shape=pltpu.HBM((copies, height, LANES), jnp.float32),
         compiler_params=pltpu.CompilerParams(vmem_limit_bytes=8 * MIB),
-    )(proj_parts, hbm(dots), loss_part.reshape(1, 1))
+    )(exchange(proj_rows, DP), loss_part.reshape(1, 1))
+    kept, got = swap(dproto)
     grad_proj, grad_proto, loss = pl.pallas_call(
         finish_kernel,
         in_specs=[pl.BlockSpec(memory_space=pltpu.SMEM)]

time: 245 us -> 242 us (0.988)
    dot_general x2 -> x0, local copies, waits for them, and re-layouts: 3.22 us -> none  [local(): lax.dot_general(hid_block, dy_group, ROW_DIMS, preferred_element_type=jnp...]
    pallas_call x2 -> x3, Pallas kernels: 11.2 us -> 12.3 us  [the longest x1 8.6 us: student_pass(): pl.pallas_call(student_kernel, grid=(rows // TALL_BLOCK,), in_specs=[whol...]
  transfers between devices with their start and end apart: 12 -> 12, of which waited for: 8 -> 8; matrix products, arithmetic and copies ran while one was open for 5% -> 4% of each run, Pallas kernels for 15% -> 16%
where the time goes in v9:
time: 242 us; the launch traced here: 241 us
  blocking collectives  93.8 us (39%)
  waiting for transfers between devices  49.7 us (21%)
  Pallas kernels  42.7 us (18%)
  starting transfers between devices  28.9 us (12%)
  between operations  14.7 us (6%)
  local copies, waits for them, and re-layouts  6.92 us (3%)
  other arithmetic  3.11 us (1%)
    all_to_all x7, blocking collectives, exchange(): return lax.all_to_all(blocks, axes, 0, 0, tiled=True)  93.8 us
    all_to_all x5, waiting for transfers between devices, exchange(): return lax.all_to_all(blocks, axes, 0, 0, tiled=True)  45.7 us
    all_to_all x5, starting transfers between devices, exchange(): return lax.all_to_all(blocks, axes, 0, 0, tiled=True)  25.4 us
    pallas_call x1, Pallas kernels, gradient_pass(): pl.pallas_call(gradient_kernel, grid=(width // CHUNK,), in_specs=[whole(r...  10.4 us
    pallas_call x1, Pallas kernels, student_pass(): pl.pallas_call(student_kernel, grid=(rows // TALL_BLOCK,), in_specs=[whol...  8.6 us
  transfers between devices with their start and end apart: 12, of which 8 were waited for; matrix products, arithmetic and copies ran while one was open for 4% of the time, Pallas kernels for 16%

profile of v9, /device:TPU:2, one launch (start us, length us, event | category | flops | bytes accessed | tf_op | source)
XLA Modules:
  0.0 241.3 jit_solution(9164141896432763288)
XLA Ops:
  7.9 2.1 shard_map.85
  10.0 6.4 %all-to-all-start = ((bf16[8,128,384]{2,1,0:T(8,128)(2,1)}), bf16[8,128,384]{2,1,0:T(8,128)(2,1)}, u32[]{:S(2)}, u32[]{:S(2)}) async-start(bf16[8,128,384]{2,1,0:T(8,128)(2,1)} %get-tuple-element.37), calls=%async_computation | async-start | bytes 1572864 | tf_op jit(solution)/shard_map/all_to_all | solution.py:32
  17.7 10.1 %all-to-all-done = bf16[8,128,384]{2,1,0:T(8,128)(2,1)} async-done(((bf16[8,128,384]{2,1,0:T(8,128)(2,1)}), bf16[8,128,384]{2,1,0:T(8,128)(2,1)}, u32[]{:S(2)}, u32[]{:S(2)}) %all-to-all-start) | async-done | bytes 786464 | tf_op jit(solution)/shard_map/all_to_all | solution.py:32
  31.5 5.9 %all-to-all-start.1 = ((bf16[32,32,384]{2,1,0:T(8,128)(2,1)}), bf16[32,32,384]{2,1,0:T(8,128)(2,1)}, u32[]{:S(2)}, u32[]{:S(2)}) async-start(bf16[32,32,384]{2,1,0:T(8,128)(2,1)} %shard_map.86), calls=%async_computation.1 | async-start | bytes 1572864 | tf_op jit(solution)/shard_map/all_to_all | solution.py:32
  37.6 1.8 copy-done.4
  39.4 2.4 shard_map.87
  44.2 8.4 %all-to-all-done.1 = bf16[32,32,384]{2,1,0:T(8,128)(2,1)} async-done(((bf16[32,32,384]{2,1,0:T(8,128)(2,1)}), bf16[32,32,384]{2,1,0:T(8,128)(2,1)}, u32[]{:S(2)}, u32[]{:S(2)}) %all-to-all-start.1) | async-done | bytes 786464 | tf_op jit(solution)/shard_map/all_to_all | solution.py:32
  52.7 2.2 shard_map.88.y_ref
  55.8 4.2 %shard_map.89 = (f32[1024,2048]{1,0:T(8,128)S(1)}, f32[8,16,128]{2,1,0:T(8,128)S(1)}) custom-call(bf16[1024,384]{1,0:T(8,128)(2,1)} %bitcast.3.z_ref, bf16[384,2048]{1,0:T(8,128)(2,1)} %copy-done.8), custom_call_target="tpu_custom_call" | custom-call | flops 1610612736 | bytes 8388608 | tf_op jit(solution)/shard_map/pallas_call | solution.py:433
  59.9 17.3 %all_to_all.60.parts_ref = f32[8,16,128]{2,1,0:T(8,128)S(1)} all-to-all(f32[8,16,128]{2,1,0:T(8,128)S(1)} %get-tuple-element.46), channel_id=1, replica_groups=mesh['z'=8,'yh'=2,'yl'=2,'x'=4,'c'=2] {'z'}, dimensions={0} | all-to-all | bytes 131072 | tf_op jit(solution)/shard_map/all_to_all | solution.py:32
  78.4 12.0 %all_to_all.61.parts_ref = f32[32,8,128]{2,1,0:T(8,128)S(1)} all-to-all(f32[32,8,128]{2,1,0:T(8,128)S(1)} %shard_map.90), channel_id=1, replica_groups=mesh['z'=8,'yh'=2,'yl'=2,'x'=4,'c'=2] {'yh','yl','x','c'}, dimensions={0} | all-to-all | bytes 262144 | tf_op jit(solution)/shard_map/all_to_all | solution.py:32
  91.4 10.8 %all_to_all.62.parts_ref = f32[8,16,128]{2,1,0:T(8,128)S(1)} all-to-all(f32[8,16,128]{2,1,0:T(8,128)S(1)} %shard_map.91), channel_id=1, replica_groups=mesh['z'=8,'yh'=2,'yl'=2,'x'=4,'c'=2] {'z'}, dimensions={0} | all-to-all | bytes 131072 | tf_op jit(solution)/shard_map/all_to_all | solution.py:32
  103.3 11.3 %all_to_all.63.parts_ref = f32[32,8,128]{2,1,0:T(8,128)S(1)} all-to-all(f32[32,8,128]{2,1,0:T(8,128)S(1)} %shard_map.92), channel_id=1, replica_groups=mesh['z'=8,'yh'=2,'yl'=2,'x'=4,'c'=2] {'yh','yl','x','c'}, dimensions={0} | all-to-all | bytes 262144 | tf_op jit(solution)/shard_map/all_to_all | solution.py:32
  115.6 10.8 %all_to_all.64.parts_ref.col_parts_ref = f32[8,16,128]{2,1,0:T(8,128)S(1)} all-to-all(f32[8,16,128]{2,1,0:T(8,128)S(1)} %shard_map.93), channel_id=1, replica_groups=mesh['z'=8,'yh'=2,'yl'=2,'x'=4,'c'=2] {'z'}, dimensions={0} | all-to-all | bytes 131072 | tf_op jit(solution)/shard_map/all_to_all | solution.py:32
  126.3 8.6 %shard_map.94 = (f32[32,24,128]{2,1,0:T(8,128)S(1)}, bf16[1024,384]{1,0:T(8,128)(2,1)S(1)}, bf16[384,1024]{1,0:T(8,128)(2,1)S(1)}) custom-call(f32[8,16,128]{2,1,0:T(8,128)S(1)} %all_to_all.64.parts_ref.col_parts_ref, f32[1024,2048]{1,0:T(8,128)} %copy-done.1, f32[1024,384]{1,0:T(8,128)} %all-gather.6.cloned.1.call-done.y_ref, ...), custom_call_target="tpu_custom_call" | custom-call | flops 1610612736 | bytes 8388608 | tf_op jit(solution)/shard_map/pallas_call | solution.py:479
  135.0 13.8 %all_to_all.65.row_parts_ref = f32[32,24,128]{2,1,0:T(8,128)S(1)} all-to-all(f32[32,24,128]{2,1,0:T(8,128)S(1)} %get-tuple-element.52), channel_id=1, replica_groups=mesh['z'=8,'yh'=2,'yl'=2,'x'=4,'c'=2] {'yh','yl','x','c'}, dimensions={0} | all-to-all | bytes 786432 | tf_op jit(solution)/shard_map/all_to_all | solution.py:32
  148.8 10.4 %shard_map.95 = (f32[1024,384]{1,0:T(8,128)}, f32[384,2048]{1,0:T(8,128)}, f32[1,2048]{1,0:T(1,128)}) custom-call(f32[32,24,128]{2,1,0:T(8,128)S(1)} %all_to_all.65.row_parts_ref, f32[8,16,128]{2,1,0:T(8,128)S(1)} %all_to_all.64.parts_ref.col_parts_ref, f32[1024,2048]{1,0:T(8,128)S(1)} %copy-done.2, bf16[1024,384]{1,0:T(8,128)(2,1)S(1)} %get-tuple-element.53.z_ref, ...), custom_call_target="tpu_custom_call" | custom-call | flops 4831838208 | bytes 8388608 | tf_op jit(solution)/shard_map/pallas_call | solution.py:510
  159.2 1.6 multiply_convert_fusion
  160.8 18.0 %all_to_all.66 = f16[32,32,384]{2,1,0:T(8,128)(2,1)S(1)} all-to-all(f16[32,32,384]{2,1,0:T(8,128)(2,1)S(1)} %bitcast.10), channel_id=1, replica_groups=mesh['z'=8,'yh'=2,'yl'=2,'x'=4,'c'=2] {'yh','yl','x','c'}, dimensions={0} | all-to-all | bytes 1572864 | tf_op jit(solution)/shard_map/all_to_all | solution.py:32
  178.9 1.7 shard_map.96
  180.6 5.4 %all-to-all-start.9 = ((bf16[16,32,384]{2,1,0:T(8,128)(2,1)}), bf16[16,32,384]{2,1,0:T(8,128)(2,1)}, u32[]{:S(2)}, u32[]{:S(2)}) async-start(bf16[16,32,384]{2,1,0:T(8,128)(2,1)} %shard_map.96), calls=%async_computation.9 | async-start | bytes 786432 | tf_op jit(solution)/shard_map/all_to_all | solution.py:32
  186.0 1.6 constant_dynamic-slice_fusion.2.hidden_ref
  187.6 5.0 %all-to-all-done.9 = bf16[16,32,384]{2,1,0:T(8,128)(2,1)} async-done(((bf16[16,32,384]{2,1,0:T(8,128)(2,1)}), bf16[16,32,384]{2,1,0:T(8,128)(2,1)}, u32[]{:S(2)}, u32[]{:S(2)}) %all-to-all-start.9) | async-done | bytes 393248 | tf_op jit(solution)/shard_map/all_to_all | solution.py:32
  192.6 2.0 shard_map.97
  194.6 4.2 %all-to-all-start.10 = ((f32[16,32,128]{2,1,0:T(8,128)}), f32[16,32,128]{2,1,0:T(8,128)}, u32[]{:S(2)}, u32[]{:S(2)}) async-start(f32[16,32,128]{2,1,0:T(8,128)} %shard_map.97), calls=%async_computation.10 | async-start | bytes 524288 | tf_op jit(solution)/shard_map/all_to_all | solution.py:32
  200.1 13.9 %all-to-all-done.10.parts_ref = f32[16,32,128]{2,1,0:T(8,128)} async-done(((f32[16,32,128]{2,1,0:T(8,128)}), f32[16,32,128]{2,1,0:T(8,128)}, u32[]{:S(2)}, u32[]{:S(2)}) %all-to-all-start.10) | async-done | bytes 262176 | tf_op jit(solution)/shard_map/all_to_all | solution.py:32
  214.0 1.7 shard_map.98
  215.7 3.5 %all-to-all-start.11 = ((f32[16,32,128]{2,1,0:T(8,128)}), f32[16,32,128]{2,1,0:T(8,128)S(1)}, u32[]{:S(2)}, u32[]{:S(2)}) async-start(f32[16,32,128]{2,1,0:T(8,128)} %shard_map.98), calls=%async_computation.11 | async-start | bytes 524288 | tf_op jit(solution)/shard_map/all_to_all | solution.py:32
  219.3 1.8 constant_dynamic-slice_fusion
  221.1 3.3 %collective-permute-start.2 = (f32[24,2048]{1,0:T(8,128)}, f32[24,2048]{1,0:T(8,128)}, u32[]{:S(2)}, u32[]{:S(2)}) collective-permute-start(f32[24,2048]{1,0:T(8,128)} %get-tuple-element.67), channel_id=1, source_target_pairs={{0,16},{16,0},{1,17},{17,1},{2,18},{18,2},{3,19},{19,3},{4,20},{20... | collective-permute-start | bytes 589832 | tf_op jit(solution)/shard_map/ppermute | solution.py:63
  224.4 8.3 %all-to-all-done.11.parts_ref = f32[16,32,128]{2,1,0:T(8,128)S(1)} async-done(((f32[16,32,128]{2,1,0:T(8,128)}), f32[16,32,128]{2,1,0:T(8,128)S(1)}, u32[]{:S(2)}, u32[]{:S(2)}) %all-to-all-start.11) | async-done | bytes 262176 | tf_op jit(solution)/shard_map/all_to_all | solution.py:32
  232.7 2.1 shard_map.99
  (48 shorter events, 14.3 us)
Async XLA Ops:
  7.2 30.3 %copy-start = (bf16[384,4096]{1,0:T(8,128)(2,1)S(1)}, bf16[384,4096]{1,0:T(8,128)(2,1)}, u32[]{:S(2)}) copy-start(bf16[384,4096]{1,0:T(8,128)(2,1)} %param.10) | copy-start | bytes 9437188
  7.2 45.5 %all-gather.4.cloned.1.call-start = ((), (), s32[]{:S(2)}) async-start(), calls=%async_computation.13 | async-start | bytes 1671168 | tf_op jit(solution)/shard_map/all_gather | solution.py:564
  10.0 17.7 %all-to-all-start = ((bf16[8,128,384]{2,1,0:T(8,128)(2,1)}), bf16[8,128,384]{2,1,0:T(8,128)(2,1)}, u32[]{:S(2)}, u32[]{:S(2)}) async-start(bf16[8,128,384]{2,1,0:T(8,128)(2,1)} %get-tuple-element.37), calls=%async_computation | async-start | bytes 1572864 | tf_op jit(solution)/shard_map/all_to_all | solution.py:32
  16.4 1.3 collective-permute-start
  29.2 1.3 collective-permute-start.1
  31.5 21.1 %all-to-all-start.1 = ((bf16[32,32,384]{2,1,0:T(8,128)(2,1)}), bf16[32,32,384]{2,1,0:T(8,128)(2,1)}, u32[]{:S(2)}, u32[]{:S(2)}) async-start(bf16[32,32,384]{2,1,0:T(8,128)(2,1)} %shard_map.86), calls=%async_computation.1 | async-start | bytes 1572864 | tf_op jit(solution)/shard_map/all_to_all | solution.py:32
  37.4 78.2 %all-gather.6.cloned.1.call-start = ((), (), s32[]{:S(2)}) async-start(), calls=%async_computation.14 | async-start | bytes 1622016 | tf_op jit(solution)/shard_map/all_gather | solution.py:579
  37.4 1.9 copy-start.4
  41.8 1.5 copy-start.7
  41.8 1.6 copy-start.8
  41.8 10.9 %copy-start.6 = (bf16[32,2048]{1,0:T(8,128)(2,1)S(1)}, bf16[32,2048]{1,0:T(8,128)(2,1)}, u32[]{:S(2)}) copy-start(bf16[32,2048]{1,0:T(8,128)(2,1)} %hidden_ref.3) | copy-start | bytes 393220
  55.0 104.2 %all-gather.8.cloned.1.call-start = ((), (), s32[]{:S(2)}) async-start(), calls=%async_computation.15 | async-start | bytes 2228224 | tf_op jit(solution)/shard_map/all_gather | solution.py:580
  55.7 163.6 %reduce-scatter.2.cloned.1.call-start = ((), (), s32[]{:S(2)}) async-start(), calls=%async_computation.16 | async-start | bytes 3538944 | tf_op jit(solution)/shard_map/reduce_scatter | solution.py:600
  59.9 54.7 %copy-start.1 = (f32[1024,2048]{1,0:T(8,128)}, f32[1024,2048]{1,0:T(8,128)S(1)}, u32[]{:S(2)}) copy-start(f32[1024,2048]{1,0:T(8,128)S(1)} %get-tuple-element.47.exp_ref) | copy-start | bytes 25165828
  126.3 22.4 %copy-start.2 = (f32[1024,2048]{1,0:T(8,128)S(1)}, f32[1024,2048]{1,0:T(8,128)}, u32[]{:S(2)}) copy-start(f32[1024,2048]{1,0:T(8,128)} %copy-done.1) | copy-start | bytes 25165828
  126.3 22.4 %copy-start.3 = (bf16[384,2048]{1,0:T(8,128)(2,1)S(1)}, bf16[384,2048]{1,0:T(8,128)(2,1)}, u32[]{:S(2)}) copy-start(bf16[384,2048]{1,0:T(8,128)(2,1)} %constant_dynamic-slice_fusion.3.v_ref) | copy-start | bytes 4718596
  126.3 22.4 %copy-start.5 = (f32[1024,384]{1,0:T(8,128)S(1)}, f32[1024,384]{1,0:T(8,128)}, u32[]{:S(2)}) copy-start(f32[1024,384]{1,0:T(8,128)} %all-gather.6.cloned.1.call-done.y_ref) | copy-start | bytes 4718596
  180.6 12.1 %all-to-all-start.9 = ((bf16[16,32,384]{2,1,0:T(8,128)(2,1)}), bf16[16,32,384]{2,1,0:T(8,128)(2,1)}, u32[]{:S(2)}, u32[]{:S(2)}) async-start(bf16[16,32,384]{2,1,0:T(8,128)(2,1)} %shard_map.96), calls=%async_computation.9 | async-start | bytes 786432 | tf_op jit(solution)/shard_map/all_to_all | solution.py:32
  194.6 19.4 %all-to-all-start.10 = ((f32[16,32,128]{2,1,0:T(8,128)}), f32[16,32,128]{2,1,0:T(8,128)}, u32[]{:S(2)}, u32[]{:S(2)}) async-start(f32[16,32,128]{2,1,0:T(8,128)} %shard_map.97), calls=%async_computation.10 | async-start | bytes 524288 | tf_op jit(solution)/shard_map/all_to_all | solution.py:32
  215.7 16.9 %all-to-all-start.11 = ((f32[16,32,128]{2,1,0:T(8,128)}), f32[16,32,128]{2,1,0:T(8,128)S(1)}, u32[]{:S(2)}, u32[]{:S(2)}) async-start(f32[16,32,128]{2,1,0:T(8,128)} %shard_map.98), calls=%async_computation.11 | async-start | bytes 524288 | tf_op jit(solution)/shard_map/all_to_all | solution.py:32
  221.1 11.6 %collective-permute-start.2 = (f32[24,2048]{1,0:T(8,128)}, f32[24,2048]{1,0:T(8,128)}, u32[]{:S(2)}, u32[]{:S(2)}) collective-permute-start(f32[24,2048]{1,0:T(8,128)} %get-tuple-element.67), channel_id=1, source_target_pairs={{0,16},{16,0},{1,17},{17,1},{2,18},{18,2},{3,19},{19,3},{4,20},{20... | collective-permute-start | bytes 589832 | tf_op jit(solution)/shard_map/ppermute | solution.py:63
Sparse Core Ops, SparseCore 0:
  9.9 42.7 all-gather.3
  55.8 49.4 all-gather.5
  107.2 35.8 all-gather.7
  159.3 41.2 reduce-scatter.1

commit v10 on v9

--- a/solution.py
+++ b/solution.py
@@ -55,11 +55,34 @@
     )(part, over_cores(part[rows:]))
 
 
-def swap(block):
-    side = lax.axis_index("yh")
+def shares_kernel(side_ref, block_ref, ready_ref, kept_ref, sent_ref):
+    del ready_ref
+    rows = kept_ref.shape[0]
+
+    @pl.when(side_ref[0] == 0)
+    def _():
+        kept_ref[...] = block_ref[0:rows, :]
+        sent_ref[...] = block_ref[rows:, :]
+
+    @pl.when(side_ref[0] != 0)
+    def _():
+        kept_ref[...] = block_ref[rows:, :]
+        sent_ref[...] = block_ref[0:rows, :]
+
+
+def swap(block, ready):
     rows = block.shape[0] // lax.axis_size("yh")
-    kept = lax.dynamic_slice_in_dim(block, side * rows, rows, 0)
-    sent = lax.dynamic_slice_in_dim(block, (1 - side) * rows, rows, 0)
+    share = pltpu.HBM((rows, block.shape[1]), jnp.float32)
+    kept, sent = pl.pallas_call(
+        shares_kernel,
+        in_specs=[
+            pl.BlockSpec(memory_space=pltpu.SMEM),
+            pl.BlockSpec(memory_space=pltpu.VMEM),
+            pl.BlockSpec(memory_space=pl.ANY),
+        ],
+        out_shape=[share, share],
+        compiler_params=pltpu.CompilerParams(vmem_limit_bytes=8 * MIB),
+    )(lax.axis_index("yh").reshape(1), hbm(block), hbm(ready))
     return kept, lax.ppermute(sent, "yh", [(0, 1), (1, 0)])
 
 
@@ -295,7 +318,8 @@
         out_ref[i, height - tail : height, :] = jnp.broadcast_to(dots, (tail, LANES))
 
 
-def collect_kernel(parts_ref, loss_ref, out_ref):
+def collect_kernel(parts_ref, loss_ref, ready_ref, out_ref):
+    del ready_ref
     copies, height = parts_ref.shape[:2]
     sides = []
     for side in range(2):
@@ -615,12 +639,14 @@
         out_shape=pltpu.HBM((copies, height, LANES), jnp.float32),
         compiler_params=pltpu.CompilerParams(vmem_limit_bytes=8 * MIB),
     )(hbm(hid_block), hbm(dy_group), hbm(dots))
+    kept, got = swap(dproto, proj_rows)
     collected = pl.pallas_call(
         collect_kernel,
-        out_shape=pltpu.HBM((copies, height, LANES), jnp.float32),
+        in_specs=[pl.BlockSpec(memory_space=pltpu.VMEM)] * 2
+        + [pl.BlockSpec(memory_space=pl.ANY)],
+        out_shape=f32(copies, height, LANES),
         compiler_params=pltpu.CompilerParams(vmem_limit_bytes=8 * MIB),
-    )(exchange(proj_rows, DP), loss_part.reshape(1, 1))
-    kept, got = swap(dproto)
+    )(exchange(proj_rows, DP), loss_part.reshape(1, 1), hbm(got))
     grad_proj, grad_proto, loss = pl.pallas_call(
         finish_kernel,
         in_specs=[pl.BlockSpec(memory_space=pltpu.SMEM)]

time: 242 us -> 245 us (1.012)
  blocking collectives: 93.8 us -> 113 us
  waiting for transfers between devices: 49.7 us -> 36.9 us
  starting transfers between devices: 28.9 us -> 24.8 us
    all_to_all x7 -> x8, blocking collectives: 93.8 us -> 113 us  [exchange(): return lax.all_to_all(blocks, axes, 0, 0, tiled=True)]
    all_to_all x5 -> x4, waiting for transfers between devices: 45.7 us -> 30.9 us  [exchange(): return lax.all_to_all(blocks, axes, 0, 0, tiled=True)]
    all_to_all x5 -> x4, starting transfers between devices: 25.4 us -> 21.9 us  [exchange(): return lax.all_to_all(blocks, axes, 0, 0, tiled=True)]
  transfers between devices with their start and end apart: 12 -> 11, of which waited for: 8 -> 8; matrix products, arithmetic and copies ran while one was open for 4% -> 3% of each run, Pallas kernels for 16% -> 16%
where the time goes in v10:
time: 245 us; the launch traced here: 243 us
  blocking collectives  113 us (46%)
  Pallas kernels  43.8 us (18%)
  waiting for transfers between devices  36.9 us (15%)
  starting transfers between devices  24.8 us (10%)
  between operations  14.6 us (6%)
  local copies, waits for them, and re-layouts  5.13 us (2%)
  other arithmetic  3.13 us (1%)
    all_to_all x8, blocking collectives, exchange(): return lax.all_to_all(blocks, axes, 0, 0, tiled=True)  113 us
    all_to_all x4, waiting for transfers between devices, exchange(): return lax.all_to_all(blocks, axes, 0, 0, tiled=True)  30.9 us
    all_to_all x4, starting transfers between devices, exchange(): return lax.all_to_all(blocks, axes, 0, 0, tiled=True)  21.9 us
    pallas_call x1, Pallas kernels, gradient_pass(): pl.pallas_call(gradient_kernel, grid=(width // CHUNK,), in_specs=[whole(r...  10.4 us
    pallas_call x1, Pallas kernels, student_pass(): pl.pallas_call(student_kernel, grid=(rows // TALL_BLOCK,), in_specs=[whol...  8.6 us
  transfers between devices with their start and end apart: 11, of which 8 were waited for; matrix products, arithmetic and copies ran while one was open for 3% of the time, Pallas kernels for 16%

profile of v10, /device:TPU:2, one launch (start us, length us, event | category | flops | bytes accessed | tf_op | source)
XLA Modules:
  0.0 243.2 jit_solution(3558256348184200032)
XLA Ops:
  7.9 2.1 shard_map.85
  10.1 6.4 %all-to-all-start = ((bf16[8,128,384]{2,1,0:T(8,128)(2,1)}), bf16[8,128,384]{2,1,0:T(8,128)(2,1)}, u32[]{:S(2)}, u32[]{:S(2)}) async-start(bf16[8,128,384]{2,1,0:T(8,128)(2,1)} %get-tuple-element.39), calls=%async_computation | async-start | bytes 1572864 | tf_op jit(solution)/shard_map/all_to_all | solution.py:32
  17.7 10.1 %all-to-all-done = bf16[8,128,384]{2,1,0:T(8,128)(2,1)} async-done(((bf16[8,128,384]{2,1,0:T(8,128)(2,1)}), bf16[8,128,384]{2,1,0:T(8,128)(2,1)}, u32[]{:S(2)}, u32[]{:S(2)}) %all-to-all-start) | async-done | bytes 786464 | tf_op jit(solution)/shard_map/all_to_all | solution.py:32
  31.5 5.9 %all-to-all-start.1 = ((bf16[32,32,384]{2,1,0:T(8,128)(2,1)}), bf16[32,32,384]{2,1,0:T(8,128)(2,1)}, u32[]{:S(2)}, u32[]{:S(2)}) async-start(bf16[32,32,384]{2,1,0:T(8,128)(2,1)} %shard_map.86), calls=%async_computation.1 | async-start | bytes 1572864 | tf_op jit(solution)/shard_map/all_to_all | solution.py:32
  37.6 1.8 copy-done.4
  39.4 2.4 shard_map.87
  41.9 1.5 constant_dynamic-slice_fusion.1.v_ref
  44.2 8.4 %all-to-all-done.1 = bf16[32,32,384]{2,1,0:T(8,128)(2,1)} async-done(((bf16[32,32,384]{2,1,0:T(8,128)(2,1)}), bf16[32,32,384]{2,1,0:T(8,128)(2,1)}, u32[]{:S(2)}, u32[]{:S(2)}) %all-to-all-start.1) | async-done | bytes 786464 | tf_op jit(solution)/shard_map/all_to_all | solution.py:32
  52.7 2.2 shard_map.88.y_ref
  55.8 4.2 %shard_map.89 = (f32[1024,2048]{1,0:T(8,128)S(1)}, f32[8,16,128]{2,1,0:T(8,128)S(1)}) custom-call(bf16[1024,384]{1,0:T(8,128)(2,1)} %bitcast.3.z_ref, bf16[384,2048]{1,0:T(8,128)(2,1)} %copy-done.8), custom_call_target="tpu_custom_call" | custom-call | flops 1610612736 | bytes 8388608 | tf_op jit(solution)/shard_map/pallas_call | solution.py:457
  60.0 17.3 %all_to_all.60.parts_ref = f32[8,16,128]{2,1,0:T(8,128)S(1)} all-to-all(f32[8,16,128]{2,1,0:T(8,128)S(1)} %get-tuple-element.48), channel_id=1, replica_groups=mesh['z'=8,'yh'=2,'yl'=2,'x'=4,'c'=2] {'z'}, dimensions={0} | all-to-all | bytes 131072 | tf_op jit(solution)/shard_map/all_to_all | solution.py:32
  78.5 12.0 %all_to_all.61.parts_ref = f32[32,8,128]{2,1,0:T(8,128)S(1)} all-to-all(f32[32,8,128]{2,1,0:T(8,128)S(1)} %shard_map.90), channel_id=1, replica_groups=mesh['z'=8,'yh'=2,'yl'=2,'x'=4,'c'=2] {'yh','yl','x','c'}, dimensions={0} | all-to-all | bytes 262144 | tf_op jit(solution)/shard_map/all_to_all | solution.py:32
  91.4 10.8 %all_to_all.62.parts_ref = f32[8,16,128]{2,1,0:T(8,128)S(1)} all-to-all(f32[8,16,128]{2,1,0:T(8,128)S(1)} %shard_map.91), channel_id=1, replica_groups=mesh['z'=8,'yh'=2,'yl'=2,'x'=4,'c'=2] {'z'}, dimensions={0} | all-to-all | bytes 131072 | tf_op jit(solution)/shard_map/all_to_all | solution.py:32
  103.4 11.3 %all_to_all.63.parts_ref = f32[32,8,128]{2,1,0:T(8,128)S(1)} all-to-all(f32[32,8,128]{2,1,0:T(8,128)S(1)} %shard_map.92), channel_id=1, replica_groups=mesh['z'=8,'yh'=2,'yl'=2,'x'=4,'c'=2] {'yh','yl','x','c'}, dimensions={0} | all-to-all | bytes 262144 | tf_op jit(solution)/shard_map/all_to_all | solution.py:32
  115.6 10.8 %all_to_all.64.parts_ref.col_parts_ref = f32[8,16,128]{2,1,0:T(8,128)S(1)} all-to-all(f32[8,16,128]{2,1,0:T(8,128)S(1)} %shard_map.93), channel_id=1, replica_groups=mesh['z'=8,'yh'=2,'yl'=2,'x'=4,'c'=2] {'z'}, dimensions={0} | all-to-all | bytes 131072 | tf_op jit(solution)/shard_map/all_to_all | solution.py:32
  126.4 8.6 %shard_map.94 = (f32[32,24,128]{2,1,0:T(8,128)S(1)}, bf16[1024,384]{1,0:T(8,128)(2,1)S(1)}, bf16[384,1024]{1,0:T(8,128)(2,1)S(1)}) custom-call(f32[8,16,128]{2,1,0:T(8,128)S(1)} %all_to_all.64.parts_ref.col_parts_ref, f32[1024,2048]{1,0:T(8,128)} %copy-done.1, f32[1024,384]{1,0:T(8,128)} %all-gather.6.cloned.1.call-done.y_ref, ...), custom_call_target="tpu_custom_call" | custom-call | flops 1610612736 | bytes 8388608 | tf_op jit(solution)/shard_map/pallas_call | solution.py:503
  135.0 13.8 %all_to_all.65.row_parts_ref = f32[32,24,128]{2,1,0:T(8,128)S(1)} all-to-all(f32[32,24,128]{2,1,0:T(8,128)S(1)} %get-tuple-element.54), channel_id=1, replica_groups=mesh['z'=8,'yh'=2,'yl'=2,'x'=4,'c'=2] {'yh','yl','x','c'}, dimensions={0} | all-to-all | bytes 786432 | tf_op jit(solution)/shard_map/all_to_all | solution.py:32
  148.8 10.4 %shard_map.95 = (f32[1024,384]{1,0:T(8,128)}, f32[384,2048]{1,0:T(8,128)}, f32[1,2048]{1,0:T(1,128)}) custom-call(f32[32,24,128]{2,1,0:T(8,128)S(1)} %all_to_all.65.row_parts_ref, f32[8,16,128]{2,1,0:T(8,128)S(1)} %all_to_all.64.parts_ref.col_parts_ref, f32[1024,2048]{1,0:T(8,128)S(1)} %copy-done.2, bf16[1024,384]{1,0:T(8,128)(2,1)S(1)} %get-tuple-element.55.z_ref, ...), custom_call_target="tpu_custom_call" | custom-call | flops 4831838208 | bytes 8388608 | tf_op jit(solution)/shard_map/pallas_call | solution.py:534
  159.2 1.6 multiply_convert_fusion
  160.7 18.0 %all_to_all.66 = f16[32,32,384]{2,1,0:T(8,128)(2,1)S(1)} all-to-all(f16[32,32,384]{2,1,0:T(8,128)(2,1)S(1)} %bitcast.10), channel_id=1, replica_groups=mesh['z'=8,'yh'=2,'yl'=2,'x'=4,'c'=2] {'yh','yl','x','c'}, dimensions={0} | all-to-all | bytes 1572864 | tf_op jit(solution)/shard_map/all_to_all | solution.py:32
  178.9 1.7 shard_map.96
  180.6 5.4 %all-to-all-start.9 = ((bf16[16,32,384]{2,1,0:T(8,128)(2,1)}), bf16[16,32,384]{2,1,0:T(8,128)(2,1)}, u32[]{:S(2)}, u32[]{:S(2)}) async-start(bf16[16,32,384]{2,1,0:T(8,128)(2,1)} %shard_map.96), calls=%async_computation.9 | async-start | bytes 786432 | tf_op jit(solution)/shard_map/all_to_all | solution.py:32
  186.0 1.6 constant_dynamic-slice_fusion.hidden_ref
  187.6 5.0 %all-to-all-done.9 = bf16[16,32,384]{2,1,0:T(8,128)(2,1)} async-done(((bf16[16,32,384]{2,1,0:T(8,128)(2,1)}), bf16[16,32,384]{2,1,0:T(8,128)(2,1)}, u32[]{:S(2)}, u32[]{:S(2)}) %all-to-all-start.9) | async-done | bytes 393248 | tf_op jit(solution)/shard_map/all_to_all | solution.py:32
  192.6 2.0 shard_map.97.ready_ref
  194.6 4.2 %all-to-all-start.10 = ((f32[16,32,128]{2,1,0:T(8,128)}), f32[16,32,128]{2,1,0:T(8,128)}, u32[]{:S(2)}, u32[]{:S(2)}) async-start(f32[16,32,128]{2,1,0:T(8,128)} %shard_map.97.ready_ref), calls=%async_computation.10 | async-start | bytes 524288 | tf_op jit(solution)/shard_map/all_to_all | solution.py:32
  198.8 2.0 reduce-scatter.2.cloned.1.call-done.block_ref
  200.8 1.8 shard_map.98
  202.6 2.7 %collective-permute-start.2 = (f32[24,2048]{1,0:T(8,128)}, f32[24,2048]{1,0:T(8,128)}, u32[]{:S(2)}, u32[]{:S(2)}) collective-permute-start(f32[24,2048]{1,0:T(8,128)} %get-tuple-element.64), channel_id=1, source_target_pairs={{0,16},{16,0},{1,17},{17,1},{2,18},{18,2},{3,19},{19,3},{4,20},{20... | collective-permute-start | bytes 589832 | tf_op jit(solution)/shard_map/ppermute | solution.py:86
  206.6 7.4 %all-to-all-done.10.parts_ref = f32[16,32,128]{2,1,0:T(8,128)} async-done(((f32[16,32,128]{2,1,0:T(8,128)}), f32[16,32,128]{2,1,0:T(8,128)}, u32[]{:S(2)}, u32[]{:S(2)}) %all-to-all-start.10) | async-done | bytes 262176 | tf_op jit(solution)/shard_map/all_to_all | solution.py:32
  215.0 19.6 %all_to_all.67.parts_ref = f32[16,32,128]{2,1,0:T(8,128)S(1)} all-to-all(f32[16,32,128]{2,1,0:T(8,128)S(1)} %shard_map.99), channel_id=1, replica_groups=mesh['z'=8,'yh'=2,'yl'=2,'x'=4,'c'=2] {'z','yh'}, dimensions={0} | all-to-all | bytes 524288 | tf_op jit(solution)/shard_map/all_to_all | solution.py:32
  234.6 2.1 shard_map.100
  (47 shorter events, 13.9 us)
Async XLA Ops:
  7.2 30.3 %copy-start = (bf16[384,4096]{1,0:T(8,128)(2,1)S(1)}, bf16[384,4096]{1,0:T(8,128)(2,1)}, u32[]{:S(2)}) copy-start(bf16[384,4096]{1,0:T(8,128)(2,1)} %param.10) | copy-start | bytes 9437188
  7.2 45.6 %all-gather.4.cloned.1.call-start = ((), (), s32[]{:S(2)}) async-start(), calls=%async_computation.13 | async-start | bytes 1671168 | tf_op jit(solution)/shard_map/all_gather | solution.py:588
  10.1 17.7 %all-to-all-start = ((bf16[8,128,384]{2,1,0:T(8,128)(2,1)}), bf16[8,128,384]{2,1,0:T(8,128)(2,1)}, u32[]{:S(2)}, u32[]{:S(2)}) async-start(bf16[8,128,384]{2,1,0:T(8,128)(2,1)} %get-tuple-element.39), calls=%async_computation | async-start | bytes 1572864 | tf_op jit(solution)/shard_map/all_to_all | solution.py:32
  16.4 1.3 collective-permute-start
  29.2 1.3 collective-permute-start.1
  31.5 21.1 %all-to-all-start.1 = ((bf16[32,32,384]{2,1,0:T(8,128)(2,1)}), bf16[32,32,384]{2,1,0:T(8,128)(2,1)}, u32[]{:S(2)}, u32[]{:S(2)}) async-start(bf16[32,32,384]{2,1,0:T(8,128)(2,1)} %shard_map.86), calls=%async_computation.1 | async-start | bytes 1572864 | tf_op jit(solution)/shard_map/all_to_all | solution.py:32
  37.4 78.2 %all-gather.6.cloned.1.call-start = ((), (), s32[]{:S(2)}) async-start(), calls=%async_computation.14 | async-start | bytes 1622016 | tf_op jit(solution)/shard_map/all_gather | solution.py:603
  37.5 1.9 copy-start.4
  41.8 1.5 copy-start.7
  41.8 1.6 copy-start.8
  41.8 10.9 %copy-start.6 = (bf16[32,2048]{1,0:T(8,128)(2,1)S(1)}, bf16[32,2048]{1,0:T(8,128)(2,1)}, u32[]{:S(2)}) copy-start(bf16[32,2048]{1,0:T(8,128)(2,1)} %hidden_ref.3) | copy-start | bytes 393220
  55.0 104.2 %all-gather.8.cloned.1.call-start = ((), (), s32[]{:S(2)}) async-start(), calls=%async_computation.15 | async-start | bytes 2228224 | tf_op jit(solution)/shard_map/all_gather | solution.py:604
  55.8 145.0 %reduce-scatter.2.cloned.1.call-start = ((), (), s32[]{:S(2)}) async-start(), calls=%async_computation.16 | async-start | bytes 3538944 | tf_op jit(solution)/shard_map/reduce_scatter | solution.py:624
  60.0 54.7 %copy-start.1 = (f32[1024,2048]{1,0:T(8,128)}, f32[1024,2048]{1,0:T(8,128)S(1)}, u32[]{:S(2)}) copy-start(f32[1024,2048]{1,0:T(8,128)S(1)} %get-tuple-element.49.exp_ref) | copy-start | bytes 25165828
  126.4 22.4 %copy-start.2 = (f32[1024,2048]{1,0:T(8,128)S(1)}, f32[1024,2048]{1,0:T(8,128)}, u32[]{:S(2)}) copy-start(f32[1024,2048]{1,0:T(8,128)} %copy-done.1) | copy-start | bytes 25165828
  126.4 22.4 %copy-start.3 = (bf16[384,2048]{1,0:T(8,128)(2,1)S(1)}, bf16[384,2048]{1,0:T(8,128)(2,1)}, u32[]{:S(2)}) copy-start(bf16[384,2048]{1,0:T(8,128)(2,1)} %constant_dynamic-slice_fusion.1.v_ref) | copy-start | bytes 4718596
  126.4 22.4 %copy-start.5 = (f32[1024,384]{1,0:T(8,128)S(1)}, f32[1024,384]{1,0:T(8,128)}, u32[]{:S(2)}) copy-start(f32[1024,384]{1,0:T(8,128)} %all-gather.6.cloned.1.call-done.y_ref) | copy-start | bytes 4718596
  180.6 12.0 %all-to-all-start.9 = ((bf16[16,32,384]{2,1,0:T(8,128)(2,1)}), bf16[16,32,384]{2,1,0:T(8,128)(2,1)}, u32[]{:S(2)}, u32[]{:S(2)}) async-start(bf16[16,32,384]{2,1,0:T(8,128)(2,1)} %shard_map.96), calls=%async_computation.9 | async-start | bytes 786432 | tf_op jit(solution)/shard_map/all_to_all | solution.py:32
  194.6 19.4 %all-to-all-start.10 = ((f32[16,32,128]{2,1,0:T(8,128)}), f32[16,32,128]{2,1,0:T(8,128)}, u32[]{:S(2)}, u32[]{:S(2)}) async-start(f32[16,32,128]{2,1,0:T(8,128)} %shard_map.97.ready_ref), calls=%async_computation.10 | async-start | bytes 524288 | tf_op jit(solution)/shard_map/all_to_all | solution.py:32
  202.6 11.5 %collective-permute-start.2 = (f32[24,2048]{1,0:T(8,128)}, f32[24,2048]{1,0:T(8,128)}, u32[]{:S(2)}, u32[]{:S(2)}) collective-permute-start(f32[24,2048]{1,0:T(8,128)} %get-tuple-element.64), channel_id=1, source_target_pairs={{0,16},{16,0},{1,17},{17,1},{2,18},{18,2},{3,19},{19,3},{4,20},{20... | collective-permute-start | bytes 589832 | tf_op jit(solution)/shard_map/ppermute | solution.py:86
Sparse Core Ops, SparseCore 0:
  9.9 42.8 all-gather.3
  55.9 49.4 all-gather.5
  107.2 36.1 all-gather.7
  159.3 41.4 reduce-scatter.1

commit v11 on v9

--- a/solution.py
+++ b/solution.py
@@ -538,7 +538,7 @@
         ],
         compiler_params=params(28),
         cost_estimate=cost(6 * z.size * width, exp.size * 4, exp.size),
-    )(row_parts, col_parts, exp, z, zt, v, y)
+    )(row_parts, col_parts, hbm(exp), z, zt, v, y)
 
 
 def backward_kernel(sum_ref, y_ref, out_ref):

time: 242 us -> 243 us (level)
  no operation moved by 1% of the time
where the time goes in v11:
time: 243 us; the launch traced here: 242 us
  blocking collectives  93.8 us (39%)
  waiting for transfers between devices  49.6 us (20%)
  Pallas kernels  43.7 us (18%)
  starting transfers between devices  29 us (12%)
  between operations  14.7 us (6%)
  local copies, waits for them, and re-layouts  7.01 us (3%)
  other arithmetic  3.12 us (1%)
    all_to_all x7, blocking collectives, exchange(): return lax.all_to_all(blocks, axes, 0, 0, tiled=True)  93.8 us
    all_to_all x5, waiting for transfers between devices, exchange(): return lax.all_to_all(blocks, axes, 0, 0, tiled=True)  45.4 us
    all_to_all x5, starting transfers between devices, exchange(): return lax.all_to_all(blocks, axes, 0, 0, tiled=True)  25.4 us
    pallas_call x1, Pallas kernels, gradient_pass(): pl.pallas_call(gradient_kernel, grid=(width // CHUNK,), in_specs=[whole(r...  11.4 us
    pallas_call x1, Pallas kernels, student_pass(): pl.pallas_call(student_kernel, grid=(rows // TALL_BLOCK,), in_specs=[whol...  8.59 us
  transfers between devices with their start and end apart: 12, of which 8 were waited for; matrix products, arithmetic and copies ran while one was open for 4% of the time, Pallas kernels for 16%

profile of v11, /device:TPU:2, one launch (start us, length us, event | category | flops | bytes accessed | tf_op | source)
XLA Modules:
  0.0 242.2 jit_solution(8856910692994203381)
XLA Ops:
  7.9 2.1 shard_map.85
  10.1 6.4 %all-to-all-start = ((bf16[8,128,384]{2,1,0:T(8,128)(2,1)}), bf16[8,128,384]{2,1,0:T(8,128)(2,1)}, u32[]{:S(2)}, u32[]{:S(2)}) async-start(bf16[8,128,384]{2,1,0:T(8,128)(2,1)} %get-tuple-element.37), calls=%async_computation | async-start | bytes 1572864 | tf_op jit(solution)/shard_map/all_to_all | solution.py:32
  17.7 10.1 %all-to-all-done = bf16[8,128,384]{2,1,0:T(8,128)(2,1)} async-done(((bf16[8,128,384]{2,1,0:T(8,128)(2,1)}), bf16[8,128,384]{2,1,0:T(8,128)(2,1)}, u32[]{:S(2)}, u32[]{:S(2)}) %all-to-all-start) | async-done | bytes 786464 | tf_op jit(solution)/shard_map/all_to_all | solution.py:32
  31.5 5.9 %all-to-all-start.1 = ((bf16[32,32,384]{2,1,0:T(8,128)(2,1)}), bf16[32,32,384]{2,1,0:T(8,128)(2,1)}, u32[]{:S(2)}, u32[]{:S(2)}) async-start(bf16[32,32,384]{2,1,0:T(8,128)(2,1)} %shard_map.86), calls=%async_computation.1 | async-start | bytes 1572864 | tf_op jit(solution)/shard_map/all_to_all | solution.py:32
  37.6 1.8 copy-done.3
  39.4 2.4 shard_map.87
  41.9 1.6 constant_dynamic-slice_fusion.3.v_ref
  44.3 8.1 %all-to-all-done.1 = bf16[32,32,384]{2,1,0:T(8,128)(2,1)} async-done(((bf16[32,32,384]{2,1,0:T(8,128)(2,1)}), bf16[32,32,384]{2,1,0:T(8,128)(2,1)}, u32[]{:S(2)}, u32[]{:S(2)}) %all-to-all-start.1) | async-done | bytes 786464 | tf_op jit(solution)/shard_map/all_to_all | solution.py:32
  52.7 2.2 shard_map.88.y_ref
  55.8 4.2 %shard_map.89 = (f32[1024,2048]{1,0:T(8,128)S(1)}, f32[8,16,128]{2,1,0:T(8,128)S(1)}) custom-call(bf16[1024,384]{1,0:T(8,128)(2,1)} %bitcast.3.z_ref, bf16[384,2048]{1,0:T(8,128)(2,1)} %copy-done.7), custom_call_target="tpu_custom_call" | custom-call | flops 1610612736 | bytes 8388608 | tf_op jit(solution)/shard_map/pallas_call | solution.py:433
  60.0 17.3 %all_to_all.60.parts_ref = f32[8,16,128]{2,1,0:T(8,128)S(1)} all-to-all(f32[8,16,128]{2,1,0:T(8,128)S(1)} %get-tuple-element.46), channel_id=1, replica_groups=mesh['z'=8,'yh'=2,'yl'=2,'x'=4,'c'=2] {'z'}, dimensions={0} | all-to-all | bytes 131072 | tf_op jit(solution)/shard_map/all_to_all | solution.py:32
  78.5 11.9 %all_to_all.61.parts_ref = f32[32,8,128]{2,1,0:T(8,128)S(1)} all-to-all(f32[32,8,128]{2,1,0:T(8,128)S(1)} %shard_map.90), channel_id=1, replica_groups=mesh['z'=8,'yh'=2,'yl'=2,'x'=4,'c'=2] {'yh','yl','x','c'}, dimensions={0} | all-to-all | bytes 262144 | tf_op jit(solution)/shard_map/all_to_all | solution.py:32
  91.4 10.8 %all_to_all.62.parts_ref = f32[8,16,128]{2,1,0:T(8,128)S(1)} all-to-all(f32[8,16,128]{2,1,0:T(8,128)S(1)} %shard_map.91), channel_id=1, replica_groups=mesh['z'=8,'yh'=2,'yl'=2,'x'=4,'c'=2] {'z'}, dimensions={0} | all-to-all | bytes 131072 | tf_op jit(solution)/shard_map/all_to_all | solution.py:32
  103.3 11.3 %all_to_all.63.parts_ref = f32[32,8,128]{2,1,0:T(8,128)S(1)} all-to-all(f32[32,8,128]{2,1,0:T(8,128)S(1)} %shard_map.92), channel_id=1, replica_groups=mesh['z'=8,'yh'=2,'yl'=2,'x'=4,'c'=2] {'yh','yl','x','c'}, dimensions={0} | all-to-all | bytes 262144 | tf_op jit(solution)/shard_map/all_to_all | solution.py:32
  115.6 10.8 %all_to_all.64.parts_ref.col_parts_ref = f32[8,16,128]{2,1,0:T(8,128)S(1)} all-to-all(f32[8,16,128]{2,1,0:T(8,128)S(1)} %shard_map.93), channel_id=1, replica_groups=mesh['z'=8,'yh'=2,'yl'=2,'x'=4,'c'=2] {'z'}, dimensions={0} | all-to-all | bytes 131072 | tf_op jit(solution)/shard_map/all_to_all | solution.py:32
  126.4 8.6 %shard_map.94 = (f32[32,24,128]{2,1,0:T(8,128)S(1)}, bf16[1024,384]{1,0:T(8,128)(2,1)S(1)}, bf16[384,1024]{1,0:T(8,128)(2,1)S(1)}) custom-call(f32[8,16,128]{2,1,0:T(8,128)S(1)} %all_to_all.64.parts_ref.col_parts_ref, f32[1024,2048]{1,0:T(8,128)} %copy-done.1, f32[1024,384]{1,0:T(8,128)} %all-gather.6.cloned.1.call-done.y_ref, ...), custom_call_target="tpu_custom_call" | custom-call | flops 1610612736 | bytes 8388608 | tf_op jit(solution)/shard_map/pallas_call | solution.py:479
  135.0 13.8 %all_to_all.65.row_parts_ref = f32[32,24,128]{2,1,0:T(8,128)S(1)} all-to-all(f32[32,24,128]{2,1,0:T(8,128)S(1)} %get-tuple-element.52), channel_id=1, replica_groups=mesh['z'=8,'yh'=2,'yl'=2,'x'=4,'c'=2] {'yh','yl','x','c'}, dimensions={0} | all-to-all | bytes 786432 | tf_op jit(solution)/shard_map/all_to_all | solution.py:32
  148.7 11.4 %shard_map.95 = (f32[1024,384]{1,0:T(8,128)}, f32[384,2048]{1,0:T(8,128)}, f32[1,2048]{1,0:T(1,128)}) custom-call(f32[32,24,128]{2,1,0:T(8,128)S(1)} %all_to_all.65.row_parts_ref, f32[8,16,128]{2,1,0:T(8,128)S(1)} %all_to_all.64.parts_ref.col_parts_ref, f32[1024,2048]{1,0:T(8,128)} %copy-done.1, bf16[1024,384]{1,0:T(8,128)(2,1)S(1)} %get-tuple-element.53.z_ref, ...), custom_call_target="tpu_custom_call" | custom-call | flops 4831838208 | bytes 8388608 | tf_op jit(solution)/shard_map/pallas_call | solution.py:510
  161.7 18.0 %all_to_all.66 = f16[32,32,384]{2,1,0:T(8,128)(2,1)S(1)} all-to-all(f16[32,32,384]{2,1,0:T(8,128)(2,1)S(1)} %bitcast.10), channel_id=1, replica_groups=mesh['z'=8,'yh'=2,'yl'=2,'x'=4,'c'=2] {'yh','yl','x','c'}, dimensions={0} | all-to-all | bytes 1572864 | tf_op jit(solution)/shard_map/all_to_all | solution.py:32
  179.8 1.7 shard_map.96
  181.5 5.5 %all-to-all-start.9 = ((bf16[16,32,384]{2,1,0:T(8,128)(2,1)}), bf16[16,32,384]{2,1,0:T(8,128)(2,1)}, u32[]{:S(2)}, u32[]{:S(2)}) async-start(bf16[16,32,384]{2,1,0:T(8,128)(2,1)} %shard_map.96), calls=%async_computation.9 | async-start | bytes 786432 | tf_op jit(solution)/shard_map/all_to_all | solution.py:32
  186.9 1.6 constant_dynamic-slice_fusion.2.hidden_ref
  188.5 5.0 %all-to-all-done.9 = bf16[16,32,384]{2,1,0:T(8,128)(2,1)} async-done(((bf16[16,32,384]{2,1,0:T(8,128)(2,1)}), bf16[16,32,384]{2,1,0:T(8,128)(2,1)}, u32[]{:S(2)}, u32[]{:S(2)}) %all-to-all-start.9) | async-done | bytes 393248 | tf_op jit(solution)/shard_map/all_to_all | solution.py:32
  193.6 2.0 shard_map.97
  195.5 4.2 %all-to-all-start.10 = ((f32[16,32,128]{2,1,0:T(8,128)}), f32[16,32,128]{2,1,0:T(8,128)}, u32[]{:S(2)}, u32[]{:S(2)}) async-start(f32[16,32,128]{2,1,0:T(8,128)} %shard_map.97), calls=%async_computation.10 | async-start | bytes 524288 | tf_op jit(solution)/shard_map/all_to_all | solution.py:32
  201.1 13.9 %all-to-all-done.10.parts_ref = f32[16,32,128]{2,1,0:T(8,128)} async-done(((f32[16,32,128]{2,1,0:T(8,128)}), f32[16,32,128]{2,1,0:T(8,128)}, u32[]{:S(2)}, u32[]{:S(2)}) %all-to-all-start.10) | async-done | bytes 262176 | tf_op jit(solution)/shard_map/all_to_all | solution.py:32
  215.0 1.7 shard_map.98
  216.7 3.5 %all-to-all-start.11 = ((f32[16,32,128]{2,1,0:T(8,128)}), f32[16,32,128]{2,1,0:T(8,128)S(1)}, u32[]{:S(2)}, u32[]{:S(2)}) async-start(f32[16,32,128]{2,1,0:T(8,128)} %shard_map.98), calls=%async_computation.11 | async-start | bytes 524288 | tf_op jit(solution)/shard_map/all_to_all | solution.py:32
  220.3 1.8 constant_dynamic-slice_fusion
  222.1 3.3 %collective-permute-start.2 = (f32[24,2048]{1,0:T(8,128)}, f32[24,2048]{1,0:T(8,128)}, u32[]{:S(2)}, u32[]{:S(2)}) collective-permute-start(f32[24,2048]{1,0:T(8,128)} %get-tuple-element.67), channel_id=1, source_target_pairs={{0,16},{16,0},{1,17},{17,1},{2,18},{18,2},{3,19},{19,3},{4,20},{20... | collective-permute-start | bytes 589832 | tf_op jit(solution)/shard_map/ppermute | solution.py:63
  225.3 8.2 %all-to-all-done.11.parts_ref = f32[16,32,128]{2,1,0:T(8,128)S(1)} async-done(((f32[16,32,128]{2,1,0:T(8,128)}), f32[16,32,128]{2,1,0:T(8,128)S(1)}, u32[]{:S(2)}, u32[]{:S(2)}) %all-to-all-start.11) | async-done | bytes 262176 | tf_op jit(solution)/shard_map/all_to_all | solution.py:32
  233.6 2.1 shard_map.99
  (46 shorter events, 14.6 us)
Async XLA Ops:
  7.2 30.3 %copy-start = (bf16[384,4096]{1,0:T(8,128)(2,1)S(1)}, bf16[384,4096]{1,0:T(8,128)(2,1)}, u32[]{:S(2)}) copy-start(bf16[384,4096]{1,0:T(8,128)(2,1)} %param.10) | copy-start | bytes 9437188
  7.2 45.6 %all-gather.4.cloned.1.call-start = ((), (), s32[]{:S(2)}) async-start(), calls=%async_computation.13 | async-start | bytes 1671168 | tf_op jit(solution)/shard_map/all_gather | solution.py:564
  10.1 17.7 %all-to-all-start = ((bf16[8,128,384]{2,1,0:T(8,128)(2,1)}), bf16[8,128,384]{2,1,0:T(8,128)(2,1)}, u32[]{:S(2)}, u32[]{:S(2)}) async-start(bf16[8,128,384]{2,1,0:T(8,128)(2,1)} %get-tuple-element.37), calls=%async_computation | async-start | bytes 1572864 | tf_op jit(solution)/shard_map/all_to_all | solution.py:32
  16.4 1.3 collective-permute-start
  29.2 1.3 collective-permute-start.1
  31.5 20.9 %all-to-all-start.1 = ((bf16[32,32,384]{2,1,0:T(8,128)(2,1)}), bf16[32,32,384]{2,1,0:T(8,128)(2,1)}, u32[]{:S(2)}, u32[]{:S(2)}) async-start(bf16[32,32,384]{2,1,0:T(8,128)(2,1)} %shard_map.86), calls=%async_computation.1 | async-start | bytes 1572864 | tf_op jit(solution)/shard_map/all_to_all | solution.py:32
  37.4 78.2 %all-gather.6.cloned.1.call-start = ((), (), s32[]{:S(2)}) async-start(), calls=%async_computation.14 | async-start | bytes 1622016 | tf_op jit(solution)/shard_map/all_gather | solution.py:579
  37.5 1.9 copy-start.3
  41.8 1.6 copy-start.6
  41.8 1.7 copy-start.7
  41.8 10.9 %copy-start.5 = (bf16[32,2048]{1,0:T(8,128)(2,1)S(1)}, bf16[32,2048]{1,0:T(8,128)(2,1)}, u32[]{:S(2)}) copy-start(bf16[32,2048]{1,0:T(8,128)(2,1)} %hidden_ref.3) | copy-start | bytes 393220
  55.0 105.1 %all-gather.8.cloned.1.call-start = ((), (), s32[]{:S(2)}) async-start(), calls=%async_computation.15 | async-start | bytes 2228224 | tf_op jit(solution)/shard_map/all_gather | solution.py:580
  55.8 164.5 %reduce-scatter.2.cloned.1.call-start = ((), (), s32[]{:S(2)}) async-start(), calls=%async_computation.16 | async-start | bytes 3538944 | tf_op jit(solution)/shard_map/reduce_scatter | solution.py:600
  60.0 54.6 %copy-start.1 = (f32[1024,2048]{1,0:T(8,128)}, f32[1024,2048]{1,0:T(8,128)S(1)}, u32[]{:S(2)}) copy-start(f32[1024,2048]{1,0:T(8,128)S(1)} %get-tuple-element.47.exp_ref) | copy-start | bytes 25165828
  126.4 22.4 %copy-start.2 = (bf16[384,2048]{1,0:T(8,128)(2,1)S(1)}, bf16[384,2048]{1,0:T(8,128)(2,1)}, u32[]{:S(2)}) copy-start(bf16[384,2048]{1,0:T(8,128)(2,1)} %constant_dynamic-slice_fusion.3.v_ref) | copy-start | bytes 4718596
  126.4 22.4 %copy-start.4 = (f32[1024,384]{1,0:T(8,128)S(1)}, f32[1024,384]{1,0:T(8,128)}, u32[]{:S(2)}) copy-start(f32[1024,384]{1,0:T(8,128)} %all-gather.6.cloned.1.call-done.y_ref) | copy-start | bytes 4718596
  181.5 12.1 %all-to-all-start.9 = ((bf16[16,32,384]{2,1,0:T(8,128)(2,1)}), bf16[16,32,384]{2,1,0:T(8,128)(2,1)}, u32[]{:S(2)}, u32[]{:S(2)}) async-start(bf16[16,32,384]{2,1,0:T(8,128)(2,1)} %shard_map.96), calls=%async_computation.9 | async-start | bytes 786432 | tf_op jit(solution)/shard_map/all_to_all | solution.py:32
  195.5 19.4 %all-to-all-start.10 = ((f32[16,32,128]{2,1,0:T(8,128)}), f32[16,32,128]{2,1,0:T(8,128)}, u32[]{:S(2)}, u32[]{:S(2)}) async-start(f32[16,32,128]{2,1,0:T(8,128)} %shard_map.97), calls=%async_computation.10 | async-start | bytes 524288 | tf_op jit(solution)/shard_map/all_to_all | solution.py:32
  216.7 16.9 %all-to-all-start.11 = ((f32[16,32,128]{2,1,0:T(8,128)}), f32[16,32,128]{2,1,0:T(8,128)S(1)}, u32[]{:S(2)}, u32[]{:S(2)}) async-start(f32[16,32,128]{2,1,0:T(8,128)} %shard_map.98), calls=%async_computation.11 | async-start | bytes 524288 | tf_op jit(solution)/shard_map/all_to_all | solution.py:32
  222.1 11.5 %collective-permute-start.2 = (f32[24,2048]{1,0:T(8,128)}, f32[24,2048]{1,0:T(8,128)}, u32[]{:S(2)}, u32[]{:S(2)}) collective-permute-start(f32[24,2048]{1,0:T(8,128)} %get-tuple-element.67), channel_id=1, source_target_pairs={{0,16},{16,0},{1,17},{17,1},{2,18},{18,2},{3,19},{19,3},{4,20},{20... | collective-permute-start | bytes 589832 | tf_op jit(solution)/shard_map/ppermute | solution.py:63
Sparse Core Ops, SparseCore 0:
  9.9 42.8 all-gather.3
  55.9 49.4 all-gather.5
  107.2 36.1 all-gather.7
  160.2 41.2 reduce-scatter.1
